TPU v7x, 256 devices: a whole 4x4x8 slice. The times are simulated.
256 devices in a mesh: ctx: 32 (over z, x), head: 8 (over y, core).
Axes of the slice: x: 4, y: 4, z: 8, core: 2. Of those that a mesh axis runs over, the one named last changes fastest.
Arguments:
- activations: bfloat16 [32768, 2048], P('ctx'), may hold values from -6 to 6
- qkv_weight: bfloat16 [2048, 6144], P(None, 'head'), may hold values from -0.125 to 0.125
- level_proj: bfloat16 [2048, 336], P(None, 'head'), may hold values from -0.125 to 0.125
- log_gate: float32 [32768, 16], P('ctx', 'head'), may hold values from -4 to 0, as said below
- prior_parts: float32 [32, 4, 16, 128, 128], P('ctx', None, 'head'), may hold values from -18 to 18
- out_weight: bfloat16 [2048, 2048], P('head'), may hold values from -0.125 to 0.125
Outputs:
- layer_out: bfloat16 [32768, 2048], P(('ctx', 'head'))
Inputs may be any that keep to these rules, and one draw needn't show every extreme that they name: `log_gate`: every entry is negative.
All inputs are finite; a program needn't handle non-finite values.
Results may differ from a plain program's by a relative error of at most 0.023.
Values may be sent and summed in bfloat16 or wider, within the bound.
No kernel may reach another device: no remote copies, remote signals or barrier semaphores. Data moves between devices by JAX's collectives and lax.ppermute only.
A program may use at most 128 MiB of HBM per device.

v0:
```python
import jax
import jax.numpy as jnp
from jax import lax
from jax.sharding import PartitionSpec as P

DH = 128
LEVELS = 21
PRIOR = 4


def level_of(left, right):
    differing = jnp.bitwise_xor(left, right)
    counted = jnp.zeros_like(differing)
    for bit_number in range(31):
        counted = counted + (jnp.right_shift(differing, bit_number) > 0).astype(jnp.int32)
    return counted


def shards(activations, qkv_weight, level_proj, log_gate, prior_parts, out_weight):
    block_len = activations.shape[0]
    local_heads = log_gate.shape[1]
    head_dim = DH
    query_scale = DH ** (-0.5)
    highest = lax.Precision.HIGHEST
    ctx_count = lax.axis_size("ctx")
    ctx_bits = ctx_count.bit_length() - 1
    position = lax.axis_index("ctx")
    base_level = block_len.bit_length()
    prior_level = (block_len * ctx_count).bit_length()
    earlier = lax.psum(prior_parts[0].astype(jnp.bfloat16), "ctx").astype(jnp.float32)
    projected = jnp.dot(activations, qkv_weight, preferred_element_type=jnp.float32).astype(
        jnp.bfloat16
    )
    projected = projected.reshape(block_len, local_heads, 3, head_dim)
    query = projected[:, :, 0]
    key_rows = projected[:, :, 1]
    values = projected[:, :, 2]
    level_weight = jax.nn.softplus(
        jnp.dot(activations, level_proj, preferred_element_type=jnp.float32)
    )
    level_weight = level_weight.reshape(block_len, local_heads, LEVELS)
    cumulative = jnp.cumsum(log_gate, axis=0)
    block_decay = cumulative[-1]
    to_end = jnp.exp(block_decay[None] - cumulative)
    summary = jnp.einsum(
        "shi,shj->hij",
        to_end[:, :, None] * key_rows.astype(jnp.float32),
        values.astype(jnp.float32),
        precision=highest,
    )
    scores = (
        jnp.einsum("thd,shd->hts", query, key_rows, preferred_element_type=jnp.float32)
        * query_scale
    )
    positions = jnp.arange(block_len, dtype=jnp.int32)
    levels_local = level_of(positions[:, None], positions[None, :])
    causal = positions[:, None] >= positions[None, :]
    weight_heads = jnp.transpose(level_weight, (1, 0, 2))
    pair_weight = jnp.zeros_like(scores)
    for level_index in range(base_level):
        pair_weight = pair_weight + jnp.where(
            levels_local[None] == level_index,
            weight_heads[:, :, level_index : level_index + 1],
            0.0,
        )
    cum_heads = jnp.transpose(cumulative)
    gap_matrix = cum_heads[:, :, None] - cum_heads[:, None, :]
    decay_matrix = jnp.where(causal[None], jnp.exp(jnp.where(causal[None], gap_matrix, 0.0)), 0.0)
    mixing = (pair_weight * decay_matrix * scores).astype(jnp.bfloat16)
    inside = jnp.einsum("hts,shj->thj", mixing, values, preferred_element_type=jnp.float32)
    all_decays = lax.all_gather(block_decay[None], "ctx", axis=0, tiled=True)
    block_ends = jnp.cumsum(all_decays, axis=0)
    offset = lax.dynamic_index_in_dim(block_ends - all_decays, position, 0, keepdims=False)
    bit_index = jnp.arange(ctx_bits, dtype=jnp.int32)
    upper_bit = jnp.bitwise_and(jnp.right_shift(position, bit_index), 1) == 1
    incoming = lax.all_gather(summary[None].astype(jnp.bfloat16), "ctx", axis=0, tiled=True).astype(
        jnp.float32
    )
    piece_count = incoming.shape[0]
    block_ids = jnp.arange(piece_count, dtype=jnp.int32)
    valid_rows = block_ids < position
    decay_gap = jnp.where(valid_rows[:, None], offset[None] - block_ends, 0.0)
    carry_factor = jnp.where(valid_rows[:, None], jnp.exp(decay_gap), 0.0)
    same_high = (
        jnp.right_shift(block_ids[None], bit_index[:, None] + 1)
        == jnp.right_shift(position, bit_index + 1)[:, None]
    )
    bit_zero = jnp.bitwise_and(jnp.right_shift(block_ids[None], bit_index[:, None]), 1) == 0
    grouped = same_high & bit_zero & upper_bit[:, None]
    coefficient = grouped.astype(jnp.float32)[:, :, None] * carry_factor[None]
    level_states = jnp.zeros((ctx_bits, local_heads, head_dim, head_dim), jnp.float32) + jnp.einsum(
        "kjh,jhab->khab", coefficient, incoming, precision=highest
    )
    stacked = jnp.concatenate([level_states, earlier], axis=0).astype(jnp.bfloat16)
    reads = jnp.einsum("thi,nhij->tnhj", query, stacked, preferred_element_type=jnp.float32)
    across_weight = (
        level_weight[:, :, base_level : base_level + ctx_bits]
        * jnp.exp(cumulative)[:, :, None]
        * query_scale
    )
    across = jnp.sum(
        jnp.transpose(across_weight, (0, 2, 1))[:, :, :, None] * reads[:, :ctx_bits], axis=1
    )
    prior_weight = (
        level_weight[:, :, prior_level : prior_level + PRIOR]
        * jnp.exp(offset[None] + cumulative)[:, :, None]
        * query_scale
    )
    prior_term = jnp.sum(
        jnp.transpose(prior_weight, (0, 2, 1))[:, :, :, None] * reads[:, ctx_bits:], axis=1
    )
    mixed_heads = inside + across + prior_term
    normed = mixed_heads * lax.rsqrt(
        jnp.mean(mixed_heads * mixed_heads, axis=-1, keepdims=True) + 1e-06
    )
    normed = normed.astype(jnp.bfloat16).reshape(block_len, local_heads * head_dim)
    return lax.psum_scatter(
        jnp.dot(normed, out_weight, preferred_element_type=jnp.float32).astype(jnp.bfloat16),
        "head",
        scatter_dimension=0,
        tiled=True,
    )


def solution(mesh):
    placed = (
        P("ctx", None),
        P(None, "head"),
        P(None, "head"),
        P("ctx", "head"),
        P("ctx", None, "head", None, None),
        P("head", None),
    )
    return jax.shard_map(
        shards, mesh=mesh, in_specs=placed, out_specs=P(("ctx", "head"), None), check_vma=False
    )
```

profile of v0, /device:TPU:1, one launch (start us, length us, event | category | flops | bytes accessed | tf_op | source)
XLA Modules:
  0.0 362.0 jit_solution(4424441865522089758)
XLA Ops:
  6.5 0.0 copy-start
  6.5 0.0 all-gather.4.cloned.1.call-start
  6.5 0.8 copy.139
  7.4 0.6 reduce-window.6
  8.0 0.2 slice_reduce_fusion
  8.1 0.2 reduce-window.9
  8.3 0.1 add_bitcast_fusion
  8.4 0.0 copy-start.3
  8.4 0.2 slice_reduce_fusion.1
  8.6 0.4 copy-done.3
  9.0 33.7 %all-gather.1 = f32[32,1,2]{2,1,0:T(1,128)S(1)} all-gather(f32[1,1,2]{2,1,0:T(1,128)S(1)} %bitcast.132), channel_id=1, replica_groups=mesh['ctx'=32,'head'=8] {'ctx'}, dimensions={0}, use_global_device_ids=true | all-gather | bytes 264 | tf_op jit(solution)/shard_map/all_gather | solution.py:71
  42.6 0.1 copy.79
  42.7 0.1 copy.80
  42.8 0.1 reduce_window_sum.36
  42.9 0.1 bitcast_exponential_fusion
  43.0 0.0 copy-done
  43.0 5.7 %convolution_convert_fusion.1 = bf16[1024,768]{0,1:T(8,128)(2,1)S(1)} fusion(bf16[1024,2048]{1,0:T(8,128)(2,1)} %param.6, bf16[2048,768]{1,0:T(8,128)(2,1)S(1)} %copy-done), kind=kOutput, calls=%fused_computation.56 | convolution fusion | flops 3222011904 | bytes 8912896 | tf_op jit(solution)/shard_map/dot_general | solution.py:31
  48.6 0.0 copy-start.1
  48.7 1.1 copy-done.1
  49.8 0.8 slice.98
  50.6 2.0 copy.103
  52.7 3.2 convolution_convert_fusion.2
  55.8 0.0 all-gather.4.cloned.1.call-update
  55.9 0.0 all-reduce.2.cloned.1.call-start
  55.9 1.1 convert_element_type.1846
  57.0 0.9 copy.137
  57.9 0.0 all-reduce.2.cloned.1.call-update
  57.9 0.5 reduce-scatter.2.cloned.1.call-start
  58.5 0.6 iota_add_fusion
  59.0 0.5 and_compare_fusion.1
  59.5 18.7 %broadcast_compare_fusion = (pred[1024,1024]{1,0:T(8,128)(4,1)}, pred[1024,1024]{1,0:T(8,128)(4,1)}) fusion(), kind=kLoop, calls=%fused_computation.45 | loop fusion | flops 132120576 | bytes 2097152 | tf_op jit(solution)/shard_map/eq | solution.py:62
  78.2 18.6 %broadcast_compare_fusion.2 = (pred[1024,1024]{1,0:T(8,128)(4,1)}, pred[1024,1024]{1,0:T(8,128)(4,1)}) fusion(), kind=kLoop, calls=%fused_computation.47 | loop fusion | flops 132120576 | bytes 2097152 | tf_op jit(solution)/shard_map/eq | solution.py:62
  96.9 0.0 copy-start.2
  96.9 18.7 %broadcast_compare_fusion.4 = (pred[1024,1024]{1,0:T(8,128)(4,1)}, pred[1024,1024]{1,0:T(8,128)(4,1)}) fusion(), kind=kLoop, calls=%fused_computation.49 | loop fusion | flops 132120576 | bytes 2097152 | tf_op jit(solution)/shard_map/eq | solution.py:62
  115.6 18.7 %broadcast_compare_fusion.6 = (pred[1024,1024]{1,0:T(8,128)(4,1)}, pred[1024,1024]{1,0:T(8,128)(4,1)}) fusion(), kind=kLoop, calls=%fused_computation.51 | loop fusion | flops 132120576 | bytes 2097152 | tf_op jit(solution)/shard_map/eq | solution.py:62
  134.3 18.7 %broadcast_compare_fusion.8 = (pred[1024,1024]{1,0:T(8,128)(4,1)}, pred[1024,1024]{1,0:T(8,128)(4,1)}) fusion(), kind=kLoop, calls=%fused_computation.53 | loop fusion | flops 132120576 | bytes 2097152 | tf_op jit(solution)/shard_map/eq | solution.py:62
  152.9 18.1 %broadcast_compare_fusion.10 = pred[1024,1024]{1,0:T(8,128)(4,1)} fusion(), kind=kLoop, calls=%fused_computation.55 | loop fusion | flops 131072000 | bytes 1048576 | tf_op jit(solution)/shard_map/eq | solution.py:62
  171.0 1.3 iota_compare_fusion
  172.3 0.1 exponential_select_fusion
  172.4 0.7 copy.82
  173.0 0.0 copy-done.2
  173.0 3.6 %compare_select_fusion = f32[1024,42]{0,1:T(8,128)S(1)} fusion(bf16[1024,2048]{1,0:T(8,128)(2,1)} %param.6, bf16[2048,42]{0,1:T(8,128)(2,1)S(1)} %copy-done.2), kind=kOutput, calls=%fused_computation.69 | convolution fusion | flops 176418816 | bytes 4538368 | tf_op jit(solution)/shard_map/dot_general | solution.py:39
  176.8 0.1 fusion.46
  176.9 0.7 fusion.39
  177.6 0.0 all-gather.4.cloned.1.call-done
  177.6 4.2 %fusion.13 = bf16[5,2,128,128]{3,0,2,1:T(8,128)(2,1)} fusion(bf16[32,2,128,128]{3,2,1,0:T(8,128)(2,1)} %bitcast.118, f32[32,2]{0,1:T(2,128)} %copy.82, f32[5,32]{1,0:T(8,128)S(1)} %fusion.39), kind=kOutput, calls=%fused_computation.61 | convolution fusion | flops 63078720 | bytes 2425728 | tf_op jit(solution)/shard_map/kjh,jhab->khab/dot_general | solution.py:91
  181.8 99.3 %all-reduce.2.cloned.1.call-done = bf16[4,2,128,128]{3,0,2,1:T(4,128)(2,1)} async-done(((bf16[4,2,128,128]{3,0,2,1:T(4,128)(2,1)}), bf16[4,2,128,128]{3,0,2,1:T(4,128)(2,1)}) %all-reduce.2.cloned.1.call-update) | async-done | bytes 262160 | tf_op jit(solution)/shard_map/psum | solution.py:30
  281.1 1.5 pad_maximum_fusion
  282.7 2.5 convolution_bitcast_fusion
  285.1 1.7 fusion
  286.8 0.0 copy-start.4
  286.8 1.6 fusion.1
  288.4 0.0 copy-done.4
  288.4 22.0 %multiply_reduce_fusion = (f32[1024,2]{0,1:T(2,128)S(1)}, f32[1024,2,128]{0,2,1:T(8,128)}) fusion(f32[1024,2,128]{0,2,1:T(8,128)} %fusion.1, f32[1024,2,128]{0,2,1:T(8,128)} %fusion, f32[2,1024]{1,0:T(2,128)S(1)} %bitcast.128, f32[2,1024]{1,0:T(2,128)S(1)} %get-tuple-element.25, f32[2,1024]{1,0:T(2,128)S(1)} %get-tuple-element.26, ...), kind=kOutput, calls=%fused_computation.65 | convolution fusion | flops 1133508608 | bytes 17416192 | tf_op jit(solution)/shard_map/hts,shj->thj/dot_general | solution.py:70
  310.4 1.3 multiply_convert_fusion.8
  311.7 4.5 %convolution_convert_fusion = bf16[1024,2048]{1,0:T(8,128)(2,1)} fusion(bf16[1024,256]{0,1:T(8,128)(2,1)S(1)} %bitcast.117, bf16[256,2048]{1,0:T(8,128)(2,1)} %param.11), kind=kOutput, calls=%fused_computation.40 | convolution fusion | flops 1075838976 | bytes 5767168 | tf_op jit(solution)/shard_map/dot_general | solution.py:118
  316.2 0.0 reduce-scatter.2.cloned.1.call-update
  316.2 39.0 %reduce-scatter.2.cloned.1.call-done = bf16[128,2048]{1,0:T(8,128)(2,1)} async-done(((bf16[1024,2048]{1,0:T(8,128)(2,1)}), bf16[128,2048]{1,0:T(8,128)(2,1)}) %reduce-scatter.2.cloned.1.call-update) | async-done | bytes 524304 | tf_op jit(solution)/shard_map/reduce_scatter | solution.py:117
  (13 shorter events, 0.1 us)
Async XLA Ops:
  6.5 36.4 %copy-start = (bf16[2048,768]{1,0:T(8,128)(2,1)S(1)}, bf16[2048,768]{1,0:T(8,128)(2,1)}, u32[]{:S(2)}) copy-start(bf16[2048,768]{1,0:T(8,128)(2,1)} %param.7) | copy-start | bytes 9437188
  6.5 171.1 %all-gather.4.cloned.1.call-start = ((), (), s32[]{:S(2)}) async-start(), calls=%async_computation.3 | async-start | bytes 2162688 | tf_op jit(solution)/shard_map/all_gather | solution.py:76
  8.4 0.6 copy-start.3
  48.6 1.2 copy-start.1
  55.9 225.3 %all-reduce.2.cloned.1.call-start = ((), (), s32[]{:S(2)}) async-start(), calls=%async_computation.1 | async-start | bytes 524288 | tf_op jit(solution)/shard_map/psum | solution.py:30
  57.9 297.3 %reduce-scatter.2.cloned.1.call-start = ((), (), s32[]{:S(2)}) async-start(), calls=%async_computation.2 | async-start | bytes 4718592 | tf_op jit(solution)/shard_map/reduce_scatter | solution.py:117
  96.9 76.2 %copy-start.2 = (bf16[2048,42]{0,1:T(8,128)(2,1)S(1)}, bf16[2048,42]{0,1:T(8,128)(2,1)}, u32[]{:S(2)}) copy-start(bf16[2048,42]{0,1:T(8,128)(2,1)} %param.8) | copy-start | bytes 516100
  286.8 1.6 copy-start.4
Sparse Core Ops, SparseCore 0:
  56.0 80.6 all-gather.3
  140.1 140.9 all-reduce.1
  316.4 38.8 reduce-scatter.1
where the time goes:
time: 369 us; the launch traced here: 362 us
  waiting for transfers between devices  138 us (37%)
  other arithmetic  123 us (33%)
  matrix products  45.6 us (12%)
  blocking collectives  33.7 us (9%)
  between operations  13.5 us (4%)
  local copies, waits for them, and re-layouts  7.51 us (2%)
    eq x6, other arithmetic, shards(): levels_local[None] == level_index  111 us
    psum x1, waiting for transfers between devices, shards(): lax.psum(prior_parts[0].astype(jnp.bfloat16), 'ctx').astype(jnp.float32)  99.3 us
    reduce_scatter x1, waiting for transfers between devices, shards(): lax.psum_scatter(jnp.dot(normed, out_weight, preferred_element_type=jnp.f...  39 us
    all_gather x1, blocking collectives, shards(): all_decays = lax.all_gather(block_decay[None], 'ctx', axis=0, tiled=True)  33.7 us
    dot_general x1, matrix products, shards(): jnp.einsum('hts,shj->thj', mixing, values, preferred_element_type=jnp.flo...  22 us
  transfers between devices with their start and end apart: 3, of which 2 were waited for; matrix products, arithmetic and copies ran while one was open for 35% of the time, Pallas kernels for 0%

commit v1 on v0

v1 whole, which is shorter than its diff:
```python
import functools

import jax
import jax.numpy as jnp
from jax import lax
from jax.experimental import pallas as pl
from jax.experimental.pallas import tpu as pltpu
from jax.sharding import PartitionSpec as P

DH = 128
LEVELS = 21
PRIOR = 4
CHUNK = 128
TILE = 256
NX = 4
TAIL = 16
VMEM = pl.BlockSpec(memory_space=pltpu.VMEM)
SMEM = pl.BlockSpec(memory_space=pltpu.SMEM)
F32 = jnp.float32
BF16 = jnp.bfloat16


def params(mib=48):
    return pltpu.CompilerParams(vmem_limit_bytes=mib * 1024 * 1024)


def dot(left, right, contract=((1,), (0,))):
    return lax.dot_general(left, right, (contract, ((), ())), preferred_element_type=F32)


def iota(axis, shape=(CHUNK, CHUNK)):
    return lax.broadcasted_iota(jnp.int32, shape, axis)


def decay_rows(decays):
    rows = iota(0, (TAIL, DH))
    tail = jnp.zeros((TAIL, DH), F32)
    for index, decay in enumerate(decays):
        rest = jnp.broadcast_to(decay, (1, DH))
        for piece in range(3):
            part = rest.astype(BF16).astype(F32)
            tail = jnp.where(rows == index * 3 + piece, part, tail)
            rest = rest - part
    return tail.astype(BF16)


def tail_decays(tail, heads):
    tail = tail.astype(F32)
    return [
        (tail[3 * h : 3 * h + 1] + tail[3 * h + 1 : 3 * h + 2]) + tail[3 * h + 2 : 3 * h + 3]
        for h in range(heads)
    ]


def decays_of(payload, heads):
    return tail_decays(payload[heads * DH : heads * DH + TAIL, :], heads)


def copy_parts(source, target, sems):
    count = sems.shape[0]
    size = target.shape[0] // count
    copies = []
    for i in range(count):
        part = pl.ds(i * size, size)
        copies.append(pltpu.make_async_copy(source.at[part, :], target.at[part, :], sems.at[i]))
        copies[-1].start()
    return copies


def keys_kernel(acts_hbm, weight_hbm, kv, query_weight, acts, weight, weight_sem, acts_sem):
    block = acts.shape[0]
    heads = query_weight.shape[1] // DH
    weight_copies = copy_parts(weight_hbm, weight, weight_sem)
    acts_copies = copy_parts(acts_hbm, acts, acts_sem)
    for copy in weight_copies:
        copy.wait()
    per_tile = len(acts_copies) * TILE // block
    for i in range(block // TILE):
        for copy in acts_copies[i * per_tile : (i + 1) * per_tile]:
            copy.wait()
        token = slice(i * TILE, (i + 1) * TILE)
        for h in range(heads):
            both = dot(acts[token, :], weight[:, h * 3 * DH + DH : (h + 1) * 3 * DH])
            kv[token, h * 2 * DH : (h + 1) * 2 * DH] = both.astype(BF16)
    for h in range(heads):
        query_weight[:, h * DH : (h + 1) * DH] = weight[:, h * 3 * DH : h * 3 * DH + DH]


def states_kernel(place, kv, gate, prior, chunk_states, *payloads):
    x = place[0]
    heads, block = gate.shape
    later = iota(1) > iota(0)
    for h in range(heads):
        rows = slice(h * DH, (h + 1) * DH)
        total = None
        for c in range(block // CHUNK):
            token = slice(c * CHUNK, (c + 1) * CHUNK)
            gates = gate[h : h + 1, token]
            to_end = jnp.exp(jnp.sum(jnp.where(later, gates, 0.0), axis=1, keepdims=True))
            keys = kv[token, 2 * h * DH : (2 * h + 1) * DH].astype(F32)
            values = kv[token, (2 * h + 1) * DH : (2 * h + 2) * DH]
            state = dot((keys * to_end).astype(BF16), values, ((0,), (0,)))
            chunk_states[c, h] = state
            decay = jnp.exp(jnp.sum(gates, axis=1, keepdims=True))
            total = state if total is None else total * decay + state
        for payload in payloads:
            payload[rows, :] = total.astype(BF16)
    tail = decay_rows([jnp.sum(gate[h : h + 1, :], axis=1, keepdims=True) for h in range(heads)])
    start = heads * DH + TAIL
    for d, payload in enumerate(payloads):
        payload[heads * DH : start, :] = tail
        for h in range(heads):
            payload[start + h * DH : start + (h + 1) * DH, :] = prior[x ^ d, h].astype(BF16)


def level_kernel(acts, weight, proj, after, query, level):
    for i in range(acts.shape[0] // TILE):
        rows = slice(i * TILE, (i + 1) * TILE)
        query[rows, :] = dot(acts[rows, :], weight[...]).astype(BF16)
        raw = dot(acts[rows, :], proj[...], ((1,), (1,)))
        value = (jnp.maximum(raw, 0.0) + jnp.log1p(jnp.exp(-jnp.abs(raw)))) * DH ** (-0.5)
        pad = jnp.zeros((TILE, DH - value.shape[1]), F32)
        level[rows, :] = jnp.concatenate([value, pad], axis=1)


def attend_kernel(h, query_rows, kv, level, gate, chunk_states, low_states, after, inside):
    chunks = chunk_states.shape[0]
    low_bits = low_states.shape[0]
    rows, columns = iota(0), iota(1)
    causal = rows >= columns
    differing = jnp.bitwise_xor(rows, columns)
    level_index = jnp.full((CHUNK, CHUNK), h * LEVELS, jnp.int32)
    for bit in range(7):
        level_index = level_index + (differing >= (1 << bit)).astype(jnp.int32)

    totals = [
        jnp.sum(gate[h : h + 1, c * CHUNK : (c + 1) * CHUNK], axis=1, keepdims=True)
        for c in range(chunks)
    ]
    states = {}
    sums = [chunk_states[c, h] for c in range(chunks)]
    for bit in range(3):
        width = 1 << bit
        for low in range(0, chunks, 2 * width):
            state = sums[low // width]
            for c in range(low + width, low + 2 * width):
                states[c, bit] = state.astype(BF16)
                state = state * jnp.exp(totals[c])
            sums[low // width] = state + sums[low // width + 1]
        sums = sums[::2]

    before = jnp.zeros((1, 1), F32)
    for c in range(chunks):
        token = slice(c * CHUNK, (c + 1) * CHUNK)
        level_c = level[token, :]
        gates = gate[h : h + 1, token]
        gate_column = jnp.sum(jnp.where(rows == columns, gates, 0.0), axis=1, keepdims=True)
        column = jnp.sum(jnp.where(causal, gates, 0.0), axis=1, keepdims=True)
        row = jnp.sum(jnp.where(rows <= columns, gate_column, 0.0), axis=0, keepdims=True)
        query = query_rows[token, h * DH : (h + 1) * DH]
        query_f = query.astype(F32)
        scores = dot(query, kv[token, 2 * h * DH : (2 * h + 1) * DH], ((1,), (1,)))
        weights = jnp.take_along_axis(level_c, level_index, axis=1)
        decay = jnp.exp(jnp.where(causal, column - row, -1e30))
        lhs = [(weights * decay * scores).astype(BF16)]
        rhs = [kv[token, (2 * h + 1) * DH : (2 * h + 2) * DH]]
        chunk_level = level_c * jnp.exp(column)
        for bit in range(3):
            if (c, bit) in states:
                where = h * LEVELS + 8 + bit
                lhs.append((chunk_level[:, where : where + 1] * query_f).astype(BF16))
                rhs.append(states[c, bit])
        block_level = level_c * jnp.exp(column + before)
        for n in range(low_bits):
            where = h * LEVELS + 11 + n
            lhs.append((block_level[:, where : where + 1] * query_f).astype(BF16))
            rhs.append(low_states[n, h])
        inside[token, :] = dot(jnp.concatenate(lhs, axis=1), jnp.concatenate(rhs, axis=0))
        before = before + totals[c]


def scale_kernel(h, query_rows, level, gate, after, left):
    causal = iota(0) >= iota(1)
    before = jnp.zeros((1, 1), F32)
    for c in range(left.shape[0] // CHUNK):
        token = slice(c * CHUNK, (c + 1) * CHUNK)
        gates = gate[h : h + 1, token]
        column = jnp.sum(jnp.where(causal, gates, 0.0), axis=1, keepdims=True)
        block_level = level[token, :] * jnp.exp(column + before)
        query_f = query_rows[token, h * DH : (h + 1) * DH].astype(F32)
        for n in range(left.shape[1] // DH):
            where = h * LEVELS + 13 + n
            left[token, n * DH : (n + 1) * DH] = (
                block_level[:, where : where + 1] * query_f
            ).astype(BF16)
        before = before + jnp.sum(gates, axis=1, keepdims=True)


def within_kernel(place, own, two, one, three, after, states, onward, carry):
    pieces = (own, one, two, three)
    x = place[0]
    heads = states.shape[1]
    start = heads * DH + TAIL
    quarter = heads * DH // NX
    owner = [x ^ d for d in range(NX)]
    decays = [decays_of(piece, heads) for piece in pieces]
    group_decay = []
    carry[...] = jnp.zeros_like(carry)
    for h in range(heads):
        rows = slice(h * DH, (h + 1) * DH)
        bits = [jnp.zeros((DH, DH), F32) for _ in range(2)]
        before = jnp.zeros((1, DH), F32)
        whole = jnp.zeros((1, DH), F32)
        for d in range(NX):
            whole = whole + decays[d][h]
            before = before + jnp.where(owner[d] < x, decays[d][h], 0.0)
            if d == 0:
                continue
            piece = pieces[d][rows, :].astype(F32)
            to_here = jnp.zeros((1, DH), F32)
            for e in range(1, NX):
                after_it = (owner[e] > owner[d]) & (owner[e] < x)
                to_here = to_here + jnp.where(after_it, decays[e][h], 0.0)
            scale = jnp.where(owner[d] < x, jnp.exp(to_here), 0.0)
            for bit in range(2):
                used = (
                    (((x >> bit) & 1) == 1)
                    & (((owner[d] >> bit) & 1) == 0)
                    & ((x >> (bit + 1)) == (owner[d] >> (bit + 1)))
                )
                bits[bit] = bits[bit] + piece * jnp.where(used, scale, 0.0)
        for bit in range(2):
            states[bit, h] = bits[bit].astype(BF16)
        carry[h : h + 1, :] = before
        group_decay.append(whole)
    mine = pl.ds(pl.multiple_of(x * quarter, quarter), quarter)
    group = jnp.zeros((quarter, DH), F32)
    for d in range(NX):
        to_end = jnp.zeros((1, DH), F32)
        for e in range(NX):
            decay = jnp.where(x < NX // 2, decays[e][0], decays[e][1])
            to_end = to_end + jnp.where(owner[e] > owner[d], decay, 0.0)
        group = group + pieces[d][mine, :].astype(F32) * jnp.exp(to_end)
    onward[:quarter, :] = group.astype(BF16)
    onward[quarter : quarter + TAIL, :] = decay_rows(group_decay)
    prior = own[start:, :].astype(F32)
    for piece in pieces[1:]:
        prior = prior + piece[start:, :].astype(F32)
    onward[quarter + TAIL :, :] = prior.astype(BF16)


def halves_kernel(below, above, after, first, second, sems):
    size = first.shape[0]
    copies = [
        pltpu.make_async_copy(below.at[pl.ds(0, size), :], first, sems.at[0]),
        pltpu.make_async_copy(above.at[pl.ds(size, size), :], second, sems.at[1]),
    ]
    for copy in copies:
        copy.start()
    for copy in copies:
        copy.wait()


def pair_kernel(place, own, got, carry_in, after, state_out, onward, carry):
    x, z = place[0], place[1]
    heads = 2
    quarter = heads * DH // NX
    upper = (z & 1) == 1
    decay_own = tail_decays(own[quarter : quarter + TAIL, :], heads)
    decay_got = tail_decays(got[quarter : quarter + TAIL, :], heads)
    carry[...] = jnp.zeros_like(carry)
    for h in range(heads):
        before = carry_in[h : h + 1, :]
        carry[2 + h : 3 + h, :] = before
        carry[h : h + 1, :] = before + jnp.where(upper, decay_got[h], 0.0)
    state_out[...] = jnp.where(upper, got[:quarter, :].astype(F32), 0.0).astype(BF16)
    first = x < NX // 2
    mine = jnp.where(first, decay_own[0], decay_own[1])
    theirs = jnp.where(first, decay_got[0], decay_got[1])
    scale_own = jnp.where(upper, 1.0, jnp.exp(theirs))
    scale_got = jnp.where(upper, jnp.exp(mine), 1.0)
    total = own[:quarter, :].astype(F32) * scale_own + got[:quarter, :].astype(F32) * scale_got
    onward[:quarter, :] = total.astype(BF16)
    onward[quarter : quarter + TAIL, :] = decay_rows(
        [decay_own[h] + decay_got[h] for h in range(heads)]
    )
    prior = own[quarter + TAIL :, :].astype(F32) + got[quarter + TAIL :, :].astype(F32)
    onward[quarter + TAIL :, :] = prior.astype(BF16)


def pairs_kernel(place, own, far, skip, near, carry_in, low_state, after, payload, carry):
    x, z = place[0], place[1]
    heads = 2
    quarter = heads * DH // NX
    pair = z >> 1
    odd = (z & 1) == 1
    prior = slice(quarter + TAIL, own.shape[0])
    total = own[prior, :].astype(F32) + near[prior, :].astype(F32)
    total = total + skip[prior, :].astype(F32) + far[prior, :].astype(F32)

    def pick(flag, left, right):
        return jnp.where(flag, left, right)

    tail = slice(quarter, quarter + TAIL)
    tail_near, tail_skip = near[tail, :].astype(F32), skip[tail, :].astype(F32)
    decay_next = tail_decays(pick(odd, tail_near, tail_skip), heads)
    decay_prev = tail_decays(pick(odd, tail_skip, tail_near), heads)
    decay_far = tail_decays(far[tail, :], heads)
    carry[...] = carry_in[...]
    for h in range(heads):
        before = carry_in[h : h + 1, :]
        carry[4 + h : 5 + h, :] = before
        carry[6 + h : 7 + h, :] = before + pick(pair == 3, decay_prev[h], 0.0)
        offset = before + pick(pair >= 1, decay_prev[h], 0.0) + pick(pair >= 2, decay_far[h], 0.0)
        carry[h : h + 1, :] = offset + pick(pair == 3, decay_next[h], 0.0)
    state_near, state_skip = near[:quarter, :].astype(F32), skip[:quarter, :].astype(F32)
    state_next = pick(odd, state_near, state_skip)
    state_prev = pick(odd, state_skip, state_near)
    state_far = far[:quarter, :].astype(F32)
    first = x < NX // 2
    decay_one = pick(
        pair == 2,
        pick(first, decay_prev[0], decay_prev[1]),
        pick(first, decay_far[0], decay_far[1]),
    )
    zero_state = pick(pair == 2, state_far, state_next)
    one_state = pick(pair == 2, state_prev, state_far)
    high = pick(pair >= 2, zero_state * jnp.exp(decay_one) + one_state, 0.0)
    payload[:quarter, :] = low_state[...]
    payload[quarter : 2 * quarter, :] = pick((pair & 1) == 1, state_prev, 0.0).astype(BF16)
    payload[2 * quarter : 3 * quarter, :] = high.astype(BF16)
    payload[3 * quarter :, :] = total.astype(BF16)


def finish_kernel(place, carry, *refs):
    heads = 2
    insides, lefts, refs = refs[:heads], refs[heads : 2 * heads], refs[2 * heads :]
    own, two, one, three = refs[:NX]
    pieces, outs, states = (own, one, two, three), refs[NX:-1], refs[-1]
    z_bits = lefts[0].shape[1] // DH - PRIOR
    x = place[0]
    quarter = heads * DH // NX
    offsets = [jnp.exp(carry[h : h + 1, :]) for h in range(heads)]
    for d in range(NX):
        owner = x ^ d
        first = owner < NX // 2
        for bit in range(z_bits):
            before = jnp.where(first, carry[2 + 2 * bit : 3 + 2 * bit, :], carry[3 + 2 * bit : 4 + 2 * bit, :])
            piece = pieces[d][bit * quarter : (bit + 1) * quarter, :].astype(F32) * jnp.exp(before)
            where = bit * DH + lax.rem(owner, 2) * quarter
            states[owner // 2, pl.ds(pl.multiple_of(where, quarter), quarter), :] = piece.astype(BF16)
        for h in range(heads):
            rows = slice(z_bits * quarter + h * DH, z_bits * quarter + (h + 1) * DH)
            where = pl.multiple_of((z_bits + owner) * DH, DH)
            piece = pieces[d][rows, :].astype(F32) * offsets[h]
            states[h, pl.ds(where, DH), :] = piece.astype(BF16)
    rows_kernel((1, 3, 2), place, *insides, *lefts, states, *outs)


def rows_kernel(distances, place, *refs):
    heads = 2
    insides, lefts = refs[:heads], refs[heads : 2 * heads]
    states, outs = refs[2 * heads], refs[-len(distances) :]
    for d, out in zip(distances, outs):
        chip = place[2] ^ d
        token = pl.ds(pl.multiple_of(chip * TILE, TILE), TILE)
        for h in range(heads):
            u = insides[h][token, :] + dot(lefts[h][token, :], states[h])
            normed = u * lax.rsqrt(jnp.mean(u * u, axis=1, keepdims=True) + 1e-06)
            out[:, h * DH : (h + 1) * DH] = normed.astype(BF16)


def near_kernel(place, *refs):
    refs, (mine, theirs, rows) = refs[:-3], refs[-3:]
    pieces, weights = refs[: len(refs) // 2], refs[len(refs) // 2 :]

    @pl.when(pl.program_id(0) == 0)
    def _():
        for d, piece in enumerate(pieces):
            for side in range(2):
                where = pl.multiple_of((place[3] ^ side) * CHUNK, CHUNK)
                rows[d, side * CHUNK : (side + 1) * CHUNK, :] = piece[pl.ds(where, CHUNK), :]

    total = dot(rows[0], weights[0][...])
    for d in range(1, len(pieces)):
        total = total + dot(rows[d], weights[d][...])
    mine[...] = total[:CHUNK]
    theirs[...] = total[CHUNK:]


def far_kernel(side, place, piece, first, second, near, out):
    weight = jnp.concatenate([first[...], second[...]], axis=0)
    where = pl.multiple_of((place[3] ^ side) * CHUNK, CHUNK)
    total = near[...] + dot(piece[pl.ds(where, CHUNK), :], weight)
    out[...] = total.astype(out.dtype)


ANY = pl.BlockSpec(memory_space=pl.ANY)
HBM = pl.BlockSpec(memory_space=pltpu.HBM)


def small(kernel, shapes, *operands, specs=None, outs=None, scratch=(), flops=0, mib=24):
    return pl.pallas_call(
        kernel,
        out_shape=shapes,
        in_specs=specs or [SMEM if o.dtype == jnp.int32 else VMEM for o in operands],
        out_specs=outs or jax.tree.map(lambda _: VMEM, shapes),
        scratch_shapes=list(scratch),
        compiler_params=params(mib),
        cost_estimate=pl.CostEstimate(flops=flops, bytes_accessed=1 << 20, transcendentals=0),
    )(*operands)


def shards(activations, qkv_weight, level_proj, log_gate, prior_parts, out_weight):
    block, width = activations.shape
    heads = log_gate.shape[1]
    nz = lax.axis_size("ctx") // NX
    nh = lax.axis_size("head")
    ny = nh // 2
    z_bits = nz.bit_length() - 1
    chunks = block // CHUNK
    rows = heads * DH
    quarter = rows // NX
    shape = jax.ShapeDtypeStruct
    ctx = lax.axis_index("ctx").astype(jnp.int32)
    head = lax.axis_index("head").astype(jnp.int32)
    place = jnp.stack([ctx % NX, ctx // NX, head // 2, head % 2])

    def along_x(array, d):
        return lax.ppermute(
            array, "ctx", [(z * NX + x, z * NX + (x ^ d)) for z in range(nz) for x in range(NX)]
        )

    def across_z(array, target):
        return lax.ppermute(
            array, "ctx", [(z * NX + x, target(z) % nz * NX + x) for z in range(nz) for x in range(NX)]
        )

    def along_y(array, d):
        return lax.ppermute(
            array, "head", [(y * 2 + c, (y ^ d) * 2 + c) for y in range(ny) for c in range(2)]
        )

    below, above = along_y(out_weight, 1), along_y(out_weight, 3)
    gate = log_gate.T
    sent = shape((rows + TAIL + rows, DH), BF16)
    dma = pltpu.SemaphoreType.DMA
    kv, query_weight = small(
        keys_kernel,
        [shape((block, 2 * rows), BF16), shape((width, rows), BF16)],
        activations,
        qkv_weight,
        specs=[HBM] * 2,
        scratch=[
            pltpu.VMEM(activations.shape, BF16),
            pltpu.VMEM(qkv_weight.shape, BF16),
            dma((8,)),
            dma((8,)),
        ],
        flops=4 * block * width * rows,
        mib=50,
    )
    chunk_states, *payloads = small(
        states_kernel,
        [shape((chunks, heads, DH, DH), F32)] + [sent] * NX,
        place,
        kv,
        gate,
        prior_parts[0],
    )
    pieces = [payloads[0]] + [along_x(payloads[d], d) for d in range(1, NX)]

    query, level = small(
        level_kernel,
        [shape((block, rows), BF16), shape((block, DH), F32)],
        activations,
        query_weight,
        level_proj.T,
        payloads[0],
        specs=[VMEM] * 3 + [ANY],
        flops=4 * block * width * rows,
        mib=24,
    )

    def scaled(h, after):
        return small(
            functools.partial(scale_kernel, h),
            shape((block, (z_bits + PRIOR) * DH), BF16),
            query,
            level,
            gate,
            after,
            specs=[VMEM] * 3 + [ANY],
            flops=1 << 30,
        )

    lefts = [scaled(0, payloads[0])]
    low_states, onward, carry = small(
        within_kernel,
        [
            shape((2, heads, DH, DH), BF16),
            shape((quarter + TAIL + rows, DH), BF16),
            shape((8, DH), F32),
        ],
        place,
        pieces[0],
        pieces[2],
        pieces[1],
        pieces[3],
        lefts[0],
        specs=[SMEM] + [VMEM] * NX + [ANY],
    )

    def attend(h, after):
        return small(
            functools.partial(attend_kernel, h),
            shape((block, DH), F32),
            query,
            kv,
            level,
            gate,
            chunk_states,
            low_states,
            after,
            specs=[VMEM] * 6 + [ANY],
            flops=1 << 30,
        )

    got = across_z(onward, lambda z: z ^ 1)
    insides = [attend(0, onward)]
    state, onward, carry = small(
        pair_kernel,
        [shape((quarter, DH), BF16), shape(onward.shape, BF16), shape((8, DH), F32)],
        place,
        onward,
        got,
        carry,
        insides[0],
        specs=[SMEM] + [VMEM] * 3 + [ANY],
    )
    far = across_z(onward, lambda z: z + 3 if z % 2 else z - 3)
    skip = across_z(onward, lambda z: z + 2 if z % 2 else z - 2)
    near = across_z(onward, lambda z: z + 1 if z % 2 else z - 1)
    insides.append(attend(1, onward))
    halves = small(
        halves_kernel,
        [shape((rows // 2, width), BF16)] * 2,
        below,
        above,
        insides[1],
        specs=[ANY] * 3,
        outs=[VMEM] * 2,
        scratch=[dma((2,))],
        mib=4,
    )
    far_weight = along_y(halves[0], 3), along_y(halves[1], 1)
    payload, carry = small(
        pairs_kernel,
        [shape((z_bits * quarter + rows, DH), BF16), shape((8, DH), F32)],
        place,
        onward,
        far,
        skip,
        near,
        carry,
        state,
        halves[0],
        specs=[SMEM] + [VMEM] * 6 + [ANY],
    )
    lefts.append(scaled(1, payload))
    pieces = [payload] + [along_x(payload, d) for d in range(1, NX)]
    rows_out = shape((block // ny, rows), BF16)
    normed = [None] * ny
    normed[1], normed[3], normed[2], states = small(
        finish_kernel,
        [rows_out] * 3 + [shape((heads, (z_bits + PRIOR) * DH, DH), BF16)],
        place,
        carry,
        *insides,
        *lefts,
        pieces[0],
        pieces[2],
        pieces[1],
        pieces[3],
        flops=1 << 28,
    )
    normed[0] = small(
        functools.partial(rows_kernel, (0,)),
        rows_out,
        place,
        *insides,
        *lefts,
        states,
        normed[1],
        specs=[SMEM] + [VMEM] * 5 + [ANY],
        flops=1 << 28,
    )
    normed = [normed[0]] + [along_y(normed[d], d) for d in range(1, ny)]
    columns = 1024 if width % 1024 == 0 else width
    fixed = pl.BlockSpec((2 * CHUNK, rows), lambda i: (0, 0))
    weight_block = pl.BlockSpec((rows, columns), lambda i: (0, i))
    out_block = pl.BlockSpec((CHUNK, columns), lambda i: (0, i))
    half_block = pl.BlockSpec((rows // 2, columns), lambda i: (0, i))
    mine, theirs = pl.pallas_call(
        near_kernel,
        grid=(width // columns,),
        in_specs=[SMEM] + [fixed] * 3 + [weight_block] * 3,
        out_specs=[out_block] * 2,
        out_shape=[shape((CHUNK, width), F32)] * 2,
        scratch_shapes=[pltpu.VMEM((3, 2 * CHUNK, rows), BF16)],
        compiler_params=params(24),
        cost_estimate=pl.CostEstimate(flops=8 << 28, bytes_accessed=5 << 20, transcendentals=0),
    )(place, normed[0], normed[1], normed[3], out_weight, below, above)

    def add_far(side, near, dtype):
        return pl.pallas_call(
            functools.partial(far_kernel, side),
            grid=(width // columns,),
            in_specs=[SMEM, fixed, half_block, half_block, out_block],
            out_specs=out_block,
            out_shape=shape((CHUNK, width), dtype),
            compiler_params=params(24),
            cost_estimate=pl.CostEstimate(flops=1 << 28, bytes_accessed=3 << 20, transcendentals=0),
        )(place, normed[2], *far_weight, near)

    send = add_far(1, theirs, BF16)
    got = lax.ppermute(send, "head", [(i, i ^ 1) for i in range(nh)])
    keep = add_far(0, mine, F32)
    return (keep + got.astype(F32)).astype(BF16)


def solution(mesh):
    placed = (
        P("ctx", None),
        P(None, "head"),
        P(None, "head"),
        P("ctx", "head"),
        P("ctx", None, "head", None, None),
        P("head", None),
    )
    return jax.shard_map(
        shards, mesh=mesh, in_specs=placed, out_specs=P(("ctx", "head"), None), check_vma=False
    )
```

time: 369 us -> 68.4 us (0.19); the launches traced: 362 us -> 68.3 us
  waiting for transfers between devices: 138 us -> 6.94 us
  other arithmetic: 123 us -> 0.97 us
  matrix products: 45.6 us -> 0 us
  blocking collectives: 33.7 us -> 0 us
  starting transfers between devices: 0.55 us -> 33.5 us
  Pallas kernels: 0 us -> 26.7 us
  between operations: 13.5 us -> 0.22 us
  local copies, waits for them, and re-layouts: 7.51 us -> 0.02 us
    eq x7 -> x0, other arithmetic: 112 us -> none  [the longest x6 111 us: shards(): levels_local[None] == level_index]
    psum x1 -> x0, waiting for transfers between devices: 99.3 us -> none  [shards(): lax.psum(prior_parts[0].astype(jnp.bfloat16), 'ctx').astype(jnp.float32)]
    dot_general x7 -> x0, matrix products: 45.6 us -> none  [the longest x1 22 us: shards(): jnp.einsum('hts,shj->thj', mixing, values, preferred_element_type=jnp.flo...]
    reduce_scatter x1 -> x0, waiting for transfers between devices: 39 us -> none  [shards(): lax.psum_scatter(jnp.dot(normed, out_weight, preferred_element_type=jnp.f...]
    all_gather x1 -> x0, blocking collectives: 33.7 us -> none  [shards(): all_decays = lax.all_gather(block_decay[None], 'ctx', axis=0, tiled=True)]
    ppermute x0 -> x18, starting transfers between devices: none -> 33.5 us  [the longest x4 11.2 us: across_z(): lax.ppermute(array, 'ctx', [(z * NX + x, target(z) % nz * NX + x) for z i...]
    pallas_call x0 -> x16, Pallas kernels: none -> 26.7 us  [the longest x13 22.3 us: small(): pl.pallas_call(kernel, out_shape=shapes, in_specs=specs or [SMEM if o.dty...]
    ppermute x0 -> x18, waiting for transfers between devices: none -> 6.94 us  [the longest x6 3.62 us: along_x(): lax.ppermute(array, 'ctx', [(z * NX + x, z * NX + (x ^ d)) for z in range...]
  transfers between devices with their start and end apart: 3 -> 18, of which waited for: 2 -> 8; matrix products, arithmetic and copies ran while one was open for 35% -> 0% of each run, Pallas kernels for 0% -> 37%
where the time goes in v1:
time: 68.4 us; the launch traced here: 68.3 us
  starting transfers between devices  33.5 us (49%)
  Pallas kernels  26.7 us (39%)
  waiting for transfers between devices  6.94 us (10%)
  other arithmetic  0.97 us (1%)
    pallas_call x13, Pallas kernels, small(): pl.pallas_call(kernel, out_shape=shapes, in_specs=specs or [SMEM if o.dty...  22.3 us
    ppermute x4, starting transfers between devices, across_z(): lax.ppermute(array, 'ctx', [(z * NX + x, target(z) % nz * NX + x) for z i...  11.2 us
    ppermute x7, starting transfers between devices, along_y(): lax.ppermute(array, 'head', [(y * 2 + c, (y ^ d) * 2 + c) for y in range(...  8.23 us
    ppermute x6, starting transfers between devices, along_x(): lax.ppermute(array, 'ctx', [(z * NX + x, z * NX + (x ^ d)) for z in range...  7.03 us
    ppermute x1, starting transfers between devices, shards(): got = lax.ppermute(send, 'head', [(i, i ^ 1) for i in range(nh)])  7.02 us
    ppermute x6, waiting for transfers between devices, along_x(): lax.ppermute(array, 'ctx', [(z * NX + x, z * NX + (x ^ d)) for z in range...  3.62 us
    pallas_call x2, Pallas kernels, add_far(): pl.pallas_call(functools.partial(far_kernel, side), grid=(width // column...  2.37 us
    ppermute x7, waiting for transfers between devices, along_y(): lax.ppermute(array, 'head', [(y * 2 + c, (y ^ d) * 2 + c) for y in range(...  2 us
  transfers between devices with their start and end apart: 18, of which 8 were waited for; matrix products, arithmetic and copies ran while one was open for 0% of the time, Pallas kernels for 37%

profile of v1, /device:TPU:1, one launch (start us, length us, event | category | flops | bytes accessed | tf_op | source)
XLA Modules:
  0.0 68.3 jit_solution(14518057014867772703)
XLA Ops:
  0.0 2.1 %collective-permute-start.7 = (bf16[256,2048]{1,0:T(8,128)(2,1)}, bf16[256,2048]{1,0:T(8,128)(2,1)S(1)}, u32[]{:S(2)}, u32[]{:S(2)}) collective-permute-start(bf16[256,2048]{1,0:T(8,128)(2,1)} %refs_3_.1), channel_id=1, source_target_pairs={{0,2},{1,3},{2,0},{3,1},{4,6},{5,7},{6,4},{7,5},{8,10},{9,11},{10,... | collective-permute-start | bytes 3145736 | tf_op jit(solution)/shard_map/ppermute | solution.py:440
  2.1 1.9 %collective-permute-start.8 = (bf16[256,2048]{1,0:T(8,128)(2,1)}, bf16[256,2048]{1,0:T(8,128)(2,1)S(1)}, u32[]{:S(2)}, u32[]{:S(2)}) collective-permute-start(bf16[256,2048]{1,0:T(8,128)(2,1)} %refs_3_.1), channel_id=1, source_target_pairs={{0,6},{1,7},{2,4},{3,5},{4,2},{5,3},{6,0},{7,1},{8,14},{9,15},{10,... | collective-permute-start | bytes 3145736 | tf_op jit(solution)/shard_map/ppermute | solution.py:440
  4.0 0.1 pad_add_fusion.place
  4.1 0.0 copy-start
  4.1 0.0 copy-start.1
  4.1 0.0 copy-start.2
  4.1 0.0 copy-start.4
  4.1 6.2 %shard_map.64 = (bf16[1024,512]{1,0:T(8,128)(2,1)S(1)}, bf16[2048,256]{1,0:T(8,128)(2,1)S(1)}) custom-call(bf16[1024,2048]{1,0:T(8,128)(2,1)} %acts.1, bf16[2048,768]{1,0:T(8,128)(2,1)} %weight_hbm.1), custom_call_target="tpu_custom_call" | custom-call | flops 2147483648 | bytes 1048576 | tf_op jit(solution)/shard_map/pallas_call | solution.py:403
  10.3 0.0 copy-done
  10.4 0.0 copy-done.1
  10.4 1.2 %shard_map.65 = (f32[8,2,128,128]{3,2,1,0:T(8,128)S(1)}, bf16[528,128]{1,0:T(8,128)(2,1)S(1)}, bf16[528,128]{1,0:T(8,128)(2,1)S(1)}, bf16[528,128]{1,0:T(8,128)(2,1)S(1)}, bf16[528,128]{1,0:T(8,128)(2,1)S(1)}) custom-call(s32[4]{0:T(128)S(1)} %pad_add_fusion.place, bf16[1024,512]{1,0:T(8,128)(2,1)S(1)} %get-tuple-element.30.kv, f32[2,1024]{1,0:T(2,128)S(1)} %bitcast.8, ...), custom_call_target="tpu_custom_call" | custom-call | bytes 1048576 | tf_op jit(solution)/shard_map/pallas_call | solution.py:403
  11.6 2.8 %collective-permute-start = (bf16[528,128]{1,0:T(8,128)(2,1)S(1)}, bf16[528,128]{1,0:T(8,128)(2,1)S(1)}, u32[]{:S(2)}, u32[]{:S(2)}) collective-permute-start(bf16[528,128]{1,0:T(8,128)(2,1)S(1)} %get-tuple-element.32), channel_id=1, source_target_pairs={{0,16},{8,24},{16,0},{24,8},{32,48},{40,56},{48,32},{56,40},{64,80... | collective-permute-start | bytes 405512 | tf_op jit(solution)/shard_map/ppermute | solution.py:430
  14.4 0.3 collective-permute-start.1
  14.7 0.6 collective-permute-start.2
  15.3 0.0 copy-done.2
  15.3 0.0 copy-done.4
  15.3 2.3 %shard_map.66 = (bf16[1024,256]{1,0:T(8,128)(2,1)S(1)}, f32[1024,128]{1,0:T(8,128)S(1)}) custom-call(bf16[1024,2048]{1,0:T(8,128)(2,1)S(1)} %copy-done.2, bf16[2048,256]{1,0:T(8,128)(2,1)S(1)} %get-tuple-element.35.weight, bf16[42,2048]{1,0:T(8,128)(2,1)S(1)} %bitcast.13, bf16[528,128]{1,0:T(8,128)(2,1)S(1)} %get-tuple-element.31.after.own), custom_call_target="tpu_custom_call" | custom-call | flops 2147483648 | bytes 1048576 | tf_op jit(solution)/shard_map/pallas_call | solution.py:403
  17.6 2.1 %shard_map.67.after.refs_2_ = bf16[1024,896]{1,0:T(8,128)(2,1)S(1)} custom-call(bf16[1024,256]{1,0:T(8,128)(2,1)S(1)} %get-tuple-element.36.query_rows, f32[1024,128]{1,0:T(8,128)S(1)} %get-tuple-element.37.level, f32[2,1024]{1,0:T(2,128)S(1)} %bitcast.9, bf16[528,128]{1,0:T(8,128)(2,1)S(1)} %get-tuple-element.31.after.own), custom_call_target="tpu_custom_call" | custom-call | flops 1073741824 | bytes 1048576 | tf_op jit(solution)/shard_map/pallas_call | solution.py:403
  19.7 0.0 collective-permute-done.two
  19.7 0.3 collective-permute-done.1.one
  20.0 1.0 %collective-permute-done.2.three = bf16[528,128]{1,0:T(8,128)(2,1)S(1)} collective-permute-done((bf16[528,128]{1,0:T(8,128)(2,1)S(1)}, bf16[528,128]{1,0:T(8,128)(2,1)S(1)}, u32[]{:S(2)}, u32[]{:S(2)}) %collective-permute-start.2) | collective-permute-done | bytes 135200 | tf_op jit(solution)/shard_map/ppermute | solution.py:430
  21.0 0.7 %shard_map.68 = (bf16[2,2,128,128]{3,2,1,0:T(8,128)(2,1)S(1)}, bf16[336,128]{1,0:T(8,128)(2,1)S(1)}, f32[8,128]{1,0:T(8,128)S(1)}) custom-call(s32[4]{0:T(128)S(1)} %pad_add_fusion.place, bf16[528,128]{1,0:T(8,128)(2,1)S(1)} %get-tuple-element.31.after.own, bf16[528,128]{1,0:T(8,128)(2,1)S(1)} %collective-permute-done.two, ...), custom_call_target="tpu_custom_call" | custom-call | bytes 1048576 | tf_op jit(solution)/shard_map/pallas_call | solution.py:403
  21.7 1.7 %collective-permute-start.3 = (bf16[336,128]{1,0:T(8,128)(2,1)S(1)}, bf16[336,128]{1,0:T(8,128)(2,1)S(1)}, u32[]{:S(2)}, u32[]{:S(2)}) collective-permute-start(bf16[336,128]{1,0:T(8,128)(2,1)S(1)} %get-tuple-element.38.after.own), channel_id=1, source_target_pairs={{0,32},{8,40},{16,48},{24,56},{32,0},{40,8},{48,16},{56,24},{64,96... | collective-permute-start | bytes 258056 | tf_op jit(solution)/shard_map/ppermute | solution.py:435
  23.4 1.9 %shard_map.69.after.refs_0_ = f32[1024,128]{1,0:T(8,128)S(1)} custom-call(bf16[1024,256]{1,0:T(8,128)(2,1)S(1)} %get-tuple-element.36.query_rows, bf16[1024,512]{1,0:T(8,128)(2,1)S(1)} %get-tuple-element.30.kv, f32[1024,128]{1,0:T(8,128)S(1)} %get-tuple-element.37.level, f32[2,1024]{1,0:T(2,128)S(1)} %bitcast.10, ...), custom_call_target="tpu_custom_call" | custom-call | flops 1073741824 | bytes 1048576 | tf_op jit(solution)/shard_map/pallas_call | solution.py:403
  25.3 0.3 collective-permute-done.3.got
  25.6 0.6 shard_map.70
  26.1 6.4 %collective-permute-start.4 = (bf16[336,128]{1,0:T(8,128)(2,1)S(1)}, bf16[336,128]{1,0:T(8,128)(2,1)S(1)}, u32[]{:S(2)}, u32[]{:S(2)}) collective-permute-start(bf16[336,128]{1,0:T(8,128)(2,1)S(1)} %get-tuple-element.42.after.own), channel_id=1, source_target_pairs={{0,160},{8,168},{16,176},{24,184},{32,128},{40,136},{48,144},{56,1... | collective-permute-start | bytes 258056 | tf_op jit(solution)/shard_map/ppermute | solution.py:435
  32.5 0.3 collective-permute-start.5
  32.8 2.8 %collective-permute-start.6 = (bf16[336,128]{1,0:T(8,128)(2,1)S(1)}, bf16[336,128]{1,0:T(8,128)(2,1)S(1)}, u32[]{:S(2)}, u32[]{:S(2)}) collective-permute-start(bf16[336,128]{1,0:T(8,128)(2,1)S(1)} %get-tuple-element.42.after.own), channel_id=1, source_target_pairs={{0,224},{8,232},{16,240},{24,248},{32,64},{40,72},{48,80},{56,88},... | collective-permute-start | bytes 258056 | tf_op jit(solution)/shard_map/ppermute | solution.py:435
  35.6 1.9 %shard_map.71.after.refs_1_ = f32[1024,128]{1,0:T(8,128)S(1)} custom-call(bf16[1024,256]{1,0:T(8,128)(2,1)S(1)} %get-tuple-element.36.query_rows, bf16[1024,512]{1,0:T(8,128)(2,1)S(1)} %get-tuple-element.30.kv, f32[1024,128]{1,0:T(8,128)S(1)} %get-tuple-element.37.level, f32[2,1024]{1,0:T(2,128)S(1)} %bitcast.11, ...), custom_call_target="tpu_custom_call" | custom-call | flops 1073741824 | bytes 1048576 | tf_op jit(solution)/shard_map/pallas_call | solution.py:403
  37.6 0.0 collective-permute-done.7.below.refs_4_
  37.6 0.0 collective-permute-done.8.above.refs_5_
  37.6 0.1 shard_map.72
  37.7 0.9 %collective-permute-start.13 = (bf16[128,2048]{1,0:T(8,128)(2,1)S(1)}, bf16[128,2048]{1,0:T(8,128)(2,1)S(1)}, u32[]{:S(2)}, u32[]{:S(2)}) collective-permute-start(bf16[128,2048]{1,0:T(8,128)(2,1)S(1)} %get-tuple-element.45.after), channel_id=1, source_target_pairs={{0,6},{1,7},{2,4},{3,5},{4,2},{5,3},{6,0},{7,1},{8,14},{9,15},{10,... | collective-permute-start | bytes 1572872 | tf_op jit(solution)/shard_map/ppermute | solution.py:440
  38.5 0.0 collective-permute-start.14
  38.5 0.0 collective-permute-done.4.far
  38.5 0.0 collective-permute-done.5.skip
  38.6 0.7 %collective-permute-done.6.near = bf16[336,128]{1,0:T(8,128)(2,1)S(1)} collective-permute-done((bf16[336,128]{1,0:T(8,128)(2,1)S(1)}, bf16[336,128]{1,0:T(8,128)(2,1)S(1)}, u32[]{:S(2)}, u32[]{:S(2)}) %collective-permute-start.6) | collective-permute-done | bytes 86048 | tf_op jit(solution)/shard_map/ppermute | solution.py:435
  39.3 0.6 shard_map.73
  39.9 0.7 collective-permute-start.10
  40.5 2.0 %collective-permute-start.11 = (bf16[448,128]{1,0:T(8,128)(2,1)S(1)}, bf16[448,128]{1,0:T(8,128)(2,1)S(1)}, u32[]{:S(2)}, u32[]{:S(2)}) collective-permute-start(bf16[448,128]{1,0:T(8,128)(2,1)S(1)} %get-tuple-element.47.after.refs_4_), channel_id=1, source_target_pairs={{0,24},{8,16},{16,8},{24,0},{32,56},{40,48},{48,40},{56,32},{64,88... | collective-permute-start | bytes 344072 | tf_op jit(solution)/shard_map/ppermute | solution.py:430
  42.5 0.7 %collective-permute-start.9 = (bf16[448,128]{1,0:T(8,128)(2,1)S(1)}, bf16[448,128]{1,0:T(8,128)(2,1)S(1)}, u32[]{:S(2)}, u32[]{:S(2)}) collective-permute-start(bf16[448,128]{1,0:T(8,128)(2,1)S(1)} %get-tuple-element.47.after.refs_4_), channel_id=1, source_target_pairs={{0,16},{8,24},{16,0},{24,8},{32,48},{40,56},{48,32},{56,40},{64,80... | collective-permute-start | bytes 344072 | tf_op jit(solution)/shard_map/ppermute | solution.py:430
  43.2 2.1 %shard_map.74.refs_3_ = bf16[1024,896]{1,0:T(8,128)(2,1)S(1)} custom-call(bf16[1024,256]{1,0:T(8,128)(2,1)S(1)} %get-tuple-element.36.query_rows, f32[1024,128]{1,0:T(8,128)S(1)} %get-tuple-element.37.level, f32[2,1024]{1,0:T(2,128)S(1)} %bitcast.12, bf16[448,128]{1,0:T(8,128)(2,1)S(1)} %get-tuple-element.47.after.refs_4_), custom_call_target="tpu_custom_call" | custom-call | flops 1073741824 | bytes 1048576 | tf_op jit(solution)/shard_map/pallas_call | solution.py:403
  45.3 0.0 collective-permute-done.10.refs_6_
  45.3 0.1 collective-permute-done.11.refs_7_
  45.4 2.3 %collective-permute-done.9.refs_5_ = bf16[448,128]{1,0:T(8,128)(2,1)S(1)} collective-permute-done((bf16[448,128]{1,0:T(8,128)(2,1)S(1)}, bf16[448,128]{1,0:T(8,128)(2,1)S(1)}, u32[]{:S(2)}, u32[]{:S(2)}) %collective-permute-start.9) | collective-permute-done | bytes 114720 | tf_op jit(solution)/shard_map/ppermute | solution.py:430
  47.7 1.6 %shard_map.75 = (bf16[256,256]{1,0:T(8,128)(2,1)S(1)}, bf16[256,256]{1,0:T(8,128)(2,1)S(1)}, bf16[256,256]{1,0:T(8,128)(2,1)S(1)}, bf16[2,896,128]{2,1,0:T(8,128)(2,1)S(1)}) custom-call(s32[4]{0:T(128)S(1)} %pad_add_fusion.place, f32[8,128]{1,0:T(8,128)S(1)} %get-tuple-element.46.carry, f32[1024,128]{1,0:T(8,128)S(1)} %shard_map.69.after.refs_0_, ...), custom_call_target="tpu_custom_call" | custom-call | flops 268435456 | bytes 1048576 | tf_op jit(solution)/shard_map/pallas_call | solution.py:403
  49.3 0.0 copy-start.3
  49.3 1.1 %collective-permute-start.15 = (bf16[256,256]{1,0:T(8,128)(2,1)S(1)}, bf16[256,256]{1,0:T(8,128)(2,1)S(1)}, u32[]{:S(2)}, u32[]{:S(2)}) collective-permute-start(bf16[256,256]{1,0:T(8,128)(2,1)S(1)} %get-tuple-element.51.refs_5_), channel_id=1, source_target_pairs={{0,2},{1,3},{2,0},{3,1},{4,6},{5,7},{6,4},{7,5},{8,10},{9,11},{10,... | collective-permute-start | bytes 393224 | tf_op jit(solution)/shard_map/ppermute | solution.py:440
  50.4 1.9 %collective-permute-start.16 = (bf16[256,256]{1,0:T(8,128)(2,1)S(1)}, bf16[256,256]{1,0:T(8,128)(2,1)S(1)}, u32[]{:S(2)}, u32[]{:S(2)}) collective-permute-start(bf16[256,256]{1,0:T(8,128)(2,1)S(1)} %get-tuple-element.52), channel_id=1, source_target_pairs={{0,6},{1,7},{2,4},{3,5},{4,2},{5,3},{6,0},{7,1},{8,14},{9,15},{10,... | collective-permute-start | bytes 393224 | tf_op jit(solution)/shard_map/ppermute | solution.py:440
  52.3 0.3 collective-permute-start.12
  52.6 1.0 %shard_map.76.refs_0_ = bf16[256,256]{1,0:T(8,128)(2,1)S(1)} custom-call(s32[4]{0:T(128)S(1)} %pad_add_fusion.place, f32[1024,128]{1,0:T(8,128)S(1)} %shard_map.69.after.refs_0_, f32[1024,128]{1,0:T(8,128)S(1)} %shard_map.71.after.refs_1_, bf16[1024,896]{1,0:T(8,128)(2,1)S(1)} %shard_map.67.after.refs_2_, bf16[1024,896]{1,0:T(8,128)(2,1)S(1)} %shard_map.74.refs_3_, ...), custom_call_target="tpu_custom_call" | custom-call | flops 268435456 | bytes 1048576 | tf_op jit(solution)/shard_map/pallas_call | solution.py:403
  53.7 0.0 collective-permute-done.15.refs_1_
  53.7 2.0 %collective-permute-done.16.refs_2_ = bf16[256,256]{1,0:T(8,128)(2,1)S(1)} collective-permute-done((bf16[256,256]{1,0:T(8,128)(2,1)S(1)}, bf16[256,256]{1,0:T(8,128)(2,1)S(1)}, u32[]{:S(2)}, u32[]{:S(2)}) %collective-permute-start.16) | collective-permute-done | bytes 131104 | tf_op jit(solution)/shard_map/ppermute | solution.py:440
  55.6 0.0 copy-done.3
  55.6 2.0 %shard_map.77 = (f32[128,2048]{1,0:T(8,128)S(1)}, f32[128,2048]{1,0:T(8,128)S(1)}) custom-call(s32[4]{0:T(128)S(1)} %pad_add_fusion.place, bf16[256,256]{1,0:T(8,128)(2,1)S(1)} %shard_map.76.refs_0_, bf16[256,256]{1,0:T(8,128)(2,1)S(1)} %collective-permute-done.15.refs_1_, bf16[256,256]{1,0:T(8,128)(2,1)S(1)} %collective-permute-done.16.refs_2_, ...), custom_call_target="tpu_custom_call" | custom-call | flops 2147483648 | bytes 5242880 | tf_op jit(solution)/shard_map/pallas_call | solution.py:604
  57.6 0.0 collective-permute-done.12.piece
  57.7 0.0 collective-permute-done.13.first
  57.7 0.0 collective-permute-done.14.second
  57.7 1.2 %shard_map.79 = bf16[128,2048]{1,0:T(8,128)(2,1)S(1)} custom-call(s32[4]{0:T(128)S(1)} %pad_add_fusion.place, bf16[256,256]{1,0:T(8,128)(2,1)S(1)} %collective-permute-done.12.piece, bf16[128,2048]{1,0:T(8,128)(2,1)S(1)} %collective-permute-done.13.first, bf16[128,2048]{1,0:T(8,128)(2,1)S(1)} %collective-permute-done.14.second, ...), custom_call_target="tpu_custom_call" | custom-call | flops 268435456 | bytes 3145728 | tf_op jit(solution)/shard_map/pallas_call | solution.py:616
  58.9 7.0 %collective-permute-start.17 = (bf16[128,2048]{1,0:T(8,128)(2,1)S(1)}, bf16[128,2048]{1,0:T(8,128)(2,1)S(1)}, u32[]{:S(2)}, u32[]{:S(2)}) collective-permute-start(bf16[128,2048]{1,0:T(8,128)(2,1)S(1)} %shard_map.79), channel_id=1, source_target_pairs={{0,1},{1,0},{2,3},{3,2},{4,5},{5,4},{6,7},{7,6},{8,9},{9,8},{10,11... | collective-permute-start | bytes 1572872 | tf_op jit(solution)/shard_map/ppermute | solution.py:627
  65.9 1.2 %shard_map.78 = f32[128,2048]{1,0:T(8,128)S(1)} custom-call(s32[4]{0:T(128)S(1)} %pad_add_fusion.place, bf16[256,256]{1,0:T(8,128)(2,1)S(1)} %collective-permute-done.12.piece, bf16[128,2048]{1,0:T(8,128)(2,1)S(1)} %collective-permute-done.13.first, bf16[128,2048]{1,0:T(8,128)(2,1)S(1)} %collective-permute-done.14.second, f32[128,2048]{1,0:T(8,128)S(1)} %get-tuple-element.53.near), custom_call_target="tpu_custom_call" | custom-call | flops 268435456 | bytes 3145728 | tf_op jit(solution)/shard_map/pallas_call | solution.py:616
  67.1 0.3 collective-permute-done.17
  67.4 0.9 %add_convert_fusion = bf16[128,2048]{1,0:T(8,128)(2,1)} fusion(f32[128,2048]{1,0:T(8,128)S(1)} %shard_map.78, bf16[128,2048]{1,0:T(8,128)(2,1)S(1)} %collective-permute-done.17), kind=kLoop, calls=%fused_computation | loop fusion | flops 786432 | bytes 2097152 | tf_op jit(solution)/shard_map/convert_element_type | solution.py:629
Async XLA Ops:
  0.0 37.6 %collective-permute-start.7 = (bf16[256,2048]{1,0:T(8,128)(2,1)}, bf16[256,2048]{1,0:T(8,128)(2,1)S(1)}, u32[]{:S(2)}, u32[]{:S(2)}) collective-permute-start(bf16[256,2048]{1,0:T(8,128)(2,1)} %refs_3_.1), channel_id=1, source_target_pairs={{0,2},{1,3},{2,0},{3,1},{4,6},{5,7},{6,4},{7,5},{8,10},{9,11},{10,... | collective-permute-start | bytes 3145736 | tf_op jit(solution)/shard_map/ppermute | solution.py:440
  2.1 35.4 %collective-permute-start.8 = (bf16[256,2048]{1,0:T(8,128)(2,1)}, bf16[256,2048]{1,0:T(8,128)(2,1)S(1)}, u32[]{:S(2)}, u32[]{:S(2)}) collective-permute-start(bf16[256,2048]{1,0:T(8,128)(2,1)} %refs_3_.1), channel_id=1, source_target_pairs={{0,6},{1,7},{2,4},{3,5},{4,2},{5,3},{6,0},{7,1},{8,14},{9,15},{10,... | collective-permute-start | bytes 3145736 | tf_op jit(solution)/shard_map/ppermute | solution.py:440
  4.1 6.2 %copy-start = (f32[1,4,2,128,128]{4,3,2,1,0:T(8,128)S(1)}, f32[1,4,2,128,128]{4,3,2,1,0:T(8,128)}, u32[]{:S(2)}) copy-start(f32[1,4,2,128,128]{4,3,2,1,0:T(8,128)} %param.10) | copy-start | bytes 1572868
  4.1 6.3 %copy-start.1 = (f32[1024,2]{0,1:T(2,128)S(1)}, f32[1024,2]{0,1:T(2,128)}, u32[]{:S(2)}) copy-start(f32[1024,2]{0,1:T(2,128)} %param.9) | copy-start | bytes 24580
  4.1 11.2 %copy-start.2 = (bf16[1024,2048]{1,0:T(8,128)(2,1)S(1)}, bf16[1024,2048]{1,0:T(8,128)(2,1)}, u32[]{:S(2)}) copy-start(bf16[1024,2048]{1,0:T(8,128)(2,1)} %acts.1) | copy-start | bytes 12582916
  4.1 11.2 %copy-start.4 = (bf16[2048,42]{0,1:T(8,128)(2,1)S(1)}, bf16[2048,42]{0,1:T(8,128)(2,1)}, u32[]{:S(2)}) copy-start(bf16[2048,42]{0,1:T(8,128)(2,1)} %param.8) | copy-start | bytes 516100
  11.6 8.1 %collective-permute-start = (bf16[528,128]{1,0:T(8,128)(2,1)S(1)}, bf16[528,128]{1,0:T(8,128)(2,1)S(1)}, u32[]{:S(2)}, u32[]{:S(2)}) collective-permute-start(bf16[528,128]{1,0:T(8,128)(2,1)S(1)} %get-tuple-element.32), channel_id=1, source_target_pairs={{0,16},{8,24},{16,0},{24,8},{32,48},{40,56},{48,32},{56,40},{64,80... | collective-permute-start | bytes 405512 | tf_op jit(solution)/shard_map/ppermute | solution.py:430
  14.4 5.6 %collective-permute-start.1 = (bf16[528,128]{1,0:T(8,128)(2,1)S(1)}, bf16[528,128]{1,0:T(8,128)(2,1)S(1)}, u32[]{:S(2)}, u32[]{:S(2)}) collective-permute-start(bf16[528,128]{1,0:T(8,128)(2,1)S(1)} %get-tuple-element.33), channel_id=1, source_target_pairs={{0,8},{8,0},{16,24},{24,16},{32,40},{40,32},{48,56},{56,48},{64,72... | collective-permute-start | bytes 405512 | tf_op jit(solution)/shard_map/ppermute | solution.py:430
  14.7 6.2 %collective-permute-start.2 = (bf16[528,128]{1,0:T(8,128)(2,1)S(1)}, bf16[528,128]{1,0:T(8,128)(2,1)S(1)}, u32[]{:S(2)}, u32[]{:S(2)}) collective-permute-start(bf16[528,128]{1,0:T(8,128)(2,1)S(1)} %get-tuple-element.34), channel_id=1, source_target_pairs={{0,24},{8,16},{16,8},{24,0},{32,56},{40,48},{48,40},{56,32},{64,88... | collective-permute-start | bytes 405512 | tf_op jit(solution)/shard_map/ppermute | solution.py:430
  21.7 3.9 %collective-permute-start.3 = (bf16[336,128]{1,0:T(8,128)(2,1)S(1)}, bf16[336,128]{1,0:T(8,128)(2,1)S(1)}, u32[]{:S(2)}, u32[]{:S(2)}) collective-permute-start(bf16[336,128]{1,0:T(8,128)(2,1)S(1)} %get-tuple-element.38.after.own), channel_id=1, source_target_pairs={{0,32},{8,40},{16,48},{24,56},{32,0},{40,8},{48,16},{56,24},{64,96... | collective-permute-start | bytes 258056 | tf_op jit(solution)/shard_map/ppermute | solution.py:435
  26.1 12.4 %collective-permute-start.4 = (bf16[336,128]{1,0:T(8,128)(2,1)S(1)}, bf16[336,128]{1,0:T(8,128)(2,1)S(1)}, u32[]{:S(2)}, u32[]{:S(2)}) collective-permute-start(bf16[336,128]{1,0:T(8,128)(2,1)S(1)} %get-tuple-element.42.after.own), channel_id=1, source_target_pairs={{0,160},{8,168},{16,176},{24,184},{32,128},{40,136},{48,144},{56,1... | collective-permute-start | bytes 258056 | tf_op jit(solution)/shard_map/ppermute | solution.py:435
  32.5 6.0 %collective-permute-start.5 = (bf16[336,128]{1,0:T(8,128)(2,1)S(1)}, bf16[336,128]{1,0:T(8,128)(2,1)S(1)}, u32[]{:S(2)}, u32[]{:S(2)}) collective-permute-start(bf16[336,128]{1,0:T(8,128)(2,1)S(1)} %get-tuple-element.42.after.own), channel_id=1, source_target_pairs={{0,192},{8,200},{16,208},{24,216},{32,96},{40,104},{48,112},{56,12... | collective-permute-start | bytes 258056 | tf_op jit(solution)/shard_map/ppermute | solution.py:435
  32.8 6.5 %collective-permute-start.6 = (bf16[336,128]{1,0:T(8,128)(2,1)S(1)}, bf16[336,128]{1,0:T(8,128)(2,1)S(1)}, u32[]{:S(2)}, u32[]{:S(2)}) collective-permute-start(bf16[336,128]{1,0:T(8,128)(2,1)S(1)} %get-tuple-element.42.after.own), channel_id=1, source_target_pairs={{0,224},{8,232},{16,240},{24,248},{32,64},{40,72},{48,80},{56,88},... | collective-permute-start | bytes 258056 | tf_op jit(solution)/shard_map/ppermute | solution.py:435
  37.7 20.0 %collective-permute-start.13 = (bf16[128,2048]{1,0:T(8,128)(2,1)S(1)}, bf16[128,2048]{1,0:T(8,128)(2,1)S(1)}, u32[]{:S(2)}, u32[]{:S(2)}) collective-permute-start(bf16[128,2048]{1,0:T(8,128)(2,1)S(1)} %get-tuple-element.45.after), channel_id=1, source_target_pairs={{0,6},{1,7},{2,4},{3,5},{4,2},{5,3},{6,0},{7,1},{8,14},{9,15},{10,... | collective-permute-start | bytes 1572872 | tf_op jit(solution)/shard_map/ppermute | solution.py:440
  38.5 19.1 %collective-permute-start.14 = (bf16[128,2048]{1,0:T(8,128)(2,1)S(1)}, bf16[128,2048]{1,0:T(8,128)(2,1)S(1)}, u32[]{:S(2)}, u32[]{:S(2)}) collective-permute-start(bf16[128,2048]{1,0:T(8,128)(2,1)S(1)} %get-tuple-element.49), channel_id=1, source_target_pairs={{0,2},{1,3},{2,0},{3,1},{4,6},{5,7},{6,4},{7,5},{8,10},{9,11},{10,... | collective-permute-start | bytes 1572872 | tf_op jit(solution)/shard_map/ppermute | solution.py:440
  39.9 5.4 %collective-permute-start.10 = (bf16[448,128]{1,0:T(8,128)(2,1)S(1)}, bf16[448,128]{1,0:T(8,128)(2,1)S(1)}, u32[]{:S(2)}, u32[]{:S(2)}) collective-permute-start(bf16[448,128]{1,0:T(8,128)(2,1)S(1)} %get-tuple-element.47.after.refs_4_), channel_id=1, source_target_pairs={{0,8},{8,0},{16,24},{24,16},{32,40},{40,32},{48,56},{56,48},{64,72... | collective-permute-start | bytes 344072 | tf_op jit(solution)/shard_map/ppermute | solution.py:430
  40.5 4.9 %collective-permute-start.11 = (bf16[448,128]{1,0:T(8,128)(2,1)S(1)}, bf16[448,128]{1,0:T(8,128)(2,1)S(1)}, u32[]{:S(2)}, u32[]{:S(2)}) collective-permute-start(bf16[448,128]{1,0:T(8,128)(2,1)S(1)} %get-tuple-element.47.after.refs_4_), channel_id=1, source_target_pairs={{0,24},{8,16},{16,8},{24,0},{32,56},{40,48},{48,40},{56,32},{64,88... | collective-permute-start | bytes 344072 | tf_op jit(solution)/shard_map/ppermute | solution.py:430
  42.5 5.2 %collective-permute-start.9 = (bf16[448,128]{1,0:T(8,128)(2,1)S(1)}, bf16[448,128]{1,0:T(8,128)(2,1)S(1)}, u32[]{:S(2)}, u32[]{:S(2)}) collective-permute-start(bf16[448,128]{1,0:T(8,128)(2,1)S(1)} %get-tuple-element.47.after.refs_4_), channel_id=1, source_target_pairs={{0,16},{8,24},{16,0},{24,8},{32,48},{40,56},{48,32},{56,40},{64,80... | collective-permute-start | bytes 344072 | tf_op jit(solution)/shard_map/ppermute | solution.py:430
  49.3 6.4 %copy-start.3 = (bf16[256,2048]{1,0:T(8,128)(2,1)S(1)}, bf16[256,2048]{1,0:T(8,128)(2,1)}, u32[]{:S(2)}) copy-start(bf16[256,2048]{1,0:T(8,128)(2,1)} %refs_3_.1) | copy-start | bytes 3145732
  49.3 4.4 %collective-permute-start.15 = (bf16[256,256]{1,0:T(8,128)(2,1)S(1)}, bf16[256,256]{1,0:T(8,128)(2,1)S(1)}, u32[]{:S(2)}, u32[]{:S(2)}) collective-permute-start(bf16[256,256]{1,0:T(8,128)(2,1)S(1)} %get-tuple-element.51.refs_5_), channel_id=1, source_target_pairs={{0,2},{1,3},{2,0},{3,1},{4,6},{5,7},{6,4},{7,5},{8,10},{9,11},{10,... | collective-permute-start | bytes 393224 | tf_op jit(solution)/shard_map/ppermute | solution.py:440
  50.4 5.2 %collective-permute-start.16 = (bf16[256,256]{1,0:T(8,128)(2,1)S(1)}, bf16[256,256]{1,0:T(8,128)(2,1)S(1)}, u32[]{:S(2)}, u32[]{:S(2)}) collective-permute-start(bf16[256,256]{1,0:T(8,128)(2,1)S(1)} %get-tuple-element.52), channel_id=1, source_target_pairs={{0,6},{1,7},{2,4},{3,5},{4,2},{5,3},{6,0},{7,1},{8,14},{9,15},{10,... | collective-permute-start | bytes 393224 | tf_op jit(solution)/shard_map/ppermute | solution.py:440
  52.3 5.3 %collective-permute-start.12 = (bf16[256,256]{1,0:T(8,128)(2,1)S(1)}, bf16[256,256]{1,0:T(8,128)(2,1)S(1)}, u32[]{:S(2)}, u32[]{:S(2)}) collective-permute-start(bf16[256,256]{1,0:T(8,128)(2,1)S(1)} %get-tuple-element.48), channel_id=1, source_target_pairs={{0,4},{1,5},{2,6},{3,7},{4,0},{5,1},{6,2},{7,3},{8,12},{9,13},{10,... | collective-permute-start | bytes 393224 | tf_op jit(solution)/shard_map/ppermute | solution.py:440
  58.9 8.6 %collective-permute-start.17 = (bf16[128,2048]{1,0:T(8,128)(2,1)S(1)}, bf16[128,2048]{1,0:T(8,128)(2,1)S(1)}, u32[]{:S(2)}, u32[]{:S(2)}) collective-permute-start(bf16[128,2048]{1,0:T(8,128)(2,1)S(1)} %shard_map.79), channel_id=1, source_target_pairs={{0,1},{1,0},{2,3},{3,2},{4,5},{5,4},{6,7},{7,6},{8,9},{9,8},{10,11... | collective-permute-start | bytes 1572872 | tf_op jit(solution)/shard_map/ppermute | solution.py:627

commit v2 on v1

--- a/solution.py
+++ b/solution.py
@@ -335,7 +335,7 @@
 def finish_kernel(place, carry, *refs):
     heads = 2
     insides, lefts, refs = refs[:heads], refs[heads : 2 * heads], refs[2 * heads :]
-    own, two, one, three = refs[:NX]
+    own, one, two, three = refs[:NX]
     pieces, outs, states = (own, one, two, three), refs[NX:-1], refs[-1]
     z_bits = lefts[0].shape[1] // DH - PRIOR
     x = place[0]
@@ -579,8 +579,8 @@
         *insides,
         *lefts,
         pieces[0],
+        pieces[1],
         pieces[2],
-        pieces[1],
         pieces[3],
         flops=1 << 28,
     )
@@ -610,7 +610,7 @@
         scratch_shapes=[pltpu.VMEM((3, 2 * CHUNK, rows), BF16)],
         compiler_params=params(24),
         cost_estimate=pl.CostEstimate(flops=8 << 28, bytes_accessed=5 << 20, transcendentals=0),
-    )(place, normed[0], normed[1], normed[3], out_weight, below, above)
+    )(place, normed[0], normed[3], normed[1], out_weight, above, below)
 
     def add_far(side, near, dtype):
         return pl.pallas_call(

time: 68.4 us -> 66.9 us (0.978)
  waiting for transfers between devices: 6.94 us -> 5.65 us
    ppermute x7, waiting for transfers between devices: 2 us -> 0.75 us  [along_y(): lax.ppermute(array, 'head', [(y * 2 + c, (y ^ d) * 2 + c) for y in range(...]
  transfers between devices with their start and end apart: 18 -> 18, of which waited for: 8 -> 10; matrix products, arithmetic and copies ran while one was open for 0% -> 0% of each run, Pallas kernels for 37% -> 38%
where the time goes in v2:
time: 66.9 us
  starting transfers between devices  33.4 us (50%)
  Pallas kernels  26.7 us (40%)
  waiting for transfers between devices  5.65 us (8%)
  other arithmetic  0.97 us (1%)
    pallas_call x13, Pallas kernels, small(): pl.pallas_call(kernel, out_shape=shapes, in_specs=specs or [SMEM if o.dty...  22.3 us
    ppermute x4, starting transfers between devices, across_z(): lax.ppermute(array, 'ctx', [(z * NX + x, target(z) % nz * NX + x) for z i...  11.2 us
    ppermute x7, starting transfers between devices, along_y(): lax.ppermute(array, 'head', [(y * 2 + c, (y ^ d) * 2 + c) for y in range(...  8.84 us
    ppermute x6, starting transfers between devices, along_x(): lax.ppermute(array, 'ctx', [(z * NX + x, z * NX + (x ^ d)) for z in range...  6.77 us
    ppermute x1, starting transfers between devices, shards(): got = lax.ppermute(send, 'head', [(i, i ^ 1) for i in range(nh)])  6.55 us
    ppermute x6, waiting for transfers between devices, along_x(): lax.ppermute(array, 'ctx', [(z * NX + x, z * NX + (x ^ d)) for z in range...  3.59 us
    pallas_call x2, Pallas kernels, add_far(): pl.pallas_call(functools.partial(far_kernel, side), grid=(width // column...  2.36 us
    pallas_call x1, Pallas kernels, shards(): pl.pallas_call(near_kernel, grid=(width // columns,), in_specs=[SMEM] + [...  1.99 us
  transfers between devices with their start and end apart: 18, of which 10 were waited for; matrix products, arithmetic and copies ran while one was open for 0% of the time, Pallas kernels for 38%

profile of v2, /device:TPU:1, one launch (start us, length us, event | category | flops | bytes accessed | tf_op | source)
XLA Modules:
  0.0 66.9 jit_solution(12143361000036188152)
XLA Ops:
  0.0 2.1 %collective-permute-start.7 = (bf16[256,2048]{1,0:T(8,128)(2,1)}, bf16[256,2048]{1,0:T(8,128)(2,1)S(1)}, u32[]{:S(2)}, u32[]{:S(2)}) collective-permute-start(bf16[256,2048]{1,0:T(8,128)(2,1)} %refs_3_.1), channel_id=1, source_target_pairs={{0,2},{1,3},{2,0},{3,1},{4,6},{5,7},{6,4},{7,5},{8,10},{9,11},{10,... | collective-permute-start | bytes 3145736 | tf_op jit(solution)/shard_map/ppermute | solution.py:440
  2.1 1.9 %collective-permute-start.8 = (bf16[256,2048]{1,0:T(8,128)(2,1)}, bf16[256,2048]{1,0:T(8,128)(2,1)S(1)}, u32[]{:S(2)}, u32[]{:S(2)}) collective-permute-start(bf16[256,2048]{1,0:T(8,128)(2,1)} %refs_3_.1), channel_id=1, source_target_pairs={{0,6},{1,7},{2,4},{3,5},{4,2},{5,3},{6,0},{7,1},{8,14},{9,15},{10,... | collective-permute-start | bytes 3145736 | tf_op jit(solution)/shard_map/ppermute | solution.py:440
  4.0 0.1 pad_add_fusion.place
  4.1 0.0 copy-start
  4.1 0.0 copy-start.1
  4.1 0.0 copy-start.2
  4.1 0.0 copy-start.4
  4.1 6.2 %shard_map.64 = (bf16[1024,512]{1,0:T(8,128)(2,1)S(1)}, bf16[2048,256]{1,0:T(8,128)(2,1)S(1)}) custom-call(bf16[1024,2048]{1,0:T(8,128)(2,1)} %acts.1, bf16[2048,768]{1,0:T(8,128)(2,1)} %weight_hbm.1), custom_call_target="tpu_custom_call" | custom-call | flops 2147483648 | bytes 1048576 | tf_op jit(solution)/shard_map/pallas_call | solution.py:403
  10.3 0.0 copy-done
  10.4 0.0 copy-done.1
  10.4 1.2 %shard_map.65 = (f32[8,2,128,128]{3,2,1,0:T(8,128)S(1)}, bf16[528,128]{1,0:T(8,128)(2,1)S(1)}, bf16[528,128]{1,0:T(8,128)(2,1)S(1)}, bf16[528,128]{1,0:T(8,128)(2,1)S(1)}, bf16[528,128]{1,0:T(8,128)(2,1)S(1)}) custom-call(s32[4]{0:T(128)S(1)} %pad_add_fusion.place, bf16[1024,512]{1,0:T(8,128)(2,1)S(1)} %get-tuple-element.30.kv, f32[2,1024]{1,0:T(2,128)S(1)} %bitcast.8, ...), custom_call_target="tpu_custom_call" | custom-call | bytes 1048576 | tf_op jit(solution)/shard_map/pallas_call | solution.py:403
  11.6 2.8 %collective-permute-start = (bf16[528,128]{1,0:T(8,128)(2,1)S(1)}, bf16[528,128]{1,0:T(8,128)(2,1)S(1)}, u32[]{:S(2)}, u32[]{:S(2)}) collective-permute-start(bf16[528,128]{1,0:T(8,128)(2,1)S(1)} %get-tuple-element.32), channel_id=1, source_target_pairs={{0,16},{8,24},{16,0},{24,8},{32,48},{40,56},{48,32},{56,40},{64,80... | collective-permute-start | bytes 405512 | tf_op jit(solution)/shard_map/ppermute | solution.py:430
  14.4 0.3 collective-permute-start.1
  14.7 0.6 collective-permute-start.2
  15.3 0.0 copy-done.2
  15.3 0.0 copy-done.4
  15.3 2.3 %shard_map.66 = (bf16[1024,256]{1,0:T(8,128)(2,1)S(1)}, f32[1024,128]{1,0:T(8,128)S(1)}) custom-call(bf16[1024,2048]{1,0:T(8,128)(2,1)S(1)} %copy-done.2, bf16[2048,256]{1,0:T(8,128)(2,1)S(1)} %get-tuple-element.35.weight, bf16[42,2048]{1,0:T(8,128)(2,1)S(1)} %bitcast.13, bf16[528,128]{1,0:T(8,128)(2,1)S(1)} %get-tuple-element.31.after.own), custom_call_target="tpu_custom_call" | custom-call | flops 2147483648 | bytes 1048576 | tf_op jit(solution)/shard_map/pallas_call | solution.py:403
  17.6 2.1 %shard_map.67.after.refs_2_ = bf16[1024,896]{1,0:T(8,128)(2,1)S(1)} custom-call(bf16[1024,256]{1,0:T(8,128)(2,1)S(1)} %get-tuple-element.36.query_rows, f32[1024,128]{1,0:T(8,128)S(1)} %get-tuple-element.37.level, f32[2,1024]{1,0:T(2,128)S(1)} %bitcast.9, bf16[528,128]{1,0:T(8,128)(2,1)S(1)} %get-tuple-element.31.after.own), custom_call_target="tpu_custom_call" | custom-call | flops 1073741824 | bytes 1048576 | tf_op jit(solution)/shard_map/pallas_call | solution.py:403
  19.7 0.0 collective-permute-done.two
  19.7 0.3 collective-permute-done.1.one
  20.0 1.0 %collective-permute-done.2.three = bf16[528,128]{1,0:T(8,128)(2,1)S(1)} collective-permute-done((bf16[528,128]{1,0:T(8,128)(2,1)S(1)}, bf16[528,128]{1,0:T(8,128)(2,1)S(1)}, u32[]{:S(2)}, u32[]{:S(2)}) %collective-permute-start.2) | collective-permute-done | bytes 135200 | tf_op jit(solution)/shard_map/ppermute | solution.py:430
  21.0 0.7 %shard_map.68 = (bf16[2,2,128,128]{3,2,1,0:T(8,128)(2,1)S(1)}, bf16[336,128]{1,0:T(8,128)(2,1)S(1)}, f32[8,128]{1,0:T(8,128)S(1)}) custom-call(s32[4]{0:T(128)S(1)} %pad_add_fusion.place, bf16[528,128]{1,0:T(8,128)(2,1)S(1)} %get-tuple-element.31.after.own, bf16[528,128]{1,0:T(8,128)(2,1)S(1)} %collective-permute-done.two, ...), custom_call_target="tpu_custom_call" | custom-call | bytes 1048576 | tf_op jit(solution)/shard_map/pallas_call | solution.py:403
  21.7 1.7 %collective-permute-start.3 = (bf16[336,128]{1,0:T(8,128)(2,1)S(1)}, bf16[336,128]{1,0:T(8,128)(2,1)S(1)}, u32[]{:S(2)}, u32[]{:S(2)}) collective-permute-start(bf16[336,128]{1,0:T(8,128)(2,1)S(1)} %get-tuple-element.38.after.own), channel_id=1, source_target_pairs={{0,32},{8,40},{16,48},{24,56},{32,0},{40,8},{48,16},{56,24},{64,96... | collective-permute-start | bytes 258056 | tf_op jit(solution)/shard_map/ppermute | solution.py:435
  23.4 1.9 %shard_map.69.after.refs_0_ = f32[1024,128]{1,0:T(8,128)S(1)} custom-call(bf16[1024,256]{1,0:T(8,128)(2,1)S(1)} %get-tuple-element.36.query_rows, bf16[1024,512]{1,0:T(8,128)(2,1)S(1)} %get-tuple-element.30.kv, f32[1024,128]{1,0:T(8,128)S(1)} %get-tuple-element.37.level, f32[2,1024]{1,0:T(2,128)S(1)} %bitcast.10, ...), custom_call_target="tpu_custom_call" | custom-call | flops 1073741824 | bytes 1048576 | tf_op jit(solution)/shard_map/pallas_call | solution.py:403
  25.3 0.3 collective-permute-done.3.got
  25.6 0.6 shard_map.70
  26.1 6.4 %collective-permute-start.4 = (bf16[336,128]{1,0:T(8,128)(2,1)S(1)}, bf16[336,128]{1,0:T(8,128)(2,1)S(1)}, u32[]{:S(2)}, u32[]{:S(2)}) collective-permute-start(bf16[336,128]{1,0:T(8,128)(2,1)S(1)} %get-tuple-element.42.after.own), channel_id=1, source_target_pairs={{0,160},{8,168},{16,176},{24,184},{32,128},{40,136},{48,144},{56,1... | collective-permute-start | bytes 258056 | tf_op jit(solution)/shard_map/ppermute | solution.py:435
  32.5 0.3 collective-permute-start.5
  32.8 2.8 %collective-permute-start.6 = (bf16[336,128]{1,0:T(8,128)(2,1)S(1)}, bf16[336,128]{1,0:T(8,128)(2,1)S(1)}, u32[]{:S(2)}, u32[]{:S(2)}) collective-permute-start(bf16[336,128]{1,0:T(8,128)(2,1)S(1)} %get-tuple-element.42.after.own), channel_id=1, source_target_pairs={{0,224},{8,232},{16,240},{24,248},{32,64},{40,72},{48,80},{56,88},... | collective-permute-start | bytes 258056 | tf_op jit(solution)/shard_map/ppermute | solution.py:435
  35.6 1.9 %shard_map.71.after.refs_1_ = f32[1024,128]{1,0:T(8,128)S(1)} custom-call(bf16[1024,256]{1,0:T(8,128)(2,1)S(1)} %get-tuple-element.36.query_rows, bf16[1024,512]{1,0:T(8,128)(2,1)S(1)} %get-tuple-element.30.kv, f32[1024,128]{1,0:T(8,128)S(1)} %get-tuple-element.37.level, f32[2,1024]{1,0:T(2,128)S(1)} %bitcast.11, ...), custom_call_target="tpu_custom_call" | custom-call | flops 1073741824 | bytes 1048576 | tf_op jit(solution)/shard_map/pallas_call | solution.py:403
  37.6 0.0 collective-permute-done.7.below.refs_5_
  37.6 0.0 collective-permute-done.8.above.refs_4_
  37.6 0.1 shard_map.72
  37.7 0.9 %collective-permute-start.13 = (bf16[128,2048]{1,0:T(8,128)(2,1)S(1)}, bf16[128,2048]{1,0:T(8,128)(2,1)S(1)}, u32[]{:S(2)}, u32[]{:S(2)}) collective-permute-start(bf16[128,2048]{1,0:T(8,128)(2,1)S(1)} %get-tuple-element.45.after), channel_id=1, source_target_pairs={{0,6},{1,7},{2,4},{3,5},{4,2},{5,3},{6,0},{7,1},{8,14},{9,15},{10,... | collective-permute-start | bytes 1572872 | tf_op jit(solution)/shard_map/ppermute | solution.py:440
  38.5 0.0 collective-permute-start.14
  38.5 0.0 collective-permute-done.4.far
  38.5 0.0 collective-permute-done.5.skip
  38.6 0.7 %collective-permute-done.6.near = bf16[336,128]{1,0:T(8,128)(2,1)S(1)} collective-permute-done((bf16[336,128]{1,0:T(8,128)(2,1)S(1)}, bf16[336,128]{1,0:T(8,128)(2,1)S(1)}, u32[]{:S(2)}, u32[]{:S(2)}) %collective-permute-start.6) | collective-permute-done | bytes 86048 | tf_op jit(solution)/shard_map/ppermute | solution.py:435
  39.3 0.6 shard_map.73
  39.9 2.3 %collective-permute-start.10 = (bf16[448,128]{1,0:T(8,128)(2,1)S(1)}, bf16[448,128]{1,0:T(8,128)(2,1)S(1)}, u32[]{:S(2)}, u32[]{:S(2)}) collective-permute-start(bf16[448,128]{1,0:T(8,128)(2,1)S(1)} %get-tuple-element.47.after.refs_4_), channel_id=1, source_target_pairs={{0,16},{8,24},{16,0},{24,8},{32,48},{40,56},{48,32},{56,40},{64,80... | collective-permute-start | bytes 344072 | tf_op jit(solution)/shard_map/ppermute | solution.py:430
  42.2 0.7 %collective-permute-start.11 = (bf16[448,128]{1,0:T(8,128)(2,1)S(1)}, bf16[448,128]{1,0:T(8,128)(2,1)S(1)}, u32[]{:S(2)}, u32[]{:S(2)}) collective-permute-start(bf16[448,128]{1,0:T(8,128)(2,1)S(1)} %get-tuple-element.47.after.refs_4_), channel_id=1, source_target_pairs={{0,24},{8,16},{16,8},{24,0},{32,56},{40,48},{48,40},{56,32},{64,88... | collective-permute-start | bytes 344072 | tf_op jit(solution)/shard_map/ppermute | solution.py:430
  42.9 0.0 collective-permute-start.9
  42.9 2.1 %shard_map.74.refs_3_ = bf16[1024,896]{1,0:T(8,128)(2,1)S(1)} custom-call(bf16[1024,256]{1,0:T(8,128)(2,1)S(1)} %get-tuple-element.36.query_rows, f32[1024,128]{1,0:T(8,128)S(1)} %get-tuple-element.37.level, f32[2,1024]{1,0:T(2,128)S(1)} %bitcast.12, bf16[448,128]{1,0:T(8,128)(2,1)S(1)} %get-tuple-element.47.after.refs_4_), custom_call_target="tpu_custom_call" | custom-call | flops 1073741824 | bytes 1048576 | tf_op jit(solution)/shard_map/pallas_call | solution.py:403
  45.0 0.1 collective-permute-done.10.refs_6_
  45.1 2.3 %collective-permute-done.11.refs_7_ = bf16[448,128]{1,0:T(8,128)(2,1)S(1)} collective-permute-done((bf16[448,128]{1,0:T(8,128)(2,1)S(1)}, bf16[448,128]{1,0:T(8,128)(2,1)S(1)}, u32[]{:S(2)}, u32[]{:S(2)}) %collective-permute-start.11) | collective-permute-done | bytes 114720 | tf_op jit(solution)/shard_map/ppermute | solution.py:430
  47.4 0.0 collective-permute-done.9.refs_5_
  47.4 1.6 %shard_map.75 = (bf16[256,256]{1,0:T(8,128)(2,1)S(1)}, bf16[256,256]{1,0:T(8,128)(2,1)S(1)}, bf16[256,256]{1,0:T(8,128)(2,1)S(1)}, bf16[2,896,128]{2,1,0:T(8,128)(2,1)S(1)}) custom-call(s32[4]{0:T(128)S(1)} %pad_add_fusion.place, f32[8,128]{1,0:T(8,128)S(1)} %get-tuple-element.46.carry, f32[1024,128]{1,0:T(8,128)S(1)} %shard_map.69.after.refs_0_, ...), custom_call_target="tpu_custom_call" | custom-call | flops 268435456 | bytes 1048576 | tf_op jit(solution)/shard_map/pallas_call | solution.py:403
  49.0 0.0 copy-start.3
  49.0 1.6 %collective-permute-start.15 = (bf16[256,256]{1,0:T(8,128)(2,1)S(1)}, bf16[256,256]{1,0:T(8,128)(2,1)S(1)}, u32[]{:S(2)}, u32[]{:S(2)}) collective-permute-start(bf16[256,256]{1,0:T(8,128)(2,1)S(1)} %get-tuple-element.52), channel_id=1, source_target_pairs={{0,6},{1,7},{2,4},{3,5},{4,2},{5,3},{6,0},{7,1},{8,14},{9,15},{10,... | collective-permute-start | bytes 393224 | tf_op jit(solution)/shard_map/ppermute | solution.py:440
  50.6 0.6 collective-permute-start.16
  51.2 1.8 %collective-permute-start.12 = (bf16[256,256]{1,0:T(8,128)(2,1)S(1)}, bf16[256,256]{1,0:T(8,128)(2,1)S(1)}, u32[]{:S(2)}, u32[]{:S(2)}) collective-permute-start(bf16[256,256]{1,0:T(8,128)(2,1)S(1)} %get-tuple-element.48), channel_id=1, source_target_pairs={{0,4},{1,5},{2,6},{3,7},{4,0},{5,1},{6,2},{7,3},{8,12},{9,13},{10,... | collective-permute-start | bytes 393224 | tf_op jit(solution)/shard_map/ppermute | solution.py:440
  52.9 1.0 %shard_map.76.refs_0_ = bf16[256,256]{1,0:T(8,128)(2,1)S(1)} custom-call(s32[4]{0:T(128)S(1)} %pad_add_fusion.place, f32[1024,128]{1,0:T(8,128)S(1)} %shard_map.69.after.refs_0_, f32[1024,128]{1,0:T(8,128)S(1)} %shard_map.71.after.refs_1_, bf16[1024,896]{1,0:T(8,128)(2,1)S(1)} %shard_map.67.after.refs_2_, bf16[1024,896]{1,0:T(8,128)(2,1)S(1)} %shard_map.74.refs_3_, ...), custom_call_target="tpu_custom_call" | custom-call | flops 268435456 | bytes 1048576 | tf_op jit(solution)/shard_map/pallas_call | solution.py:403
  54.0 0.2 collective-permute-done.15.refs_1_
  54.1 0.3 collective-permute-done.16.refs_2_
  54.4 0.0 copy-done.3
  54.4 2.0 %shard_map.77 = (f32[128,2048]{1,0:T(8,128)S(1)}, f32[128,2048]{1,0:T(8,128)S(1)}) custom-call(s32[4]{0:T(128)S(1)} %pad_add_fusion.place, bf16[256,256]{1,0:T(8,128)(2,1)S(1)} %shard_map.76.refs_0_, bf16[256,256]{1,0:T(8,128)(2,1)S(1)} %collective-permute-done.15.refs_1_, bf16[256,256]{1,0:T(8,128)(2,1)S(1)} %collective-permute-done.16.refs_2_, ...), custom_call_target="tpu_custom_call" | custom-call | flops 2147483648 | bytes 5242880 | tf_op jit(solution)/shard_map/pallas_call | solution.py:604
  56.4 0.3 collective-permute-done.12.piece
  56.7 0.0 collective-permute-done.13.first
  56.7 0.0 collective-permute-done.14.second
  56.7 1.2 %shard_map.79 = bf16[128,2048]{1,0:T(8,128)(2,1)S(1)} custom-call(s32[4]{0:T(128)S(1)} %pad_add_fusion.place, bf16[256,256]{1,0:T(8,128)(2,1)S(1)} %collective-permute-done.12.piece, bf16[128,2048]{1,0:T(8,128)(2,1)S(1)} %collective-permute-done.13.first, bf16[128,2048]{1,0:T(8,128)(2,1)S(1)} %collective-permute-done.14.second, ...), custom_call_target="tpu_custom_call" | custom-call | flops 268435456 | bytes 3145728 | tf_op jit(solution)/shard_map/pallas_call | solution.py:616
  57.9 6.6 %collective-permute-start.17 = (bf16[128,2048]{1,0:T(8,128)(2,1)S(1)}, bf16[128,2048]{1,0:T(8,128)(2,1)S(1)}, u32[]{:S(2)}, u32[]{:S(2)}) collective-permute-start(bf16[128,2048]{1,0:T(8,128)(2,1)S(1)} %shard_map.79), channel_id=1, source_target_pairs={{0,1},{1,0},{2,3},{3,2},{4,5},{5,4},{6,7},{7,6},{8,9},{9,8},{10,11... | collective-permute-start | bytes 1572872 | tf_op jit(solution)/shard_map/ppermute | solution.py:627
  64.4 1.2 %shard_map.78 = f32[128,2048]{1,0:T(8,128)S(1)} custom-call(s32[4]{0:T(128)S(1)} %pad_add_fusion.place, bf16[256,256]{1,0:T(8,128)(2,1)S(1)} %collective-permute-done.12.piece, bf16[128,2048]{1,0:T(8,128)(2,1)S(1)} %collective-permute-done.13.first, bf16[128,2048]{1,0:T(8,128)(2,1)S(1)} %collective-permute-done.14.second, f32[128,2048]{1,0:T(8,128)S(1)} %get-tuple-element.53.near), custom_call_target="tpu_custom_call" | custom-call | flops 268435456 | bytes 3145728 | tf_op jit(solution)/shard_map/pallas_call | solution.py:616
  65.6 0.3 collective-permute-done.17
  66.0 0.9 %add_convert_fusion = bf16[128,2048]{1,0:T(8,128)(2,1)} fusion(f32[128,2048]{1,0:T(8,128)S(1)} %shard_map.78, bf16[128,2048]{1,0:T(8,128)(2,1)S(1)} %collective-permute-done.17), kind=kLoop, calls=%fused_computation | loop fusion | flops 786432 | bytes 2097152 | tf_op jit(solution)/shard_map/convert_element_type | solution.py:629
Async XLA Ops:
  0.0 37.6 %collective-permute-start.7 = (bf16[256,2048]{1,0:T(8,128)(2,1)}, bf16[256,2048]{1,0:T(8,128)(2,1)S(1)}, u32[]{:S(2)}, u32[]{:S(2)}) collective-permute-start(bf16[256,2048]{1,0:T(8,128)(2,1)} %refs_3_.1), channel_id=1, source_target_pairs={{0,2},{1,3},{2,0},{3,1},{4,6},{5,7},{6,4},{7,5},{8,10},{9,11},{10,... | collective-permute-start | bytes 3145736 | tf_op jit(solution)/shard_map/ppermute | solution.py:440
  2.1 35.4 %collective-permute-start.8 = (bf16[256,2048]{1,0:T(8,128)(2,1)}, bf16[256,2048]{1,0:T(8,128)(2,1)S(1)}, u32[]{:S(2)}, u32[]{:S(2)}) collective-permute-start(bf16[256,2048]{1,0:T(8,128)(2,1)} %refs_3_.1), channel_id=1, source_target_pairs={{0,6},{1,7},{2,4},{3,5},{4,2},{5,3},{6,0},{7,1},{8,14},{9,15},{10,... | collective-permute-start | bytes 3145736 | tf_op jit(solution)/shard_map/ppermute | solution.py:440
  4.1 6.2 %copy-start = (f32[1,4,2,128,128]{4,3,2,1,0:T(8,128)S(1)}, f32[1,4,2,128,128]{4,3,2,1,0:T(8,128)}, u32[]{:S(2)}) copy-start(f32[1,4,2,128,128]{4,3,2,1,0:T(8,128)} %param.10) | copy-start | bytes 1572868
  4.1 6.3 %copy-start.1 = (f32[1024,2]{0,1:T(2,128)S(1)}, f32[1024,2]{0,1:T(2,128)}, u32[]{:S(2)}) copy-start(f32[1024,2]{0,1:T(2,128)} %param.9) | copy-start | bytes 24580
  4.1 11.2 %copy-start.2 = (bf16[1024,2048]{1,0:T(8,128)(2,1)S(1)}, bf16[1024,2048]{1,0:T(8,128)(2,1)}, u32[]{:S(2)}) copy-start(bf16[1024,2048]{1,0:T(8,128)(2,1)} %acts.1) | copy-start | bytes 12582916
  4.1 11.2 %copy-start.4 = (bf16[2048,42]{0,1:T(8,128)(2,1)S(1)}, bf16[2048,42]{0,1:T(8,128)(2,1)}, u32[]{:S(2)}) copy-start(bf16[2048,42]{0,1:T(8,128)(2,1)} %param.8) | copy-start | bytes 516100
  11.6 8.1 %collective-permute-start = (bf16[528,128]{1,0:T(8,128)(2,1)S(1)}, bf16[528,128]{1,0:T(8,128)(2,1)S(1)}, u32[]{:S(2)}, u32[]{:S(2)}) collective-permute-start(bf16[528,128]{1,0:T(8,128)(2,1)S(1)} %get-tuple-element.32), channel_id=1, source_target_pairs={{0,16},{8,24},{16,0},{24,8},{32,48},{40,56},{48,32},{56,40},{64,80... | collective-permute-start | bytes 405512 | tf_op jit(solution)/shard_map/ppermute | solution.py:430
  14.4 5.6 %collective-permute-start.1 = (bf16[528,128]{1,0:T(8,128)(2,1)S(1)}, bf16[528,128]{1,0:T(8,128)(2,1)S(1)}, u32[]{:S(2)}, u32[]{:S(2)}) collective-permute-start(bf16[528,128]{1,0:T(8,128)(2,1)S(1)} %get-tuple-element.33), channel_id=1, source_target_pairs={{0,8},{8,0},{16,24},{24,16},{32,40},{40,32},{48,56},{56,48},{64,72... | collective-permute-start | bytes 405512 | tf_op jit(solution)/shard_map/ppermute | solution.py:430
  14.7 6.2 %collective-permute-start.2 = (bf16[528,128]{1,0:T(8,128)(2,1)S(1)}, bf16[528,128]{1,0:T(8,128)(2,1)S(1)}, u32[]{:S(2)}, u32[]{:S(2)}) collective-permute-start(bf16[528,128]{1,0:T(8,128)(2,1)S(1)} %get-tuple-element.34), channel_id=1, source_target_pairs={{0,24},{8,16},{16,8},{24,0},{32,56},{40,48},{48,40},{56,32},{64,88... | collective-permute-start | bytes 405512 | tf_op jit(solution)/shard_map/ppermute | solution.py:430
  21.7 3.9 %collective-permute-start.3 = (bf16[336,128]{1,0:T(8,128)(2,1)S(1)}, bf16[336,128]{1,0:T(8,128)(2,1)S(1)}, u32[]{:S(2)}, u32[]{:S(2)}) collective-permute-start(bf16[336,128]{1,0:T(8,128)(2,1)S(1)} %get-tuple-element.38.after.own), channel_id=1, source_target_pairs={{0,32},{8,40},{16,48},{24,56},{32,0},{40,8},{48,16},{56,24},{64,96... | collective-permute-start | bytes 258056 | tf_op jit(solution)/shard_map/ppermute | solution.py:435
  26.1 12.4 %collective-permute-start.4 = (bf16[336,128]{1,0:T(8,128)(2,1)S(1)}, bf16[336,128]{1,0:T(8,128)(2,1)S(1)}, u32[]{:S(2)}, u32[]{:S(2)}) collective-permute-start(bf16[336,128]{1,0:T(8,128)(2,1)S(1)} %get-tuple-element.42.after.own), channel_id=1, source_target_pairs={{0,160},{8,168},{16,176},{24,184},{32,128},{40,136},{48,144},{56,1... | collective-permute-start | bytes 258056 | tf_op jit(solution)/shard_map/ppermute | solution.py:435
  32.5 6.0 %collective-permute-start.5 = (bf16[336,128]{1,0:T(8,128)(2,1)S(1)}, bf16[336,128]{1,0:T(8,128)(2,1)S(1)}, u32[]{:S(2)}, u32[]{:S(2)}) collective-permute-start(bf16[336,128]{1,0:T(8,128)(2,1)S(1)} %get-tuple-element.42.after.own), channel_id=1, source_target_pairs={{0,192},{8,200},{16,208},{24,216},{32,96},{40,104},{48,112},{56,12... | collective-permute-start | bytes 258056 | tf_op jit(solution)/shard_map/ppermute | solution.py:435
  32.8 6.5 %collective-permute-start.6 = (bf16[336,128]{1,0:T(8,128)(2,1)S(1)}, bf16[336,128]{1,0:T(8,128)(2,1)S(1)}, u32[]{:S(2)}, u32[]{:S(2)}) collective-permute-start(bf16[336,128]{1,0:T(8,128)(2,1)S(1)} %get-tuple-element.42.after.own), channel_id=1, source_target_pairs={{0,224},{8,232},{16,240},{24,248},{32,64},{40,72},{48,80},{56,88},... | collective-permute-start | bytes 258056 | tf_op jit(solution)/shard_map/ppermute | solution.py:435
  37.7 19.0 %collective-permute-start.13 = (bf16[128,2048]{1,0:T(8,128)(2,1)S(1)}, bf16[128,2048]{1,0:T(8,128)(2,1)S(1)}, u32[]{:S(2)}, u32[]{:S(2)}) collective-permute-start(bf16[128,2048]{1,0:T(8,128)(2,1)S(1)} %get-tuple-element.45.after), channel_id=1, source_target_pairs={{0,6},{1,7},{2,4},{3,5},{4,2},{5,3},{6,0},{7,1},{8,14},{9,15},{10,... | collective-permute-start | bytes 1572872 | tf_op jit(solution)/shard_map/ppermute | solution.py:440
  38.5 18.2 %collective-permute-start.14 = (bf16[128,2048]{1,0:T(8,128)(2,1)S(1)}, bf16[128,2048]{1,0:T(8,128)(2,1)S(1)}, u32[]{:S(2)}, u32[]{:S(2)}) collective-permute-start(bf16[128,2048]{1,0:T(8,128)(2,1)S(1)} %get-tuple-element.49), channel_id=1, source_target_pairs={{0,2},{1,3},{2,0},{3,1},{4,6},{5,7},{6,4},{7,5},{8,10},{9,11},{10,... | collective-permute-start | bytes 1572872 | tf_op jit(solution)/shard_map/ppermute | solution.py:440
  39.9 5.2 %collective-permute-start.10 = (bf16[448,128]{1,0:T(8,128)(2,1)S(1)}, bf16[448,128]{1,0:T(8,128)(2,1)S(1)}, u32[]{:S(2)}, u32[]{:S(2)}) collective-permute-start(bf16[448,128]{1,0:T(8,128)(2,1)S(1)} %get-tuple-element.47.after.refs_4_), channel_id=1, source_target_pairs={{0,16},{8,24},{16,0},{24,8},{32,48},{40,56},{48,32},{56,40},{64,80... | collective-permute-start | bytes 344072 | tf_op jit(solution)/shard_map/ppermute | solution.py:430
  42.2 5.1 %collective-permute-start.11 = (bf16[448,128]{1,0:T(8,128)(2,1)S(1)}, bf16[448,128]{1,0:T(8,128)(2,1)S(1)}, u32[]{:S(2)}, u32[]{:S(2)}) collective-permute-start(bf16[448,128]{1,0:T(8,128)(2,1)S(1)} %get-tuple-element.47.after.refs_4_), channel_id=1, source_target_pairs={{0,24},{8,16},{16,8},{24,0},{32,56},{40,48},{48,40},{56,32},{64,88... | collective-permute-start | bytes 344072 | tf_op jit(solution)/shard_map/ppermute | solution.py:430
  42.9 4.4 %collective-permute-start.9 = (bf16[448,128]{1,0:T(8,128)(2,1)S(1)}, bf16[448,128]{1,0:T(8,128)(2,1)S(1)}, u32[]{:S(2)}, u32[]{:S(2)}) collective-permute-start(bf16[448,128]{1,0:T(8,128)(2,1)S(1)} %get-tuple-element.47.after.refs_4_), channel_id=1, source_target_pairs={{0,8},{8,0},{16,24},{24,16},{32,40},{40,32},{48,56},{56,48},{64,72... | collective-permute-start | bytes 344072 | tf_op jit(solution)/shard_map/ppermute | solution.py:430
  49.0 5.4 %copy-start.3 = (bf16[256,2048]{1,0:T(8,128)(2,1)S(1)}, bf16[256,2048]{1,0:T(8,128)(2,1)}, u32[]{:S(2)}) copy-start(bf16[256,2048]{1,0:T(8,128)(2,1)} %refs_3_.1) | copy-start | bytes 3145732
  49.0 5.1 %collective-permute-start.15 = (bf16[256,256]{1,0:T(8,128)(2,1)S(1)}, bf16[256,256]{1,0:T(8,128)(2,1)S(1)}, u32[]{:S(2)}, u32[]{:S(2)}) collective-permute-start(bf16[256,256]{1,0:T(8,128)(2,1)S(1)} %get-tuple-element.52), channel_id=1, source_target_pairs={{0,6},{1,7},{2,4},{3,5},{4,2},{5,3},{6,0},{7,1},{8,14},{9,15},{10,... | collective-permute-start | bytes 393224 | tf_op jit(solution)/shard_map/ppermute | solution.py:440
  50.6 3.8 %collective-permute-start.16 = (bf16[256,256]{1,0:T(8,128)(2,1)S(1)}, bf16[256,256]{1,0:T(8,128)(2,1)S(1)}, u32[]{:S(2)}, u32[]{:S(2)}) collective-permute-start(bf16[256,256]{1,0:T(8,128)(2,1)S(1)} %get-tuple-element.51.refs_5_), channel_id=1, source_target_pairs={{0,2},{1,3},{2,0},{3,1},{4,6},{5,7},{6,4},{7,5},{8,10},{9,11},{10,... | collective-permute-start | bytes 393224 | tf_op jit(solution)/shard_map/ppermute | solution.py:440
  51.2 5.5 %collective-permute-start.12 = (bf16[256,256]{1,0:T(8,128)(2,1)S(1)}, bf16[256,256]{1,0:T(8,128)(2,1)S(1)}, u32[]{:S(2)}, u32[]{:S(2)}) collective-permute-start(bf16[256,256]{1,0:T(8,128)(2,1)S(1)} %get-tuple-element.48), channel_id=1, source_target_pairs={{0,4},{1,5},{2,6},{3,7},{4,0},{5,1},{6,2},{7,3},{8,12},{9,13},{10,... | collective-permute-start | bytes 393224 | tf_op jit(solution)/shard_map/ppermute | solution.py:440
  57.9 8.1 %collective-permute-start.17 = (bf16[128,2048]{1,0:T(8,128)(2,1)S(1)}, bf16[128,2048]{1,0:T(8,128)(2,1)S(1)}, u32[]{:S(2)}, u32[]{:S(2)}) collective-permute-start(bf16[128,2048]{1,0:T(8,128)(2,1)S(1)} %shard_map.79), channel_id=1, source_target_pairs={{0,1},{1,0},{2,3},{3,2},{4,5},{5,4},{6,7},{7,6},{8,9},{9,8},{10,11... | collective-permute-start | bytes 1572872 | tf_op jit(solution)/shard_map/ppermute | solution.py:627

commit v3 on v2

--- a/solution.py
+++ b/solution.py
@@ -63,7 +63,7 @@
     for i in range(count):
         part = pl.ds(i * size, size)
         copies.append(pltpu.make_async_copy(source.at[part, :], target.at[part, :], sems.at[i]))
-        copies[-1].start()
+        copies[-1].start(priority=1)
     return copies
 
 

time: 66.9 us -> 66.9 us (level)
  no operation moved by 1% of the time
where the time goes in v3:
time: 66.9 us
  starting transfers between devices  33.4 us (50%)
  Pallas kernels  26.7 us (40%)
  waiting for transfers between devices  5.65 us (8%)
  other arithmetic  0.97 us (1%)
    pallas_call x13, Pallas kernels, small(): pl.pallas_call(kernel, out_shape=shapes, in_specs=specs or [SMEM if o.dty...  22.3 us
    ppermute x4, starting transfers between devices, across_z(): lax.ppermute(array, 'ctx', [(z * NX + x, target(z) % nz * NX + x) for z i...  11.2 us
    ppermute x7, starting transfers between devices, along_y(): lax.ppermute(array, 'head', [(y * 2 + c, (y ^ d) * 2 + c) for y in range(...  8.84 us
    ppermute x6, starting transfers between devices, along_x(): lax.ppermute(array, 'ctx', [(z * NX + x, z * NX + (x ^ d)) for z in range...  6.77 us
    ppermute x1, starting transfers between devices, shards(): got = lax.ppermute(send, 'head', [(i, i ^ 1) for i in range(nh)])  6.55 us
    ppermute x6, waiting for transfers between devices, along_x(): lax.ppermute(array, 'ctx', [(z * NX + x, z * NX + (x ^ d)) for z in range...  3.59 us
    pallas_call x2, Pallas kernels, add_far(): pl.pallas_call(functools.partial(far_kernel, side), grid=(width // column...  2.36 us
    pallas_call x1, Pallas kernels, shards(): pl.pallas_call(near_kernel, grid=(width // columns,), in_specs=[SMEM] + [...  1.99 us
  transfers between devices with their start and end apart: 18, of which 10 were waited for; matrix products, arithmetic and copies ran while one was open for 0% of the time, Pallas kernels for 38%

profile of v3, /device:TPU:1, one launch (start us, length us, event | category | flops | bytes accessed | tf_op | source)
XLA Modules:
  0.0 66.9 jit_solution(7297567602776764342)
XLA Ops:
  0.0 2.1 %collective-permute-start.7 = (bf16[256,2048]{1,0:T(8,128)(2,1)}, bf16[256,2048]{1,0:T(8,128)(2,1)S(1)}, u32[]{:S(2)}, u32[]{:S(2)}) collective-permute-start(bf16[256,2048]{1,0:T(8,128)(2,1)} %refs_3_.1), channel_id=1, source_target_pairs={{0,2},{1,3},{2,0},{3,1},{4,6},{5,7},{6,4},{7,5},{8,10},{9,11},{10,... | collective-permute-start | bytes 3145736 | tf_op jit(solution)/shard_map/ppermute | solution.py:440
  2.1 1.9 %collective-permute-start.8 = (bf16[256,2048]{1,0:T(8,128)(2,1)}, bf16[256,2048]{1,0:T(8,128)(2,1)S(1)}, u32[]{:S(2)}, u32[]{:S(2)}) collective-permute-start(bf16[256,2048]{1,0:T(8,128)(2,1)} %refs_3_.1), channel_id=1, source_target_pairs={{0,6},{1,7},{2,4},{3,5},{4,2},{5,3},{6,0},{7,1},{8,14},{9,15},{10,... | collective-permute-start | bytes 3145736 | tf_op jit(solution)/shard_map/ppermute | solution.py:440
  4.0 0.1 pad_add_fusion.place
  4.1 0.0 copy-start
  4.1 0.0 copy-start.1
  4.1 0.0 copy-start.2
  4.1 0.0 copy-start.4
  4.1 6.2 %shard_map.64 = (bf16[1024,512]{1,0:T(8,128)(2,1)S(1)}, bf16[2048,256]{1,0:T(8,128)(2,1)S(1)}) custom-call(bf16[1024,2048]{1,0:T(8,128)(2,1)} %acts.1, bf16[2048,768]{1,0:T(8,128)(2,1)} %weight_hbm.1), custom_call_target="tpu_custom_call" | custom-call | flops 2147483648 | bytes 1048576 | tf_op jit(solution)/shard_map/pallas_call | solution.py:403
  10.3 0.0 copy-done
  10.4 0.0 copy-done.1
  10.4 1.2 %shard_map.65 = (f32[8,2,128,128]{3,2,1,0:T(8,128)S(1)}, bf16[528,128]{1,0:T(8,128)(2,1)S(1)}, bf16[528,128]{1,0:T(8,128)(2,1)S(1)}, bf16[528,128]{1,0:T(8,128)(2,1)S(1)}, bf16[528,128]{1,0:T(8,128)(2,1)S(1)}) custom-call(s32[4]{0:T(128)S(1)} %pad_add_fusion.place, bf16[1024,512]{1,0:T(8,128)(2,1)S(1)} %get-tuple-element.30.kv, f32[2,1024]{1,0:T(2,128)S(1)} %bitcast.8, ...), custom_call_target="tpu_custom_call" | custom-call | bytes 1048576 | tf_op jit(solution)/shard_map/pallas_call | solution.py:403
  11.6 2.8 %collective-permute-start = (bf16[528,128]{1,0:T(8,128)(2,1)S(1)}, bf16[528,128]{1,0:T(8,128)(2,1)S(1)}, u32[]{:S(2)}, u32[]{:S(2)}) collective-permute-start(bf16[528,128]{1,0:T(8,128)(2,1)S(1)} %get-tuple-element.32), channel_id=1, source_target_pairs={{0,16},{8,24},{16,0},{24,8},{32,48},{40,56},{48,32},{56,40},{64,80... | collective-permute-start | bytes 405512 | tf_op jit(solution)/shard_map/ppermute | solution.py:430
  14.4 0.3 collective-permute-start.1
  14.7 0.6 collective-permute-start.2
  15.3 0.0 copy-done.2
  15.3 0.0 copy-done.4
  15.3 2.3 %shard_map.66 = (bf16[1024,256]{1,0:T(8,128)(2,1)S(1)}, f32[1024,128]{1,0:T(8,128)S(1)}) custom-call(bf16[1024,2048]{1,0:T(8,128)(2,1)S(1)} %copy-done.2, bf16[2048,256]{1,0:T(8,128)(2,1)S(1)} %get-tuple-element.35.weight, bf16[42,2048]{1,0:T(8,128)(2,1)S(1)} %bitcast.13, bf16[528,128]{1,0:T(8,128)(2,1)S(1)} %get-tuple-element.31.after.own), custom_call_target="tpu_custom_call" | custom-call | flops 2147483648 | bytes 1048576 | tf_op jit(solution)/shard_map/pallas_call | solution.py:403
  17.6 2.1 %shard_map.67.after.refs_2_ = bf16[1024,896]{1,0:T(8,128)(2,1)S(1)} custom-call(bf16[1024,256]{1,0:T(8,128)(2,1)S(1)} %get-tuple-element.36.query_rows, f32[1024,128]{1,0:T(8,128)S(1)} %get-tuple-element.37.level, f32[2,1024]{1,0:T(2,128)S(1)} %bitcast.9, bf16[528,128]{1,0:T(8,128)(2,1)S(1)} %get-tuple-element.31.after.own), custom_call_target="tpu_custom_call" | custom-call | flops 1073741824 | bytes 1048576 | tf_op jit(solution)/shard_map/pallas_call | solution.py:403
  19.7 0.0 collective-permute-done.two
  19.7 0.3 collective-permute-done.1.one
  20.0 1.0 %collective-permute-done.2.three = bf16[528,128]{1,0:T(8,128)(2,1)S(1)} collective-permute-done((bf16[528,128]{1,0:T(8,128)(2,1)S(1)}, bf16[528,128]{1,0:T(8,128)(2,1)S(1)}, u32[]{:S(2)}, u32[]{:S(2)}) %collective-permute-start.2) | collective-permute-done | bytes 135200 | tf_op jit(solution)/shard_map/ppermute | solution.py:430
  21.0 0.7 %shard_map.68 = (bf16[2,2,128,128]{3,2,1,0:T(8,128)(2,1)S(1)}, bf16[336,128]{1,0:T(8,128)(2,1)S(1)}, f32[8,128]{1,0:T(8,128)S(1)}) custom-call(s32[4]{0:T(128)S(1)} %pad_add_fusion.place, bf16[528,128]{1,0:T(8,128)(2,1)S(1)} %get-tuple-element.31.after.own, bf16[528,128]{1,0:T(8,128)(2,1)S(1)} %collective-permute-done.two, ...), custom_call_target="tpu_custom_call" | custom-call | bytes 1048576 | tf_op jit(solution)/shard_map/pallas_call | solution.py:403
  21.7 1.7 %collective-permute-start.3 = (bf16[336,128]{1,0:T(8,128)(2,1)S(1)}, bf16[336,128]{1,0:T(8,128)(2,1)S(1)}, u32[]{:S(2)}, u32[]{:S(2)}) collective-permute-start(bf16[336,128]{1,0:T(8,128)(2,1)S(1)} %get-tuple-element.38.after.own), channel_id=1, source_target_pairs={{0,32},{8,40},{16,48},{24,56},{32,0},{40,8},{48,16},{56,24},{64,96... | collective-permute-start | bytes 258056 | tf_op jit(solution)/shard_map/ppermute | solution.py:435
  23.4 1.9 %shard_map.69.after.refs_0_ = f32[1024,128]{1,0:T(8,128)S(1)} custom-call(bf16[1024,256]{1,0:T(8,128)(2,1)S(1)} %get-tuple-element.36.query_rows, bf16[1024,512]{1,0:T(8,128)(2,1)S(1)} %get-tuple-element.30.kv, f32[1024,128]{1,0:T(8,128)S(1)} %get-tuple-element.37.level, f32[2,1024]{1,0:T(2,128)S(1)} %bitcast.10, ...), custom_call_target="tpu_custom_call" | custom-call | flops 1073741824 | bytes 1048576 | tf_op jit(solution)/shard_map/pallas_call | solution.py:403
  25.3 0.3 collective-permute-done.3.got
  25.6 0.6 shard_map.70
  26.1 6.4 %collective-permute-start.4 = (bf16[336,128]{1,0:T(8,128)(2,1)S(1)}, bf16[336,128]{1,0:T(8,128)(2,1)S(1)}, u32[]{:S(2)}, u32[]{:S(2)}) collective-permute-start(bf16[336,128]{1,0:T(8,128)(2,1)S(1)} %get-tuple-element.42.after.own), channel_id=1, source_target_pairs={{0,160},{8,168},{16,176},{24,184},{32,128},{40,136},{48,144},{56,1... | collective-permute-start | bytes 258056 | tf_op jit(solution)/shard_map/ppermute | solution.py:435
  32.5 0.3 collective-permute-start.5
  32.8 2.8 %collective-permute-start.6 = (bf16[336,128]{1,0:T(8,128)(2,1)S(1)}, bf16[336,128]{1,0:T(8,128)(2,1)S(1)}, u32[]{:S(2)}, u32[]{:S(2)}) collective-permute-start(bf16[336,128]{1,0:T(8,128)(2,1)S(1)} %get-tuple-element.42.after.own), channel_id=1, source_target_pairs={{0,224},{8,232},{16,240},{24,248},{32,64},{40,72},{48,80},{56,88},... | collective-permute-start | bytes 258056 | tf_op jit(solution)/shard_map/ppermute | solution.py:435
  35.6 1.9 %shard_map.71.after.refs_1_ = f32[1024,128]{1,0:T(8,128)S(1)} custom-call(bf16[1024,256]{1,0:T(8,128)(2,1)S(1)} %get-tuple-element.36.query_rows, bf16[1024,512]{1,0:T(8,128)(2,1)S(1)} %get-tuple-element.30.kv, f32[1024,128]{1,0:T(8,128)S(1)} %get-tuple-element.37.level, f32[2,1024]{1,0:T(2,128)S(1)} %bitcast.11, ...), custom_call_target="tpu_custom_call" | custom-call | flops 1073741824 | bytes 1048576 | tf_op jit(solution)/shard_map/pallas_call | solution.py:403
  37.6 0.0 collective-permute-done.7.below.refs_5_
  37.6 0.0 collective-permute-done.8.above.refs_4_
  37.6 0.1 shard_map.72
  37.7 0.9 %collective-permute-start.13 = (bf16[128,2048]{1,0:T(8,128)(2,1)S(1)}, bf16[128,2048]{1,0:T(8,128)(2,1)S(1)}, u32[]{:S(2)}, u32[]{:S(2)}) collective-permute-start(bf16[128,2048]{1,0:T(8,128)(2,1)S(1)} %get-tuple-element.45.after), channel_id=1, source_target_pairs={{0,6},{1,7},{2,4},{3,5},{4,2},{5,3},{6,0},{7,1},{8,14},{9,15},{10,... | collective-permute-start | bytes 1572872 | tf_op jit(solution)/shard_map/ppermute | solution.py:440
  38.5 0.0 collective-permute-start.14
  38.5 0.0 collective-permute-done.4.far
  38.5 0.0 collective-permute-done.5.skip
  38.6 0.7 %collective-permute-done.6.near = bf16[336,128]{1,0:T(8,128)(2,1)S(1)} collective-permute-done((bf16[336,128]{1,0:T(8,128)(2,1)S(1)}, bf16[336,128]{1,0:T(8,128)(2,1)S(1)}, u32[]{:S(2)}, u32[]{:S(2)}) %collective-permute-start.6) | collective-permute-done | bytes 86048 | tf_op jit(solution)/shard_map/ppermute | solution.py:435
  39.3 0.6 shard_map.73
  39.9 2.3 %collective-permute-start.10 = (bf16[448,128]{1,0:T(8,128)(2,1)S(1)}, bf16[448,128]{1,0:T(8,128)(2,1)S(1)}, u32[]{:S(2)}, u32[]{:S(2)}) collective-permute-start(bf16[448,128]{1,0:T(8,128)(2,1)S(1)} %get-tuple-element.47.after.refs_4_), channel_id=1, source_target_pairs={{0,16},{8,24},{16,0},{24,8},{32,48},{40,56},{48,32},{56,40},{64,80... | collective-permute-start | bytes 344072 | tf_op jit(solution)/shard_map/ppermute | solution.py:430
  42.2 0.7 %collective-permute-start.11 = (bf16[448,128]{1,0:T(8,128)(2,1)S(1)}, bf16[448,128]{1,0:T(8,128)(2,1)S(1)}, u32[]{:S(2)}, u32[]{:S(2)}) collective-permute-start(bf16[448,128]{1,0:T(8,128)(2,1)S(1)} %get-tuple-element.47.after.refs_4_), channel_id=1, source_target_pairs={{0,24},{8,16},{16,8},{24,0},{32,56},{40,48},{48,40},{56,32},{64,88... | collective-permute-start | bytes 344072 | tf_op jit(solution)/shard_map/ppermute | solution.py:430
  42.9 0.0 collective-permute-start.9
  42.9 2.1 %shard_map.74.refs_3_ = bf16[1024,896]{1,0:T(8,128)(2,1)S(1)} custom-call(bf16[1024,256]{1,0:T(8,128)(2,1)S(1)} %get-tuple-element.36.query_rows, f32[1024,128]{1,0:T(8,128)S(1)} %get-tuple-element.37.level, f32[2,1024]{1,0:T(2,128)S(1)} %bitcast.12, bf16[448,128]{1,0:T(8,128)(2,1)S(1)} %get-tuple-element.47.after.refs_4_), custom_call_target="tpu_custom_call" | custom-call | flops 1073741824 | bytes 1048576 | tf_op jit(solution)/shard_map/pallas_call | solution.py:403
  45.0 0.1 collective-permute-done.10.refs_6_
  45.1 2.3 %collective-permute-done.11.refs_7_ = bf16[448,128]{1,0:T(8,128)(2,1)S(1)} collective-permute-done((bf16[448,128]{1,0:T(8,128)(2,1)S(1)}, bf16[448,128]{1,0:T(8,128)(2,1)S(1)}, u32[]{:S(2)}, u32[]{:S(2)}) %collective-permute-start.11) | collective-permute-done | bytes 114720 | tf_op jit(solution)/shard_map/ppermute | solution.py:430
  47.4 0.0 collective-permute-done.9.refs_5_
  47.4 1.6 %shard_map.75 = (bf16[256,256]{1,0:T(8,128)(2,1)S(1)}, bf16[256,256]{1,0:T(8,128)(2,1)S(1)}, bf16[256,256]{1,0:T(8,128)(2,1)S(1)}, bf16[2,896,128]{2,1,0:T(8,128)(2,1)S(1)}) custom-call(s32[4]{0:T(128)S(1)} %pad_add_fusion.place, f32[8,128]{1,0:T(8,128)S(1)} %get-tuple-element.46.carry, f32[1024,128]{1,0:T(8,128)S(1)} %shard_map.69.after.refs_0_, ...), custom_call_target="tpu_custom_call" | custom-call | flops 268435456 | bytes 1048576 | tf_op jit(solution)/shard_map/pallas_call | solution.py:403
  49.0 0.0 copy-start.3
  49.0 1.6 %collective-permute-start.15 = (bf16[256,256]{1,0:T(8,128)(2,1)S(1)}, bf16[256,256]{1,0:T(8,128)(2,1)S(1)}, u32[]{:S(2)}, u32[]{:S(2)}) collective-permute-start(bf16[256,256]{1,0:T(8,128)(2,1)S(1)} %get-tuple-element.52), channel_id=1, source_target_pairs={{0,6},{1,7},{2,4},{3,5},{4,2},{5,3},{6,0},{7,1},{8,14},{9,15},{10,... | collective-permute-start | bytes 393224 | tf_op jit(solution)/shard_map/ppermute | solution.py:440
  50.6 0.6 collective-permute-start.16
  51.2 1.8 %collective-permute-start.12 = (bf16[256,256]{1,0:T(8,128)(2,1)S(1)}, bf16[256,256]{1,0:T(8,128)(2,1)S(1)}, u32[]{:S(2)}, u32[]{:S(2)}) collective-permute-start(bf16[256,256]{1,0:T(8,128)(2,1)S(1)} %get-tuple-element.48), channel_id=1, source_target_pairs={{0,4},{1,5},{2,6},{3,7},{4,0},{5,1},{6,2},{7,3},{8,12},{9,13},{10,... | collective-permute-start | bytes 393224 | tf_op jit(solution)/shard_map/ppermute | solution.py:440
  52.9 1.0 %shard_map.76.refs_0_ = bf16[256,256]{1,0:T(8,128)(2,1)S(1)} custom-call(s32[4]{0:T(128)S(1)} %pad_add_fusion.place, f32[1024,128]{1,0:T(8,128)S(1)} %shard_map.69.after.refs_0_, f32[1024,128]{1,0:T(8,128)S(1)} %shard_map.71.after.refs_1_, bf16[1024,896]{1,0:T(8,128)(2,1)S(1)} %shard_map.67.after.refs_2_, bf16[1024,896]{1,0:T(8,128)(2,1)S(1)} %shard_map.74.refs_3_, ...), custom_call_target="tpu_custom_call" | custom-call | flops 268435456 | bytes 1048576 | tf_op jit(solution)/shard_map/pallas_call | solution.py:403
  54.0 0.2 collective-permute-done.15.refs_1_
  54.1 0.3 collective-permute-done.16.refs_2_
  54.4 0.0 copy-done.3
  54.4 2.0 %shard_map.77 = (f32[128,2048]{1,0:T(8,128)S(1)}, f32[128,2048]{1,0:T(8,128)S(1)}) custom-call(s32[4]{0:T(128)S(1)} %pad_add_fusion.place, bf16[256,256]{1,0:T(8,128)(2,1)S(1)} %shard_map.76.refs_0_, bf16[256,256]{1,0:T(8,128)(2,1)S(1)} %collective-permute-done.15.refs_1_, bf16[256,256]{1,0:T(8,128)(2,1)S(1)} %collective-permute-done.16.refs_2_, ...), custom_call_target="tpu_custom_call" | custom-call | flops 2147483648 | bytes 5242880 | tf_op jit(solution)/shard_map/pallas_call | solution.py:604
  56.4 0.3 collective-permute-done.12.piece
  56.7 0.0 collective-permute-done.13.first
  56.7 0.0 collective-permute-done.14.second
  56.7 1.2 %shard_map.79 = bf16[128,2048]{1,0:T(8,128)(2,1)S(1)} custom-call(s32[4]{0:T(128)S(1)} %pad_add_fusion.place, bf16[256,256]{1,0:T(8,128)(2,1)S(1)} %collective-permute-done.12.piece, bf16[128,2048]{1,0:T(8,128)(2,1)S(1)} %collective-permute-done.13.first, bf16[128,2048]{1,0:T(8,128)(2,1)S(1)} %collective-permute-done.14.second, ...), custom_call_target="tpu_custom_call" | custom-call | flops 268435456 | bytes 3145728 | tf_op jit(solution)/shard_map/pallas_call | solution.py:616
  57.9 6.6 %collective-permute-start.17 = (bf16[128,2048]{1,0:T(8,128)(2,1)S(1)}, bf16[128,2048]{1,0:T(8,128)(2,1)S(1)}, u32[]{:S(2)}, u32[]{:S(2)}) collective-permute-start(bf16[128,2048]{1,0:T(8,128)(2,1)S(1)} %shard_map.79), channel_id=1, source_target_pairs={{0,1},{1,0},{2,3},{3,2},{4,5},{5,4},{6,7},{7,6},{8,9},{9,8},{10,11... | collective-permute-start | bytes 1572872 | tf_op jit(solution)/shard_map/ppermute | solution.py:627
  64.4 1.2 %shard_map.78 = f32[128,2048]{1,0:T(8,128)S(1)} custom-call(s32[4]{0:T(128)S(1)} %pad_add_fusion.place, bf16[256,256]{1,0:T(8,128)(2,1)S(1)} %collective-permute-done.12.piece, bf16[128,2048]{1,0:T(8,128)(2,1)S(1)} %collective-permute-done.13.first, bf16[128,2048]{1,0:T(8,128)(2,1)S(1)} %collective-permute-done.14.second, f32[128,2048]{1,0:T(8,128)S(1)} %get-tuple-element.53.near), custom_call_target="tpu_custom_call" | custom-call | flops 268435456 | bytes 3145728 | tf_op jit(solution)/shard_map/pallas_call | solution.py:616
  65.6 0.3 collective-permute-done.17
  66.0 0.9 %add_convert_fusion = bf16[128,2048]{1,0:T(8,128)(2,1)} fusion(f32[128,2048]{1,0:T(8,128)S(1)} %shard_map.78, bf16[128,2048]{1,0:T(8,128)(2,1)S(1)} %collective-permute-done.17), kind=kLoop, calls=%fused_computation | loop fusion | flops 786432 | bytes 2097152 | tf_op jit(solution)/shard_map/convert_element_type | solution.py:629
Async XLA Ops:
  0.0 37.6 %collective-permute-start.7 = (bf16[256,2048]{1,0:T(8,128)(2,1)}, bf16[256,2048]{1,0:T(8,128)(2,1)S(1)}, u32[]{:S(2)}, u32[]{:S(2)}) collective-permute-start(bf16[256,2048]{1,0:T(8,128)(2,1)} %refs_3_.1), channel_id=1, source_target_pairs={{0,2},{1,3},{2,0},{3,1},{4,6},{5,7},{6,4},{7,5},{8,10},{9,11},{10,... | collective-permute-start | bytes 3145736 | tf_op jit(solution)/shard_map/ppermute | solution.py:440
  2.1 35.4 %collective-permute-start.8 = (bf16[256,2048]{1,0:T(8,128)(2,1)}, bf16[256,2048]{1,0:T(8,128)(2,1)S(1)}, u32[]{:S(2)}, u32[]{:S(2)}) collective-permute-start(bf16[256,2048]{1,0:T(8,128)(2,1)} %refs_3_.1), channel_id=1, source_target_pairs={{0,6},{1,7},{2,4},{3,5},{4,2},{5,3},{6,0},{7,1},{8,14},{9,15},{10,... | collective-permute-start | bytes 3145736 | tf_op jit(solution)/shard_map/ppermute | solution.py:440
  4.1 6.2 %copy-start = (f32[1,4,2,128,128]{4,3,2,1,0:T(8,128)S(1)}, f32[1,4,2,128,128]{4,3,2,1,0:T(8,128)}, u32[]{:S(2)}) copy-start(f32[1,4,2,128,128]{4,3,2,1,0:T(8,128)} %param.10) | copy-start | bytes 1572868
  4.1 6.3 %copy-start.1 = (f32[1024,2]{0,1:T(2,128)S(1)}, f32[1024,2]{0,1:T(2,128)}, u32[]{:S(2)}) copy-start(f32[1024,2]{0,1:T(2,128)} %param.9) | copy-start | bytes 24580
  4.1 11.2 %copy-start.2 = (bf16[1024,2048]{1,0:T(8,128)(2,1)S(1)}, bf16[1024,2048]{1,0:T(8,128)(2,1)}, u32[]{:S(2)}) copy-start(bf16[1024,2048]{1,0:T(8,128)(2,1)} %acts.1) | copy-start | bytes 12582916
  4.1 11.2 %copy-start.4 = (bf16[2048,42]{0,1:T(8,128)(2,1)S(1)}, bf16[2048,42]{0,1:T(8,128)(2,1)}, u32[]{:S(2)}) copy-start(bf16[2048,42]{0,1:T(8,128)(2,1)} %param.8) | copy-start | bytes 516100
  11.6 8.1 %collective-permute-start = (bf16[528,128]{1,0:T(8,128)(2,1)S(1)}, bf16[528,128]{1,0:T(8,128)(2,1)S(1)}, u32[]{:S(2)}, u32[]{:S(2)}) collective-permute-start(bf16[528,128]{1,0:T(8,128)(2,1)S(1)} %get-tuple-element.32), channel_id=1, source_target_pairs={{0,16},{8,24},{16,0},{24,8},{32,48},{40,56},{48,32},{56,40},{64,80... | collective-permute-start | bytes 405512 | tf_op jit(solution)/shard_map/ppermute | solution.py:430
  14.4 5.6 %collective-permute-start.1 = (bf16[528,128]{1,0:T(8,128)(2,1)S(1)}, bf16[528,128]{1,0:T(8,128)(2,1)S(1)}, u32[]{:S(2)}, u32[]{:S(2)}) collective-permute-start(bf16[528,128]{1,0:T(8,128)(2,1)S(1)} %get-tuple-element.33), channel_id=1, source_target_pairs={{0,8},{8,0},{16,24},{24,16},{32,40},{40,32},{48,56},{56,48},{64,72... | collective-permute-start | bytes 405512 | tf_op jit(solution)/shard_map/ppermute | solution.py:430
  14.7 6.2 %collective-permute-start.2 = (bf16[528,128]{1,0:T(8,128)(2,1)S(1)}, bf16[528,128]{1,0:T(8,128)(2,1)S(1)}, u32[]{:S(2)}, u32[]{:S(2)}) collective-permute-start(bf16[528,128]{1,0:T(8,128)(2,1)S(1)} %get-tuple-element.34), channel_id=1, source_target_pairs={{0,24},{8,16},{16,8},{24,0},{32,56},{40,48},{48,40},{56,32},{64,88... | collective-permute-start | bytes 405512 | tf_op jit(solution)/shard_map/ppermute | solution.py:430
  21.7 3.9 %collective-permute-start.3 = (bf16[336,128]{1,0:T(8,128)(2,1)S(1)}, bf16[336,128]{1,0:T(8,128)(2,1)S(1)}, u32[]{:S(2)}, u32[]{:S(2)}) collective-permute-start(bf16[336,128]{1,0:T(8,128)(2,1)S(1)} %get-tuple-element.38.after.own), channel_id=1, source_target_pairs={{0,32},{8,40},{16,48},{24,56},{32,0},{40,8},{48,16},{56,24},{64,96... | collective-permute-start | bytes 258056 | tf_op jit(solution)/shard_map/ppermute | solution.py:435
  26.1 12.4 %collective-permute-start.4 = (bf16[336,128]{1,0:T(8,128)(2,1)S(1)}, bf16[336,128]{1,0:T(8,128)(2,1)S(1)}, u32[]{:S(2)}, u32[]{:S(2)}) collective-permute-start(bf16[336,128]{1,0:T(8,128)(2,1)S(1)} %get-tuple-element.42.after.own), channel_id=1, source_target_pairs={{0,160},{8,168},{16,176},{24,184},{32,128},{40,136},{48,144},{56,1... | collective-permute-start | bytes 258056 | tf_op jit(solution)/shard_map/ppermute | solution.py:435
  32.5 6.0 %collective-permute-start.5 = (bf16[336,128]{1,0:T(8,128)(2,1)S(1)}, bf16[336,128]{1,0:T(8,128)(2,1)S(1)}, u32[]{:S(2)}, u32[]{:S(2)}) collective-permute-start(bf16[336,128]{1,0:T(8,128)(2,1)S(1)} %get-tuple-element.42.after.own), channel_id=1, source_target_pairs={{0,192},{8,200},{16,208},{24,216},{32,96},{40,104},{48,112},{56,12... | collective-permute-start | bytes 258056 | tf_op jit(solution)/shard_map/ppermute | solution.py:435
  32.8 6.5 %collective-permute-start.6 = (bf16[336,128]{1,0:T(8,128)(2,1)S(1)}, bf16[336,128]{1,0:T(8,128)(2,1)S(1)}, u32[]{:S(2)}, u32[]{:S(2)}) collective-permute-start(bf16[336,128]{1,0:T(8,128)(2,1)S(1)} %get-tuple-element.42.after.own), channel_id=1, source_target_pairs={{0,224},{8,232},{16,240},{24,248},{32,64},{40,72},{48,80},{56,88},... | collective-permute-start | bytes 258056 | tf_op jit(solution)/shard_map/ppermute | solution.py:435
  37.7 19.0 %collective-permute-start.13 = (bf16[128,2048]{1,0:T(8,128)(2,1)S(1)}, bf16[128,2048]{1,0:T(8,128)(2,1)S(1)}, u32[]{:S(2)}, u32[]{:S(2)}) collective-permute-start(bf16[128,2048]{1,0:T(8,128)(2,1)S(1)} %get-tuple-element.45.after), channel_id=1, source_target_pairs={{0,6},{1,7},{2,4},{3,5},{4,2},{5,3},{6,0},{7,1},{8,14},{9,15},{10,... | collective-permute-start | bytes 1572872 | tf_op jit(solution)/shard_map/ppermute | solution.py:440
  38.5 18.2 %collective-permute-start.14 = (bf16[128,2048]{1,0:T(8,128)(2,1)S(1)}, bf16[128,2048]{1,0:T(8,128)(2,1)S(1)}, u32[]{:S(2)}, u32[]{:S(2)}) collective-permute-start(bf16[128,2048]{1,0:T(8,128)(2,1)S(1)} %get-tuple-element.49), channel_id=1, source_target_pairs={{0,2},{1,3},{2,0},{3,1},{4,6},{5,7},{6,4},{7,5},{8,10},{9,11},{10,... | collective-permute-start | bytes 1572872 | tf_op jit(solution)/shard_map/ppermute | solution.py:440
  39.9 5.2 %collective-permute-start.10 = (bf16[448,128]{1,0:T(8,128)(2,1)S(1)}, bf16[448,128]{1,0:T(8,128)(2,1)S(1)}, u32[]{:S(2)}, u32[]{:S(2)}) collective-permute-start(bf16[448,128]{1,0:T(8,128)(2,1)S(1)} %get-tuple-element.47.after.refs_4_), channel_id=1, source_target_pairs={{0,16},{8,24},{16,0},{24,8},{32,48},{40,56},{48,32},{56,40},{64,80... | collective-permute-start | bytes 344072 | tf_op jit(solution)/shard_map/ppermute | solution.py:430
  42.2 5.1 %collective-permute-start.11 = (bf16[448,128]{1,0:T(8,128)(2,1)S(1)}, bf16[448,128]{1,0:T(8,128)(2,1)S(1)}, u32[]{:S(2)}, u32[]{:S(2)}) collective-permute-start(bf16[448,128]{1,0:T(8,128)(2,1)S(1)} %get-tuple-element.47.after.refs_4_), channel_id=1, source_target_pairs={{0,24},{8,16},{16,8},{24,0},{32,56},{40,48},{48,40},{56,32},{64,88... | collective-permute-start | bytes 344072 | tf_op jit(solution)/shard_map/ppermute | solution.py:430
  42.9 4.4 %collective-permute-start.9 = (bf16[448,128]{1,0:T(8,128)(2,1)S(1)}, bf16[448,128]{1,0:T(8,128)(2,1)S(1)}, u32[]{:S(2)}, u32[]{:S(2)}) collective-permute-start(bf16[448,128]{1,0:T(8,128)(2,1)S(1)} %get-tuple-element.47.after.refs_4_), channel_id=1, source_target_pairs={{0,8},{8,0},{16,24},{24,16},{32,40},{40,32},{48,56},{56,48},{64,72... | collective-permute-start | bytes 344072 | tf_op jit(solution)/shard_map/ppermute | solution.py:430
  49.0 5.4 %copy-start.3 = (bf16[256,2048]{1,0:T(8,128)(2,1)S(1)}, bf16[256,2048]{1,0:T(8,128)(2,1)}, u32[]{:S(2)}) copy-start(bf16[256,2048]{1,0:T(8,128)(2,1)} %refs_3_.1) | copy-start | bytes 3145732
  49.0 5.1 %collective-permute-start.15 = (bf16[256,256]{1,0:T(8,128)(2,1)S(1)}, bf16[256,256]{1,0:T(8,128)(2,1)S(1)}, u32[]{:S(2)}, u32[]{:S(2)}) collective-permute-start(bf16[256,256]{1,0:T(8,128)(2,1)S(1)} %get-tuple-element.52), channel_id=1, source_target_pairs={{0,6},{1,7},{2,4},{3,5},{4,2},{5,3},{6,0},{7,1},{8,14},{9,15},{10,... | collective-permute-start | bytes 393224 | tf_op jit(solution)/shard_map/ppermute | solution.py:440
  50.6 3.8 %collective-permute-start.16 = (bf16[256,256]{1,0:T(8,128)(2,1)S(1)}, bf16[256,256]{1,0:T(8,128)(2,1)S(1)}, u32[]{:S(2)}, u32[]{:S(2)}) collective-permute-start(bf16[256,256]{1,0:T(8,128)(2,1)S(1)} %get-tuple-element.51.refs_5_), channel_id=1, source_target_pairs={{0,2},{1,3},{2,0},{3,1},{4,6},{5,7},{6,4},{7,5},{8,10},{9,11},{10,... | collective-permute-start | bytes 393224 | tf_op jit(solution)/shard_map/ppermute | solution.py:440
  51.2 5.5 %collective-permute-start.12 = (bf16[256,256]{1,0:T(8,128)(2,1)S(1)}, bf16[256,256]{1,0:T(8,128)(2,1)S(1)}, u32[]{:S(2)}, u32[]{:S(2)}) collective-permute-start(bf16[256,256]{1,0:T(8,128)(2,1)S(1)} %get-tuple-element.48), channel_id=1, source_target_pairs={{0,4},{1,5},{2,6},{3,7},{4,0},{5,1},{6,2},{7,3},{8,12},{9,13},{10,... | collective-permute-start | bytes 393224 | tf_op jit(solution)/shard_map/ppermute | solution.py:440
  57.9 8.1 %collective-permute-start.17 = (bf16[128,2048]{1,0:T(8,128)(2,1)S(1)}, bf16[128,2048]{1,0:T(8,128)(2,1)S(1)}, u32[]{:S(2)}, u32[]{:S(2)}) collective-permute-start(bf16[128,2048]{1,0:T(8,128)(2,1)S(1)} %shard_map.79), channel_id=1, source_target_pairs={{0,1},{1,0},{2,3},{3,2},{4,5},{5,4},{6,7},{7,6},{8,9},{9,8},{10,11... | collective-permute-start | bytes 1572872 | tf_op jit(solution)/shard_map/ppermute | solution.py:627

commit v4 on v2

--- a/solution.py
+++ b/solution.py
@@ -467,6 +467,7 @@
         kv,
         gate,
         prior_parts[0],
+        flops=1 << 32,
     )
     pieces = [payloads[0]] + [along_x(payloads[d], d) for d in range(1, NX)]
 

time: 66.9 us -> 70 us (1.046)
  local copies, waits for them, and re-layouts: 0.02 us -> 3.18 us
    unnamed x10 -> x20, local copies, waits for them, and re-layouts: 0.02 us -> 3.18 us
  transfers between devices with their start and end apart: 18 -> 18, of which waited for: 10 -> 10; matrix products, arithmetic and copies ran while one was open for 0% -> 0% of each run, Pallas kernels for 38% -> 36%
where the time goes in v4:
time: 70 us; the launch traced here: 69.9 us
  starting transfers between devices  33.4 us (48%)
  Pallas kernels  26.5 us (38%)
  waiting for transfers between devices  5.6 us (8%)
  local copies, waits for them, and re-layouts  3.18 us (5%)
  other arithmetic  0.97 us (1%)
    pallas_call x13, Pallas kernels, small(): pl.pallas_call(kernel, out_shape=shapes, in_specs=specs or [SMEM if o.dty...  22.2 us
    ppermute x4, starting transfers between devices, across_z(): lax.ppermute(array, 'ctx', [(z * NX + x, target(z) % nz * NX + x) for z i...  11.2 us
    ppermute x7, starting transfers between devices, along_y(): lax.ppermute(array, 'head', [(y * 2 + c, (y ^ d) * 2 + c) for y in range(...  8.84 us
    ppermute x6, starting transfers between devices, along_x(): lax.ppermute(array, 'ctx', [(z * NX + x, z * NX + (x ^ d)) for z in range...  6.77 us
    ppermute x1, starting transfers between devices, shards(): got = lax.ppermute(send, 'head', [(i, i ^ 1) for i in range(nh)])  6.55 us
    ppermute x6, waiting for transfers between devices, along_x(): lax.ppermute(array, 'ctx', [(z * NX + x, z * NX + (x ^ d)) for z in range...  3.54 us
    unnamed x20, local copies, waits for them, and re-layouts  3.18 us
    pallas_call x2, Pallas kernels, add_far(): pl.pallas_call(functools.partial(far_kernel, side), grid=(width // column...  2.36 us
  transfers between devices with their start and end apart: 18, of which 10 were waited for; matrix products, arithmetic and copies ran while one was open for 0% of the time, Pallas kernels for 36%

profile of v4, /device:TPU:1, one launch (start us, length us, event | category | flops | bytes accessed | tf_op | source)
XLA Modules:
  0.0 69.9 jit_solution(9052762784042535375)
XLA Ops:
  0.0 2.1 %collective-permute-start.7 = (bf16[256,2048]{1,0:T(8,128)(2,1)}, bf16[256,2048]{1,0:T(8,128)(2,1)S(1)}, u32[]{:S(2)}, u32[]{:S(2)}) collective-permute-start(bf16[256,2048]{1,0:T(8,128)(2,1)} %refs_3_.1), channel_id=1, source_target_pairs={{0,2},{1,3},{2,0},{3,1},{4,6},{5,7},{6,4},{7,5},{8,10},{9,11},{10,... | collective-permute-start | bytes 3145736 | tf_op jit(solution)/shard_map/ppermute | solution.py:440
  2.1 1.9 %collective-permute-start.8 = (bf16[256,2048]{1,0:T(8,128)(2,1)}, bf16[256,2048]{1,0:T(8,128)(2,1)S(1)}, u32[]{:S(2)}, u32[]{:S(2)}) collective-permute-start(bf16[256,2048]{1,0:T(8,128)(2,1)} %refs_3_.1), channel_id=1, source_target_pairs={{0,6},{1,7},{2,4},{3,5},{4,2},{5,3},{6,0},{7,1},{8,14},{9,15},{10,... | collective-permute-start | bytes 3145736 | tf_op jit(solution)/shard_map/ppermute | solution.py:440
  4.0 6.1 %shard_map.64 = (bf16[1024,512]{1,0:T(8,128)(2,1)S(1)}, bf16[2048,256]{1,0:T(8,128)(2,1)S(1)}) custom-call(bf16[1024,2048]{1,0:T(8,128)(2,1)} %acts.1, bf16[2048,768]{1,0:T(8,128)(2,1)} %weight_hbm.1), custom_call_target="tpu_custom_call" | custom-call | flops 2147483648 | bytes 1048576 | tf_op jit(solution)/shard_map/pallas_call | solution.py:403
  10.1 0.0 copy-start.5
  10.1 1.0 %copy-done.5 = bf16[1024,512]{1,0:T(8,128)(2,1)} copy-done((bf16[1024,512]{1,0:T(8,128)(2,1)}, bf16[1024,512]{1,0:T(8,128)(2,1)S(1)}, u32[]{:S(2)}) %copy-start.5) | copy-done | bytes 1048600
  11.1 1.0 %copy-done.8 = bf16[2048,256]{1,0:T(8,128)(2,1)} copy-done((bf16[2048,256]{1,0:T(8,128)(2,1)}, bf16[2048,256]{1,0:T(8,128)(2,1)S(1)}, u32[]{:S(2)}) %copy-start.8) | copy-done | bytes 1048600
  12.0 0.1 pad_add_fusion.place
  12.1 0.0 copy-done.4
  12.1 0.0 copy-done.2
  12.1 1.2 %copy-done.6 = bf16[1024,512]{1,0:T(8,128)(2,1)S(1)} copy-done((bf16[1024,512]{1,0:T(8,128)(2,1)S(1)}, bf16[1024,512]{1,0:T(8,128)(2,1)}, u32[]{:S(2)}) %copy-start.6) | copy-done | bytes 1048600
  13.4 1.2 %shard_map.65 = (f32[8,2,128,128]{3,2,1,0:T(8,128)S(1)}, bf16[528,128]{1,0:T(8,128)(2,1)S(1)}, bf16[528,128]{1,0:T(8,128)(2,1)S(1)}, bf16[528,128]{1,0:T(8,128)(2,1)S(1)}, bf16[528,128]{1,0:T(8,128)(2,1)S(1)}) custom-call(s32[4]{0:T(128)S(1)} %pad_add_fusion.place, bf16[1024,512]{1,0:T(8,128)(2,1)S(1)} %copy-done.6, f32[2,1024]{1,0:T(2,128)S(1)} %bitcast.9, ...), custom_call_target="tpu_custom_call" | custom-call | flops 4294967296 | bytes 1048576 | tf_op jit(solution)/shard_map/pallas_call | solution.py:403
  14.6 2.8 %collective-permute-start = (bf16[528,128]{1,0:T(8,128)(2,1)S(1)}, bf16[528,128]{1,0:T(8,128)(2,1)S(1)}, u32[]{:S(2)}, u32[]{:S(2)}) collective-permute-start(bf16[528,128]{1,0:T(8,128)(2,1)S(1)} %get-tuple-element.32), channel_id=1, source_target_pairs={{0,16},{8,24},{16,0},{24,8},{32,48},{40,56},{48,32},{56,40},{64,80... | collective-permute-start | bytes 405512 | tf_op jit(solution)/shard_map/ppermute | solution.py:430
  17.4 0.3 collective-permute-start.1
  17.7 0.5 collective-permute-start.2
  18.3 0.0 copy-done
  18.3 0.0 copy-done.9
  18.3 2.4 %shard_map.66 = (bf16[1024,256]{1,0:T(8,128)(2,1)S(1)}, f32[1024,128]{1,0:T(8,128)S(1)}) custom-call(bf16[1024,2048]{1,0:T(8,128)(2,1)S(1)} %copy-done, bf16[2048,256]{1,0:T(8,128)(2,1)S(1)} %copy-done.9, bf16[42,2048]{1,0:T(8,128)(2,1)S(1)} %bitcast.8, bf16[528,128]{1,0:T(8,128)(2,1)S(1)} %get-tuple-element.31.after.own), custom_call_target="tpu_custom_call" | custom-call | flops 2147483648 | bytes 1048576 | tf_op jit(solution)/shard_map/pallas_call | solution.py:403
  20.7 0.0 copy-start.7
  20.7 2.1 %shard_map.67.after.refs_2_ = bf16[1024,896]{1,0:T(8,128)(2,1)S(1)} custom-call(bf16[1024,256]{1,0:T(8,128)(2,1)S(1)} %get-tuple-element.36.query_rows, f32[1024,128]{1,0:T(8,128)S(1)} %get-tuple-element.37.level, f32[2,1024]{1,0:T(2,128)S(1)} %bitcast.10, bf16[528,128]{1,0:T(8,128)(2,1)S(1)} %get-tuple-element.31.after.own), custom_call_target="tpu_custom_call" | custom-call | flops 1073741824 | bytes 1048576 | tf_op jit(solution)/shard_map/pallas_call | solution.py:403
  22.8 0.0 collective-permute-done.two
  22.8 0.2 collective-permute-done.1.one
  23.0 0.9 %collective-permute-done.2.three = bf16[528,128]{1,0:T(8,128)(2,1)S(1)} collective-permute-done((bf16[528,128]{1,0:T(8,128)(2,1)S(1)}, bf16[528,128]{1,0:T(8,128)(2,1)S(1)}, u32[]{:S(2)}, u32[]{:S(2)}) %collective-permute-start.2) | collective-permute-done | bytes 135200 | tf_op jit(solution)/shard_map/ppermute | solution.py:430
  24.0 0.7 %shard_map.68 = (bf16[2,2,128,128]{3,2,1,0:T(8,128)(2,1)S(1)}, bf16[336,128]{1,0:T(8,128)(2,1)S(1)}, f32[8,128]{1,0:T(8,128)S(1)}) custom-call(s32[4]{0:T(128)S(1)} %pad_add_fusion.place, bf16[528,128]{1,0:T(8,128)(2,1)S(1)} %get-tuple-element.31.after.own, bf16[528,128]{1,0:T(8,128)(2,1)S(1)} %collective-permute-done.two, ...), custom_call_target="tpu_custom_call" | custom-call | bytes 1048576 | tf_op jit(solution)/shard_map/pallas_call | solution.py:403
  24.7 1.7 %collective-permute-start.3 = (bf16[336,128]{1,0:T(8,128)(2,1)S(1)}, bf16[336,128]{1,0:T(8,128)(2,1)S(1)}, u32[]{:S(2)}, u32[]{:S(2)}) collective-permute-start(bf16[336,128]{1,0:T(8,128)(2,1)S(1)} %get-tuple-element.38.after.own), channel_id=1, source_target_pairs={{0,32},{8,40},{16,48},{24,56},{32,0},{40,8},{48,16},{56,24},{64,96... | collective-permute-start | bytes 258056 | tf_op jit(solution)/shard_map/ppermute | solution.py:435
  26.4 1.9 %shard_map.69.after.refs_0_ = f32[1024,128]{1,0:T(8,128)S(1)} custom-call(bf16[1024,256]{1,0:T(8,128)(2,1)S(1)} %get-tuple-element.36.query_rows, bf16[1024,512]{1,0:T(8,128)(2,1)S(1)} %copy-done.7, f32[1024,128]{1,0:T(8,128)S(1)} %get-tuple-element.37.level, f32[2,1024]{1,0:T(2,128)S(1)} %bitcast.11, f32[8,2,128,128]{3,2,1,0:T(8,128)S(1)} %get-tuple-element.40.chunk_states, ...), custom_call_target="tpu_custom_call" | custom-call | flops 1073741824 | bytes 1048576 | tf_op jit(solution)/shard_map/pallas_call | solution.py:403
  28.3 0.3 collective-permute-done.3.got
  28.6 0.6 shard_map.70
  29.1 6.4 %collective-permute-start.4 = (bf16[336,128]{1,0:T(8,128)(2,1)S(1)}, bf16[336,128]{1,0:T(8,128)(2,1)S(1)}, u32[]{:S(2)}, u32[]{:S(2)}) collective-permute-start(bf16[336,128]{1,0:T(8,128)(2,1)S(1)} %get-tuple-element.42.after.own), channel_id=1, source_target_pairs={{0,160},{8,168},{16,176},{24,184},{32,128},{40,136},{48,144},{56,1... | collective-permute-start | bytes 258056 | tf_op jit(solution)/shard_map/ppermute | solution.py:435
  35.5 0.3 collective-permute-start.5
  35.8 2.9 %collective-permute-start.6 = (bf16[336,128]{1,0:T(8,128)(2,1)S(1)}, bf16[336,128]{1,0:T(8,128)(2,1)S(1)}, u32[]{:S(2)}, u32[]{:S(2)}) collective-permute-start(bf16[336,128]{1,0:T(8,128)(2,1)S(1)} %get-tuple-element.42.after.own), channel_id=1, source_target_pairs={{0,224},{8,232},{16,240},{24,248},{32,64},{40,72},{48,80},{56,88},... | collective-permute-start | bytes 258056 | tf_op jit(solution)/shard_map/ppermute | solution.py:435
  38.6 1.9 %shard_map.71.after.refs_1_ = f32[1024,128]{1,0:T(8,128)S(1)} custom-call(bf16[1024,256]{1,0:T(8,128)(2,1)S(1)} %get-tuple-element.36.query_rows, bf16[1024,512]{1,0:T(8,128)(2,1)S(1)} %copy-done.7, f32[1024,128]{1,0:T(8,128)S(1)} %get-tuple-element.37.level, f32[2,1024]{1,0:T(2,128)S(1)} %bitcast.12, f32[8,2,128,128]{3,2,1,0:T(8,128)S(1)} %get-tuple-element.40.chunk_states, ...), custom_call_target="tpu_custom_call" | custom-call | flops 1073741824 | bytes 1048576 | tf_op jit(solution)/shard_map/pallas_call | solution.py:403
  40.5 0.0 collective-permute-done.7.below.refs_5_
  40.6 0.0 collective-permute-done.8.above.refs_4_
  40.6 0.1 shard_map.72
  40.7 0.9 %collective-permute-start.13 = (bf16[128,2048]{1,0:T(8,128)(2,1)S(1)}, bf16[128,2048]{1,0:T(8,128)(2,1)S(1)}, u32[]{:S(2)}, u32[]{:S(2)}) collective-permute-start(bf16[128,2048]{1,0:T(8,128)(2,1)S(1)} %get-tuple-element.45.after), channel_id=1, source_target_pairs={{0,6},{1,7},{2,4},{3,5},{4,2},{5,3},{6,0},{7,1},{8,14},{9,15},{10,... | collective-permute-start | bytes 1572872 | tf_op jit(solution)/shard_map/ppermute | solution.py:440
  41.5 0.0 collective-permute-start.14
  41.5 0.0 collective-permute-done.4.far
  41.5 0.0 collective-permute-done.5.skip
  41.5 0.7 %collective-permute-done.6.near = bf16[336,128]{1,0:T(8,128)(2,1)S(1)} collective-permute-done((bf16[336,128]{1,0:T(8,128)(2,1)S(1)}, bf16[336,128]{1,0:T(8,128)(2,1)S(1)}, u32[]{:S(2)}, u32[]{:S(2)}) %collective-permute-start.6) | collective-permute-done | bytes 86048 | tf_op jit(solution)/shard_map/ppermute | solution.py:435
  42.3 0.6 shard_map.73
  42.9 2.4 %collective-permute-start.10 = (bf16[448,128]{1,0:T(8,128)(2,1)S(1)}, bf16[448,128]{1,0:T(8,128)(2,1)S(1)}, u32[]{:S(2)}, u32[]{:S(2)}) collective-permute-start(bf16[448,128]{1,0:T(8,128)(2,1)S(1)} %get-tuple-element.47.after.refs_4_), channel_id=1, source_target_pairs={{0,16},{8,24},{16,0},{24,8},{32,48},{40,56},{48,32},{56,40},{64,80... | collective-permute-start | bytes 344072 | tf_op jit(solution)/shard_map/ppermute | solution.py:430
  45.2 0.7 %collective-permute-start.11 = (bf16[448,128]{1,0:T(8,128)(2,1)S(1)}, bf16[448,128]{1,0:T(8,128)(2,1)S(1)}, u32[]{:S(2)}, u32[]{:S(2)}) collective-permute-start(bf16[448,128]{1,0:T(8,128)(2,1)S(1)} %get-tuple-element.47.after.refs_4_), channel_id=1, source_target_pairs={{0,24},{8,16},{16,8},{24,0},{32,56},{40,48},{48,40},{56,32},{64,88... | collective-permute-start | bytes 344072 | tf_op jit(solution)/shard_map/ppermute | solution.py:430
  45.9 0.0 collective-permute-start.9
  45.9 2.1 %shard_map.74.refs_3_ = bf16[1024,896]{1,0:T(8,128)(2,1)S(1)} custom-call(bf16[1024,256]{1,0:T(8,128)(2,1)S(1)} %get-tuple-element.36.query_rows, f32[1024,128]{1,0:T(8,128)S(1)} %get-tuple-element.37.level, f32[2,1024]{1,0:T(2,128)S(1)} %bitcast.13, bf16[448,128]{1,0:T(8,128)(2,1)S(1)} %get-tuple-element.47.after.refs_4_), custom_call_target="tpu_custom_call" | custom-call | flops 1073741824 | bytes 1048576 | tf_op jit(solution)/shard_map/pallas_call | solution.py:403
  48.0 0.1 collective-permute-done.10.refs_6_
  48.1 2.3 %collective-permute-done.11.refs_7_ = bf16[448,128]{1,0:T(8,128)(2,1)S(1)} collective-permute-done((bf16[448,128]{1,0:T(8,128)(2,1)S(1)}, bf16[448,128]{1,0:T(8,128)(2,1)S(1)}, u32[]{:S(2)}, u32[]{:S(2)}) %collective-permute-start.11) | collective-permute-done | bytes 114720 | tf_op jit(solution)/shard_map/ppermute | solution.py:430
  50.4 0.0 collective-permute-done.9.refs_5_
  50.4 1.6 %shard_map.75 = (bf16[256,256]{1,0:T(8,128)(2,1)S(1)}, bf16[256,256]{1,0:T(8,128)(2,1)S(1)}, bf16[256,256]{1,0:T(8,128)(2,1)S(1)}, bf16[2,896,128]{2,1,0:T(8,128)(2,1)S(1)}) custom-call(s32[4]{0:T(128)S(1)} %pad_add_fusion.place, f32[8,128]{1,0:T(8,128)S(1)} %get-tuple-element.46.carry, f32[1024,128]{1,0:T(8,128)S(1)} %shard_map.69.after.refs_0_, ...), custom_call_target="tpu_custom_call" | custom-call | flops 268435456 | bytes 1048576 | tf_op jit(solution)/shard_map/pallas_call | solution.py:403
  52.0 0.0 copy-start.1
  52.0 1.6 %collective-permute-start.15 = (bf16[256,256]{1,0:T(8,128)(2,1)S(1)}, bf16[256,256]{1,0:T(8,128)(2,1)S(1)}, u32[]{:S(2)}, u32[]{:S(2)}) collective-permute-start(bf16[256,256]{1,0:T(8,128)(2,1)S(1)} %get-tuple-element.52), channel_id=1, source_target_pairs={{0,6},{1,7},{2,4},{3,5},{4,2},{5,3},{6,0},{7,1},{8,14},{9,15},{10,... | collective-permute-start | bytes 393224 | tf_op jit(solution)/shard_map/ppermute | solution.py:440
  53.6 0.6 collective-permute-start.16
  54.1 1.8 %collective-permute-start.12 = (bf16[256,256]{1,0:T(8,128)(2,1)S(1)}, bf16[256,256]{1,0:T(8,128)(2,1)S(1)}, u32[]{:S(2)}, u32[]{:S(2)}) collective-permute-start(bf16[256,256]{1,0:T(8,128)(2,1)S(1)} %get-tuple-element.48), channel_id=1, source_target_pairs={{0,4},{1,5},{2,6},{3,7},{4,0},{5,1},{6,2},{7,3},{8,12},{9,13},{10,... | collective-permute-start | bytes 393224 | tf_op jit(solution)/shard_map/ppermute | solution.py:440
  55.9 1.0 %shard_map.76.refs_0_ = bf16[256,256]{1,0:T(8,128)(2,1)S(1)} custom-call(s32[4]{0:T(128)S(1)} %pad_add_fusion.place, f32[1024,128]{1,0:T(8,128)S(1)} %shard_map.69.after.refs_0_, f32[1024,128]{1,0:T(8,128)S(1)} %shard_map.71.after.refs_1_, bf16[1024,896]{1,0:T(8,128)(2,1)S(1)} %shard_map.67.after.refs_2_, bf16[1024,896]{1,0:T(8,128)(2,1)S(1)} %shard_map.74.refs_3_, ...), custom_call_target="tpu_custom_call" | custom-call | flops 268435456 | bytes 1048576 | tf_op jit(solution)/shard_map/pallas_call | solution.py:403
  57.0 0.1 collective-permute-done.15.refs_1_
  57.1 0.3 collective-permute-done.16.refs_2_
  57.4 2.0 %shard_map.77 = (f32[128,2048]{1,0:T(8,128)S(1)}, f32[128,2048]{1,0:T(8,128)S(1)}) custom-call(s32[4]{0:T(128)S(1)} %pad_add_fusion.place, bf16[256,256]{1,0:T(8,128)(2,1)S(1)} %shard_map.76.refs_0_, bf16[256,256]{1,0:T(8,128)(2,1)S(1)} %collective-permute-done.15.refs_1_, bf16[256,256]{1,0:T(8,128)(2,1)S(1)} %collective-permute-done.16.refs_2_, ...), custom_call_target="tpu_custom_call" | custom-call | flops 2147483648 | bytes 5242880 | tf_op jit(solution)/shard_map/pallas_call | solution.py:605
  59.4 0.3 collective-permute-done.12.piece
  59.7 0.0 collective-permute-done.13.first
  59.7 0.0 collective-permute-done.14.second
  59.7 1.2 %shard_map.79 = bf16[128,2048]{1,0:T(8,128)(2,1)S(1)} custom-call(s32[4]{0:T(128)S(1)} %pad_add_fusion.place, bf16[256,256]{1,0:T(8,128)(2,1)S(1)} %collective-permute-done.12.piece, bf16[128,2048]{1,0:T(8,128)(2,1)S(1)} %collective-permute-done.13.first, bf16[128,2048]{1,0:T(8,128)(2,1)S(1)} %collective-permute-done.14.second, ...), custom_call_target="tpu_custom_call" | custom-call | flops 268435456 | bytes 3145728 | tf_op jit(solution)/shard_map/pallas_call | solution.py:617
  60.9 6.5 %collective-permute-start.17 = (bf16[128,2048]{1,0:T(8,128)(2,1)S(1)}, bf16[128,2048]{1,0:T(8,128)(2,1)S(1)}, u32[]{:S(2)}, u32[]{:S(2)}) collective-permute-start(bf16[128,2048]{1,0:T(8,128)(2,1)S(1)} %shard_map.79), channel_id=1, source_target_pairs={{0,1},{1,0},{2,3},{3,2},{4,5},{5,4},{6,7},{7,6},{8,9},{9,8},{10,11... | collective-permute-start | bytes 1572872 | tf_op jit(solution)/shard_map/ppermute | solution.py:628
  67.4 1.2 %shard_map.78 = f32[128,2048]{1,0:T(8,128)S(1)} custom-call(s32[4]{0:T(128)S(1)} %pad_add_fusion.place, bf16[256,256]{1,0:T(8,128)(2,1)S(1)} %collective-permute-done.12.piece, bf16[128,2048]{1,0:T(8,128)(2,1)S(1)} %collective-permute-done.13.first, bf16[128,2048]{1,0:T(8,128)(2,1)S(1)} %collective-permute-done.14.second, f32[128,2048]{1,0:T(8,128)S(1)} %get-tuple-element.53.near), custom_call_target="tpu_custom_call" | custom-call | flops 268435456 | bytes 3145728 | tf_op jit(solution)/shard_map/pallas_call | solution.py:617
  68.6 0.3 collective-permute-done.17
  69.0 0.9 %add_convert_fusion = bf16[128,2048]{1,0:T(8,128)(2,1)} fusion(f32[128,2048]{1,0:T(8,128)S(1)} %shard_map.78, bf16[128,2048]{1,0:T(8,128)(2,1)S(1)} %collective-permute-done.17), kind=kLoop, calls=%fused_computation | loop fusion | flops 786432 | bytes 2097152 | tf_op jit(solution)/shard_map/convert_element_type | solution.py:630
  (10 shorter events, 0.0 us)
Async XLA Ops:
  0.0 12.1 %copy-start.4 = (f32[1024,2]{0,1:T(2,128)S(1)}, f32[1024,2]{0,1:T(2,128)}, u32[]{:S(2)}) copy-start(f32[1024,2]{0,1:T(2,128)} %param.9) | copy-start | bytes 24580
  0.0 12.1 %copy-start.2 = (f32[1,4,2,128,128]{4,3,2,1,0:T(8,128)S(1)}, f32[1,4,2,128,128]{4,3,2,1,0:T(8,128)}, u32[]{:S(2)}) copy-start(f32[1,4,2,128,128]{4,3,2,1,0:T(8,128)} %param.10) | copy-start | bytes 1572868
  0.0 40.5 %collective-permute-start.7 = (bf16[256,2048]{1,0:T(8,128)(2,1)}, bf16[256,2048]{1,0:T(8,128)(2,1)S(1)}, u32[]{:S(2)}, u32[]{:S(2)}) collective-permute-start(bf16[256,2048]{1,0:T(8,128)(2,1)} %refs_3_.1), channel_id=1, source_target_pairs={{0,2},{1,3},{2,0},{3,1},{4,6},{5,7},{6,4},{7,5},{8,10},{9,11},{10,... | collective-permute-start | bytes 3145736 | tf_op jit(solution)/shard_map/ppermute | solution.py:440
  2.1 38.4 %collective-permute-start.8 = (bf16[256,2048]{1,0:T(8,128)(2,1)}, bf16[256,2048]{1,0:T(8,128)(2,1)S(1)}, u32[]{:S(2)}, u32[]{:S(2)}) collective-permute-start(bf16[256,2048]{1,0:T(8,128)(2,1)} %refs_3_.1), channel_id=1, source_target_pairs={{0,6},{1,7},{2,4},{3,5},{4,2},{5,3},{6,0},{7,1},{8,14},{9,15},{10,... | collective-permute-start | bytes 3145736 | tf_op jit(solution)/shard_map/ppermute | solution.py:440
  10.1 1.0 %copy-start.5 = (bf16[1024,512]{1,0:T(8,128)(2,1)}, bf16[1024,512]{1,0:T(8,128)(2,1)S(1)}, u32[]{:S(2)}) copy-start(bf16[1024,512]{1,0:T(8,128)(2,1)S(1)} %get-tuple-element.30.kv) | copy-start | bytes 3145732
  11.1 1.0 %copy-start.8 = (bf16[2048,256]{1,0:T(8,128)(2,1)}, bf16[2048,256]{1,0:T(8,128)(2,1)S(1)}, u32[]{:S(2)}) copy-start(bf16[2048,256]{1,0:T(8,128)(2,1)S(1)} %get-tuple-element.35.weight) | copy-start | bytes 3145732
  12.1 1.2 %copy-start.6 = (bf16[1024,512]{1,0:T(8,128)(2,1)S(1)}, bf16[1024,512]{1,0:T(8,128)(2,1)}, u32[]{:S(2)}) copy-start(bf16[1024,512]{1,0:T(8,128)(2,1)} %copy-done.5) | copy-start | bytes 3145732
  13.4 4.9 %copy-start = (bf16[1024,2048]{1,0:T(8,128)(2,1)S(1)}, bf16[1024,2048]{1,0:T(8,128)(2,1)}, u32[]{:S(2)}) copy-start(bf16[1024,2048]{1,0:T(8,128)(2,1)} %acts.1) | copy-start | bytes 12582916
  13.4 4.9 %copy-start.3 = (bf16[2048,42]{0,1:T(8,128)(2,1)S(1)}, bf16[2048,42]{0,1:T(8,128)(2,1)}, u32[]{:S(2)}) copy-start(bf16[2048,42]{0,1:T(8,128)(2,1)} %param.8) | copy-start | bytes 516100
  13.4 4.9 %copy-start.9 = (bf16[2048,256]{1,0:T(8,128)(2,1)S(1)}, bf16[2048,256]{1,0:T(8,128)(2,1)}, u32[]{:S(2)}) copy-start(bf16[2048,256]{1,0:T(8,128)(2,1)} %copy-done.8) | copy-start | bytes 3145732
  14.6 8.2 %collective-permute-start = (bf16[528,128]{1,0:T(8,128)(2,1)S(1)}, bf16[528,128]{1,0:T(8,128)(2,1)S(1)}, u32[]{:S(2)}, u32[]{:S(2)}) collective-permute-start(bf16[528,128]{1,0:T(8,128)(2,1)S(1)} %get-tuple-element.32), channel_id=1, source_target_pairs={{0,16},{8,24},{16,0},{24,8},{32,48},{40,56},{48,32},{56,40},{64,80... | collective-permute-start | bytes 405512 | tf_op jit(solution)/shard_map/ppermute | solution.py:430
  17.4 5.6 %collective-permute-start.1 = (bf16[528,128]{1,0:T(8,128)(2,1)S(1)}, bf16[528,128]{1,0:T(8,128)(2,1)S(1)}, u32[]{:S(2)}, u32[]{:S(2)}) collective-permute-start(bf16[528,128]{1,0:T(8,128)(2,1)S(1)} %get-tuple-element.33), channel_id=1, source_target_pairs={{0,8},{8,0},{16,24},{24,16},{32,40},{40,32},{48,56},{56,48},{64,72... | collective-permute-start | bytes 405512 | tf_op jit(solution)/shard_map/ppermute | solution.py:430
  17.7 6.2 %collective-permute-start.2 = (bf16[528,128]{1,0:T(8,128)(2,1)S(1)}, bf16[528,128]{1,0:T(8,128)(2,1)S(1)}, u32[]{:S(2)}, u32[]{:S(2)}) collective-permute-start(bf16[528,128]{1,0:T(8,128)(2,1)S(1)} %get-tuple-element.34), channel_id=1, source_target_pairs={{0,24},{8,16},{16,8},{24,0},{32,56},{40,48},{48,40},{56,32},{64,88... | collective-permute-start | bytes 405512 | tf_op jit(solution)/shard_map/ppermute | solution.py:430
  20.7 5.7 %copy-start.7 = (bf16[1024,512]{1,0:T(8,128)(2,1)S(1)}, bf16[1024,512]{1,0:T(8,128)(2,1)}, u32[]{:S(2)}) copy-start(bf16[1024,512]{1,0:T(8,128)(2,1)} %copy-done.5) | copy-start | bytes 3145732
  24.7 3.9 %collective-permute-start.3 = (bf16[336,128]{1,0:T(8,128)(2,1)S(1)}, bf16[336,128]{1,0:T(8,128)(2,1)S(1)}, u32[]{:S(2)}, u32[]{:S(2)}) collective-permute-start(bf16[336,128]{1,0:T(8,128)(2,1)S(1)} %get-tuple-element.38.after.own), channel_id=1, source_target_pairs={{0,32},{8,40},{16,48},{24,56},{32,0},{40,8},{48,16},{56,24},{64,96... | collective-permute-start | bytes 258056 | tf_op jit(solution)/shard_map/ppermute | solution.py:435
  29.1 12.4 %collective-permute-start.4 = (bf16[336,128]{1,0:T(8,128)(2,1)S(1)}, bf16[336,128]{1,0:T(8,128)(2,1)S(1)}, u32[]{:S(2)}, u32[]{:S(2)}) collective-permute-start(bf16[336,128]{1,0:T(8,128)(2,1)S(1)} %get-tuple-element.42.after.own), channel_id=1, source_target_pairs={{0,160},{8,168},{16,176},{24,184},{32,128},{40,136},{48,144},{56,1... | collective-permute-start | bytes 258056 | tf_op jit(solution)/shard_map/ppermute | solution.py:435
  35.5 6.0 %collective-permute-start.5 = (bf16[336,128]{1,0:T(8,128)(2,1)S(1)}, bf16[336,128]{1,0:T(8,128)(2,1)S(1)}, u32[]{:S(2)}, u32[]{:S(2)}) collective-permute-start(bf16[336,128]{1,0:T(8,128)(2,1)S(1)} %get-tuple-element.42.after.own), channel_id=1, source_target_pairs={{0,192},{8,200},{16,208},{24,216},{32,96},{40,104},{48,112},{56,12... | collective-permute-start | bytes 258056 | tf_op jit(solution)/shard_map/ppermute | solution.py:435
  35.8 6.5 %collective-permute-start.6 = (bf16[336,128]{1,0:T(8,128)(2,1)S(1)}, bf16[336,128]{1,0:T(8,128)(2,1)S(1)}, u32[]{:S(2)}, u32[]{:S(2)}) collective-permute-start(bf16[336,128]{1,0:T(8,128)(2,1)S(1)} %get-tuple-element.42.after.own), channel_id=1, source_target_pairs={{0,224},{8,232},{16,240},{24,248},{32,64},{40,72},{48,80},{56,88},... | collective-permute-start | bytes 258056 | tf_op jit(solution)/shard_map/ppermute | solution.py:435
  40.7 19.0 %collective-permute-start.13 = (bf16[128,2048]{1,0:T(8,128)(2,1)S(1)}, bf16[128,2048]{1,0:T(8,128)(2,1)S(1)}, u32[]{:S(2)}, u32[]{:S(2)}) collective-permute-start(bf16[128,2048]{1,0:T(8,128)(2,1)S(1)} %get-tuple-element.45.after), channel_id=1, source_target_pairs={{0,6},{1,7},{2,4},{3,5},{4,2},{5,3},{6,0},{7,1},{8,14},{9,15},{10,... | collective-permute-start | bytes 1572872 | tf_op jit(solution)/shard_map/ppermute | solution.py:440
  41.5 18.2 %collective-permute-start.14 = (bf16[128,2048]{1,0:T(8,128)(2,1)S(1)}, bf16[128,2048]{1,0:T(8,128)(2,1)S(1)}, u32[]{:S(2)}, u32[]{:S(2)}) collective-permute-start(bf16[128,2048]{1,0:T(8,128)(2,1)S(1)} %get-tuple-element.49), channel_id=1, source_target_pairs={{0,2},{1,3},{2,0},{3,1},{4,6},{5,7},{6,4},{7,5},{8,10},{9,11},{10,... | collective-permute-start | bytes 1572872 | tf_op jit(solution)/shard_map/ppermute | solution.py:440
  42.9 5.2 %collective-permute-start.10 = (bf16[448,128]{1,0:T(8,128)(2,1)S(1)}, bf16[448,128]{1,0:T(8,128)(2,1)S(1)}, u32[]{:S(2)}, u32[]{:S(2)}) collective-permute-start(bf16[448,128]{1,0:T(8,128)(2,1)S(1)} %get-tuple-element.47.after.refs_4_), channel_id=1, source_target_pairs={{0,16},{8,24},{16,0},{24,8},{32,48},{40,56},{48,32},{56,40},{64,80... | collective-permute-start | bytes 344072 | tf_op jit(solution)/shard_map/ppermute | solution.py:430
  45.2 5.1 %collective-permute-start.11 = (bf16[448,128]{1,0:T(8,128)(2,1)S(1)}, bf16[448,128]{1,0:T(8,128)(2,1)S(1)}, u32[]{:S(2)}, u32[]{:S(2)}) collective-permute-start(bf16[448,128]{1,0:T(8,128)(2,1)S(1)} %get-tuple-element.47.after.refs_4_), channel_id=1, source_target_pairs={{0,24},{8,16},{16,8},{24,0},{32,56},{40,48},{48,40},{56,32},{64,88... | collective-permute-start | bytes 344072 | tf_op jit(solution)/shard_map/ppermute | solution.py:430
  45.9 4.4 %collective-permute-start.9 = (bf16[448,128]{1,0:T(8,128)(2,1)S(1)}, bf16[448,128]{1,0:T(8,128)(2,1)S(1)}, u32[]{:S(2)}, u32[]{:S(2)}) collective-permute-start(bf16[448,128]{1,0:T(8,128)(2,1)S(1)} %get-tuple-element.47.after.refs_4_), channel_id=1, source_target_pairs={{0,8},{8,0},{16,24},{24,16},{32,40},{40,32},{48,56},{56,48},{64,72... | collective-permute-start | bytes 344072 | tf_op jit(solution)/shard_map/ppermute | solution.py:430
  52.0 5.4 %copy-start.1 = (bf16[256,2048]{1,0:T(8,128)(2,1)S(1)}, bf16[256,2048]{1,0:T(8,128)(2,1)}, u32[]{:S(2)}) copy-start(bf16[256,2048]{1,0:T(8,128)(2,1)} %refs_3_.1) | copy-start | bytes 3145732
  52.0 5.1 %collective-permute-start.15 = (bf16[256,256]{1,0:T(8,128)(2,1)S(1)}, bf16[256,256]{1,0:T(8,128)(2,1)S(1)}, u32[]{:S(2)}, u32[]{:S(2)}) collective-permute-start(bf16[256,256]{1,0:T(8,128)(2,1)S(1)} %get-tuple-element.52), channel_id=1, source_target_pairs={{0,6},{1,7},{2,4},{3,5},{4,2},{5,3},{6,0},{7,1},{8,14},{9,15},{10,... | collective-permute-start | bytes 393224 | tf_op jit(solution)/shard_map/ppermute | solution.py:440
  53.6 3.8 %collective-permute-start.16 = (bf16[256,256]{1,0:T(8,128)(2,1)S(1)}, bf16[256,256]{1,0:T(8,128)(2,1)S(1)}, u32[]{:S(2)}, u32[]{:S(2)}) collective-permute-start(bf16[256,256]{1,0:T(8,128)(2,1)S(1)} %get-tuple-element.51.refs_5_), channel_id=1, source_target_pairs={{0,2},{1,3},{2,0},{3,1},{4,6},{5,7},{6,4},{7,5},{8,10},{9,11},{10,... | collective-permute-start | bytes 393224 | tf_op jit(solution)/shard_map/ppermute | solution.py:440
  54.1 5.5 %collective-permute-start.12 = (bf16[256,256]{1,0:T(8,128)(2,1)S(1)}, bf16[256,256]{1,0:T(8,128)(2,1)S(1)}, u32[]{:S(2)}, u32[]{:S(2)}) collective-permute-start(bf16[256,256]{1,0:T(8,128)(2,1)S(1)} %get-tuple-element.48), channel_id=1, source_target_pairs={{0,4},{1,5},{2,6},{3,7},{4,0},{5,1},{6,2},{7,3},{8,12},{9,13},{10,... | collective-permute-start | bytes 393224 | tf_op jit(solution)/shard_map/ppermute | solution.py:440
  60.9 8.1 %collective-permute-start.17 = (bf16[128,2048]{1,0:T(8,128)(2,1)S(1)}, bf16[128,2048]{1,0:T(8,128)(2,1)S(1)}, u32[]{:S(2)}, u32[]{:S(2)}) collective-permute-start(bf16[128,2048]{1,0:T(8,128)(2,1)S(1)} %shard_map.79), channel_id=1, source_target_pairs={{0,1},{1,0},{2,3},{3,2},{4,5},{5,4},{6,7},{7,6},{8,9},{9,8},{10,11... | collective-permute-start | bytes 1572872 | tf_op jit(solution)/shard_map/ppermute | solution.py:628

commit v5 on v3

--- a/solution.py
+++ b/solution.py
@@ -63,7 +63,6 @@
     for i in range(count):
         part = pl.ds(i * size, size)
         copies.append(pltpu.make_async_copy(source.at[part, :], target.at[part, :], sems.at[i]))
-        copies[-1].start(priority=1)
     return copies
 
 
@@ -72,8 +71,13 @@
     heads = query_weight.shape[1] // DH
     weight_copies = copy_parts(weight_hbm, weight, weight_sem)
     acts_copies = copy_parts(acts_hbm, acts, acts_sem)
+    half = len(acts_copies) // 2
+    for copy in weight_copies + acts_copies[:half]:
+        copy.start()
     for copy in weight_copies:
         copy.wait()
+    for copy in acts_copies[half:]:
+        copy.start()
     per_tile = len(acts_copies) * TILE // block
     for i in range(block // TILE):
         for copy in acts_copies[i * per_tile : (i + 1) * per_tile]:
@@ -395,6 +399,15 @@
     out[...] = total.astype(out.dtype)
 
 
+def last_kernel(keep, *refs):
+    swapped, out = refs[:-1], refs[-1]
+    for i, got in enumerate(swapped):
+
+        @pl.when(pl.program_id(0) == i)
+        def _(got=got):
+            out[...] = (keep[...] + got[...].astype(F32)).astype(BF16)
+
+
 ANY = pl.BlockSpec(memory_space=pl.ANY)
 HBM = pl.BlockSpec(memory_space=pltpu.HBM)
 
@@ -612,21 +625,32 @@
         cost_estimate=pl.CostEstimate(flops=8 << 28, bytes_accessed=5 << 20, transcendentals=0),
     )(place, normed[0], normed[3], normed[1], out_weight, above, below)
 
-    def add_far(side, near, dtype):
+    def add_far(side, near, dtype, first, count):
+        shift = lambda block: pl.BlockSpec(block.block_shape, lambda i: (0, first + i))
         return pl.pallas_call(
             functools.partial(far_kernel, side),
-            grid=(width // columns,),
-            in_specs=[SMEM, fixed, half_block, half_block, out_block],
+            grid=(count,),
+            in_specs=[SMEM, fixed, shift(half_block), shift(half_block), shift(out_block)],
             out_specs=out_block,
-            out_shape=shape((CHUNK, width), dtype),
+            out_shape=shape((CHUNK, count * columns), dtype),
             compiler_params=params(24),
             cost_estimate=pl.CostEstimate(flops=1 << 28, bytes_accessed=3 << 20, transcendentals=0),
         )(place, normed[2], *far_weight, near)
 
-    send = add_far(1, theirs, BF16)
-    got = lax.ppermute(send, "head", [(i, i ^ 1) for i in range(nh)])
-    keep = add_far(0, mine, F32)
-    return (keep + got.astype(F32)).astype(BF16)
+    count = width // columns
+    swapped = [
+        lax.ppermute(add_far(1, theirs, BF16, i, 1), "head", [(i, i ^ 1) for i in range(nh)])
+        for i in range(count)
+    ]
+    keep = add_far(0, mine, F32, 0, count)
+    return pl.pallas_call(
+        last_kernel,
+        grid=(count,),
+        in_specs=[out_block] + [pl.BlockSpec((CHUNK, columns), lambda i: (0, 0))] * count,
+        out_specs=out_block,
+        out_shape=shape((CHUNK, width), BF16),
+        compiler_params=params(24),
+    )(keep, *swapped)
 
 
 def solution(mesh):

time: 66.9 us -> 67.3 us (level)
  Pallas kernels: 26.7 us -> 27.8 us
  other arithmetic: 0.97 us -> 0.08 us
    pallas_call x2 -> x4, Pallas kernels: 2.36 us -> 3.68 us  [the longest x3 2.75 us: add_far(): pl.pallas_call(functools.partial(far_kernel, side), grid=(count,), in_spe...]
    convert_element_type x1 -> x0, other arithmetic: 0.9 us -> none  [shards(): return (keep + got.astype(F32)).astype(BF16)]
    ppermute x1 -> x2, starting transfers between devices: 6.55 us -> 6.65 us  [shards(): lax.ppermute(add_far(1, theirs, BF16, i, 1), 'head', [(i, i ^ 1) for i in...]
  transfers between devices with their start and end apart: 18 -> 19, of which waited for: 10 -> 10; matrix products, arithmetic and copies ran while one was open for 0% -> 0% of each run, Pallas kernels for 38% -> 39%
where the time goes in v5:
time: 67.3 us; the launch traced here: 67.2 us
  starting transfers between devices  33.5 us (50%)
  Pallas kernels  27.8 us (41%)
  waiting for transfers between devices  5.62 us (8%)
    pallas_call x13, Pallas kernels, small(): pl.pallas_call(kernel, out_shape=shapes, in_specs=specs or [SMEM if o.dty...  22.1 us
    ppermute x4, starting transfers between devices, across_z(): lax.ppermute(array, 'ctx', [(z * NX + x, target(z) % nz * NX + x) for z i...  11.2 us
    ppermute x7, starting transfers between devices, along_y(): lax.ppermute(array, 'head', [(y * 2 + c, (y ^ d) * 2 + c) for y in range(...  8.84 us
    ppermute x6, starting transfers between devices, along_x(): lax.ppermute(array, 'ctx', [(z * NX + x, z * NX + (x ^ d)) for z in range...  6.77 us
    ppermute x2, starting transfers between devices, shards(): lax.ppermute(add_far(1, theirs, BF16, i, 1), 'head', [(i, i ^ 1) for i in...  6.65 us
    ppermute x6, waiting for transfers between devices, along_x(): lax.ppermute(array, 'ctx', [(z * NX + x, z * NX + (x ^ d)) for z in range...  3.6 us
    pallas_call x3, Pallas kernels, add_far(): pl.pallas_call(functools.partial(far_kernel, side), grid=(count,), in_spe...  2.75 us
    pallas_call x1, Pallas kernels, shards(): pl.pallas_call(near_kernel, grid=(width // columns,), in_specs=[SMEM] + [...  1.99 us
  transfers between devices with their start and end apart: 19, of which 10 were waited for; matrix products, arithmetic and copies ran while one was open for 0% of the time, Pallas kernels for 39%

profile of v5, /device:TPU:1, one launch (start us, length us, event | category | flops | bytes accessed | tf_op | source)
XLA Modules:
  0.0 67.2 jit_solution(3335679192544599432)
XLA Ops:
  0.0 2.1 %collective-permute-start.7 = (bf16[256,2048]{1,0:T(8,128)(2,1)}, bf16[256,2048]{1,0:T(8,128)(2,1)S(1)}, u32[]{:S(2)}, u32[]{:S(2)}) collective-permute-start(bf16[256,2048]{1,0:T(8,128)(2,1)} %refs_3_.1), channel_id=1, source_target_pairs={{0,2},{1,3},{2,0},{3,1},{4,6},{5,7},{6,4},{7,5},{8,10},{9,11},{10,... | collective-permute-start | bytes 3145736 | tf_op jit(solution)/shard_map/ppermute | solution.py:453
  2.1 1.9 %collective-permute-start.8 = (bf16[256,2048]{1,0:T(8,128)(2,1)}, bf16[256,2048]{1,0:T(8,128)(2,1)S(1)}, u32[]{:S(2)}, u32[]{:S(2)}) collective-permute-start(bf16[256,2048]{1,0:T(8,128)(2,1)} %refs_3_.1), channel_id=1, source_target_pairs={{0,6},{1,7},{2,4},{3,5},{4,2},{5,3},{6,0},{7,1},{8,14},{9,15},{10,... | collective-permute-start | bytes 3145736 | tf_op jit(solution)/shard_map/ppermute | solution.py:453
  4.0 0.1 pad_add_fusion.place
  4.1 0.0 copy-start
  4.1 6.0 %shard_map.64 = (bf16[1024,512]{1,0:T(8,128)(2,1)S(1)}, bf16[2048,256]{1,0:T(8,128)(2,1)S(1)}) custom-call(bf16[1024,2048]{1,0:T(8,128)(2,1)} %acts.1, bf16[2048,768]{1,0:T(8,128)(2,1)} %weight_hbm.1), custom_call_target="tpu_custom_call" | custom-call | flops 2147483648 | bytes 1048576 | tf_op jit(solution)/shard_map/pallas_call | solution.py:416
  10.2 0.0 copy-done
  10.2 0.0 copy-done.1
  10.2 1.2 %shard_map.65 = (f32[8,2,128,128]{3,2,1,0:T(8,128)S(1)}, bf16[528,128]{1,0:T(8,128)(2,1)S(1)}, bf16[528,128]{1,0:T(8,128)(2,1)S(1)}, bf16[528,128]{1,0:T(8,128)(2,1)S(1)}, bf16[528,128]{1,0:T(8,128)(2,1)S(1)}) custom-call(s32[4]{0:T(128)S(1)} %pad_add_fusion.place, bf16[1024,512]{1,0:T(8,128)(2,1)S(1)} %get-tuple-element.30.kv, f32[2,1024]{1,0:T(2,128)S(1)} %bitcast.8, ...), custom_call_target="tpu_custom_call" | custom-call | bytes 1048576 | tf_op jit(solution)/shard_map/pallas_call | solution.py:416
  11.4 2.8 %collective-permute-start = (bf16[528,128]{1,0:T(8,128)(2,1)S(1)}, bf16[528,128]{1,0:T(8,128)(2,1)S(1)}, u32[]{:S(2)}, u32[]{:S(2)}) collective-permute-start(bf16[528,128]{1,0:T(8,128)(2,1)S(1)} %get-tuple-element.32), channel_id=1, source_target_pairs={{0,16},{8,24},{16,0},{24,8},{32,48},{40,56},{48,32},{56,40},{64,80... | collective-permute-start | bytes 405512 | tf_op jit(solution)/shard_map/ppermute | solution.py:443
  14.2 0.3 collective-permute-start.1
  14.6 0.6 collective-permute-start.2
  15.1 0.0 copy-done.2
  15.1 0.0 copy-done.4
  15.1 2.3 %shard_map.66 = (bf16[1024,256]{1,0:T(8,128)(2,1)S(1)}, f32[1024,128]{1,0:T(8,128)S(1)}) custom-call(bf16[1024,2048]{1,0:T(8,128)(2,1)S(1)} %copy-done.2, bf16[2048,256]{1,0:T(8,128)(2,1)S(1)} %get-tuple-element.35.weight, bf16[42,2048]{1,0:T(8,128)(2,1)S(1)} %bitcast.13, bf16[528,128]{1,0:T(8,128)(2,1)S(1)} %get-tuple-element.31.after.own), custom_call_target="tpu_custom_call" | custom-call | flops 2147483648 | bytes 1048576 | tf_op jit(solution)/shard_map/pallas_call | solution.py:416
  17.4 2.1 %shard_map.67.after.refs_2_ = bf16[1024,896]{1,0:T(8,128)(2,1)S(1)} custom-call(bf16[1024,256]{1,0:T(8,128)(2,1)S(1)} %get-tuple-element.36.query_rows, f32[1024,128]{1,0:T(8,128)S(1)} %get-tuple-element.37.level, f32[2,1024]{1,0:T(2,128)S(1)} %bitcast.9, bf16[528,128]{1,0:T(8,128)(2,1)S(1)} %get-tuple-element.31.after.own), custom_call_target="tpu_custom_call" | custom-call | flops 1073741824 | bytes 1048576 | tf_op jit(solution)/shard_map/pallas_call | solution.py:416
  19.5 0.0 collective-permute-done.two
  19.5 0.3 collective-permute-done.1.one
  19.8 0.9 %collective-permute-done.2.three = bf16[528,128]{1,0:T(8,128)(2,1)S(1)} collective-permute-done((bf16[528,128]{1,0:T(8,128)(2,1)S(1)}, bf16[528,128]{1,0:T(8,128)(2,1)S(1)}, u32[]{:S(2)}, u32[]{:S(2)}) %collective-permute-start.2) | collective-permute-done | bytes 135200 | tf_op jit(solution)/shard_map/ppermute | solution.py:443
  20.8 0.7 %shard_map.68 = (bf16[2,2,128,128]{3,2,1,0:T(8,128)(2,1)S(1)}, bf16[336,128]{1,0:T(8,128)(2,1)S(1)}, f32[8,128]{1,0:T(8,128)S(1)}) custom-call(s32[4]{0:T(128)S(1)} %pad_add_fusion.place, bf16[528,128]{1,0:T(8,128)(2,1)S(1)} %get-tuple-element.31.after.own, bf16[528,128]{1,0:T(8,128)(2,1)S(1)} %collective-permute-done.two, ...), custom_call_target="tpu_custom_call" | custom-call | bytes 1048576 | tf_op jit(solution)/shard_map/pallas_call | solution.py:416
  21.5 1.7 %collective-permute-start.3 = (bf16[336,128]{1,0:T(8,128)(2,1)S(1)}, bf16[336,128]{1,0:T(8,128)(2,1)S(1)}, u32[]{:S(2)}, u32[]{:S(2)}) collective-permute-start(bf16[336,128]{1,0:T(8,128)(2,1)S(1)} %get-tuple-element.38.after.own), channel_id=1, source_target_pairs={{0,32},{8,40},{16,48},{24,56},{32,0},{40,8},{48,16},{56,24},{64,96... | collective-permute-start | bytes 258056 | tf_op jit(solution)/shard_map/ppermute | solution.py:448
  23.2 1.9 %shard_map.69.after.refs_0_ = f32[1024,128]{1,0:T(8,128)S(1)} custom-call(bf16[1024,256]{1,0:T(8,128)(2,1)S(1)} %get-tuple-element.36.query_rows, bf16[1024,512]{1,0:T(8,128)(2,1)S(1)} %get-tuple-element.30.kv, f32[1024,128]{1,0:T(8,128)S(1)} %get-tuple-element.37.level, f32[2,1024]{1,0:T(2,128)S(1)} %bitcast.10, ...), custom_call_target="tpu_custom_call" | custom-call | flops 1073741824 | bytes 1048576 | tf_op jit(solution)/shard_map/pallas_call | solution.py:416
  25.1 0.3 collective-permute-done.3.got
  25.4 0.6 shard_map.70
  26.0 6.4 %collective-permute-start.4 = (bf16[336,128]{1,0:T(8,128)(2,1)S(1)}, bf16[336,128]{1,0:T(8,128)(2,1)S(1)}, u32[]{:S(2)}, u32[]{:S(2)}) collective-permute-start(bf16[336,128]{1,0:T(8,128)(2,1)S(1)} %get-tuple-element.42.after.own), channel_id=1, source_target_pairs={{0,160},{8,168},{16,176},{24,184},{32,128},{40,136},{48,144},{56,1... | collective-permute-start | bytes 258056 | tf_op jit(solution)/shard_map/ppermute | solution.py:448
  32.3 0.3 collective-permute-start.5
  32.6 2.8 %collective-permute-start.6 = (bf16[336,128]{1,0:T(8,128)(2,1)S(1)}, bf16[336,128]{1,0:T(8,128)(2,1)S(1)}, u32[]{:S(2)}, u32[]{:S(2)}) collective-permute-start(bf16[336,128]{1,0:T(8,128)(2,1)S(1)} %get-tuple-element.42.after.own), channel_id=1, source_target_pairs={{0,224},{8,232},{16,240},{24,248},{32,64},{40,72},{48,80},{56,88},... | collective-permute-start | bytes 258056 | tf_op jit(solution)/shard_map/ppermute | solution.py:448
  35.5 1.9 %shard_map.71.after.refs_1_ = f32[1024,128]{1,0:T(8,128)S(1)} custom-call(bf16[1024,256]{1,0:T(8,128)(2,1)S(1)} %get-tuple-element.36.query_rows, bf16[1024,512]{1,0:T(8,128)(2,1)S(1)} %get-tuple-element.30.kv, f32[1024,128]{1,0:T(8,128)S(1)} %get-tuple-element.37.level, f32[2,1024]{1,0:T(2,128)S(1)} %bitcast.11, ...), custom_call_target="tpu_custom_call" | custom-call | flops 1073741824 | bytes 1048576 | tf_op jit(solution)/shard_map/pallas_call | solution.py:416
  37.4 0.0 collective-permute-done.7.below.refs_5_
  37.4 0.0 collective-permute-done.8.above.refs_4_
  37.4 0.1 shard_map.72
  37.5 0.9 %collective-permute-start.13 = (bf16[128,2048]{1,0:T(8,128)(2,1)S(1)}, bf16[128,2048]{1,0:T(8,128)(2,1)S(1)}, u32[]{:S(2)}, u32[]{:S(2)}) collective-permute-start(bf16[128,2048]{1,0:T(8,128)(2,1)S(1)} %get-tuple-element.45.after), channel_id=1, source_target_pairs={{0,6},{1,7},{2,4},{3,5},{4,2},{5,3},{6,0},{7,1},{8,14},{9,15},{10,... | collective-permute-start | bytes 1572872 | tf_op jit(solution)/shard_map/ppermute | solution.py:453
  38.3 0.0 collective-permute-start.14
  38.3 0.0 collective-permute-done.4.far
  38.3 0.0 collective-permute-done.5.skip
  38.4 0.7 %collective-permute-done.6.near = bf16[336,128]{1,0:T(8,128)(2,1)S(1)} collective-permute-done((bf16[336,128]{1,0:T(8,128)(2,1)S(1)}, bf16[336,128]{1,0:T(8,128)(2,1)S(1)}, u32[]{:S(2)}, u32[]{:S(2)}) %collective-permute-start.6) | collective-permute-done | bytes 86048 | tf_op jit(solution)/shard_map/ppermute | solution.py:448
  39.1 0.6 shard_map.73
  39.7 2.3 %collective-permute-start.10 = (bf16[448,128]{1,0:T(8,128)(2,1)S(1)}, bf16[448,128]{1,0:T(8,128)(2,1)S(1)}, u32[]{:S(2)}, u32[]{:S(2)}) collective-permute-start(bf16[448,128]{1,0:T(8,128)(2,1)S(1)} %get-tuple-element.47.after.refs_4_), channel_id=1, source_target_pairs={{0,16},{8,24},{16,0},{24,8},{32,48},{40,56},{48,32},{56,40},{64,80... | collective-permute-start | bytes 344072 | tf_op jit(solution)/shard_map/ppermute | solution.py:443
  42.0 0.7 %collective-permute-start.11 = (bf16[448,128]{1,0:T(8,128)(2,1)S(1)}, bf16[448,128]{1,0:T(8,128)(2,1)S(1)}, u32[]{:S(2)}, u32[]{:S(2)}) collective-permute-start(bf16[448,128]{1,0:T(8,128)(2,1)S(1)} %get-tuple-element.47.after.refs_4_), channel_id=1, source_target_pairs={{0,24},{8,16},{16,8},{24,0},{32,56},{40,48},{48,40},{56,32},{64,88... | collective-permute-start | bytes 344072 | tf_op jit(solution)/shard_map/ppermute | solution.py:443
  42.7 0.0 collective-permute-start.9
  42.7 2.1 %shard_map.74.refs_3_ = bf16[1024,896]{1,0:T(8,128)(2,1)S(1)} custom-call(bf16[1024,256]{1,0:T(8,128)(2,1)S(1)} %get-tuple-element.36.query_rows, f32[1024,128]{1,0:T(8,128)S(1)} %get-tuple-element.37.level, f32[2,1024]{1,0:T(2,128)S(1)} %bitcast.12, bf16[448,128]{1,0:T(8,128)(2,1)S(1)} %get-tuple-element.47.after.refs_4_), custom_call_target="tpu_custom_call" | custom-call | flops 1073741824 | bytes 1048576 | tf_op jit(solution)/shard_map/pallas_call | solution.py:416
  44.8 0.1 collective-permute-done.10.refs_6_
  44.9 2.3 %collective-permute-done.11.refs_7_ = bf16[448,128]{1,0:T(8,128)(2,1)S(1)} collective-permute-done((bf16[448,128]{1,0:T(8,128)(2,1)S(1)}, bf16[448,128]{1,0:T(8,128)(2,1)S(1)}, u32[]{:S(2)}, u32[]{:S(2)}) %collective-permute-start.11) | collective-permute-done | bytes 114720 | tf_op jit(solution)/shard_map/ppermute | solution.py:443
  47.2 0.0 collective-permute-done.9.refs_5_
  47.2 1.6 %shard_map.75 = (bf16[256,256]{1,0:T(8,128)(2,1)S(1)}, bf16[256,256]{1,0:T(8,128)(2,1)S(1)}, bf16[256,256]{1,0:T(8,128)(2,1)S(1)}, bf16[2,896,128]{2,1,0:T(8,128)(2,1)S(1)}) custom-call(s32[4]{0:T(128)S(1)} %pad_add_fusion.place, f32[8,128]{1,0:T(8,128)S(1)} %get-tuple-element.46.carry, f32[1024,128]{1,0:T(8,128)S(1)} %shard_map.69.after.refs_0_, ...), custom_call_target="tpu_custom_call" | custom-call | flops 268435456 | bytes 1048576 | tf_op jit(solution)/shard_map/pallas_call | solution.py:416
  48.8 0.0 copy-start.3
  48.8 1.6 %collective-permute-start.15 = (bf16[256,256]{1,0:T(8,128)(2,1)S(1)}, bf16[256,256]{1,0:T(8,128)(2,1)S(1)}, u32[]{:S(2)}, u32[]{:S(2)}) collective-permute-start(bf16[256,256]{1,0:T(8,128)(2,1)S(1)} %get-tuple-element.52), channel_id=1, source_target_pairs={{0,6},{1,7},{2,4},{3,5},{4,2},{5,3},{6,0},{7,1},{8,14},{9,15},{10,... | collective-permute-start | bytes 393224 | tf_op jit(solution)/shard_map/ppermute | solution.py:453
  50.4 0.6 collective-permute-start.16
  51.0 1.8 %collective-permute-start.12 = (bf16[256,256]{1,0:T(8,128)(2,1)S(1)}, bf16[256,256]{1,0:T(8,128)(2,1)S(1)}, u32[]{:S(2)}, u32[]{:S(2)}) collective-permute-start(bf16[256,256]{1,0:T(8,128)(2,1)S(1)} %get-tuple-element.48), channel_id=1, source_target_pairs={{0,4},{1,5},{2,6},{3,7},{4,0},{5,1},{6,2},{7,3},{8,12},{9,13},{10,... | collective-permute-start | bytes 393224 | tf_op jit(solution)/shard_map/ppermute | solution.py:453
  52.8 1.0 %shard_map.76.refs_0_ = bf16[256,256]{1,0:T(8,128)(2,1)S(1)} custom-call(s32[4]{0:T(128)S(1)} %pad_add_fusion.place, f32[1024,128]{1,0:T(8,128)S(1)} %shard_map.69.after.refs_0_, f32[1024,128]{1,0:T(8,128)S(1)} %shard_map.71.after.refs_1_, bf16[1024,896]{1,0:T(8,128)(2,1)S(1)} %shard_map.67.after.refs_2_, bf16[1024,896]{1,0:T(8,128)(2,1)S(1)} %shard_map.74.refs_3_, ...), custom_call_target="tpu_custom_call" | custom-call | flops 268435456 | bytes 1048576 | tf_op jit(solution)/shard_map/pallas_call | solution.py:416
  53.8 0.1 collective-permute-done.15.refs_1_
  53.9 0.3 collective-permute-done.16.refs_2_
  54.2 0.0 copy-done.3
  54.2 2.0 %shard_map.77 = (f32[128,2048]{1,0:T(8,128)S(1)}, f32[128,2048]{1,0:T(8,128)S(1)}) custom-call(s32[4]{0:T(128)S(1)} %pad_add_fusion.place, bf16[256,256]{1,0:T(8,128)(2,1)S(1)} %shard_map.76.refs_0_, bf16[256,256]{1,0:T(8,128)(2,1)S(1)} %collective-permute-done.15.refs_1_, bf16[256,256]{1,0:T(8,128)(2,1)S(1)} %collective-permute-done.16.refs_2_, ...), custom_call_target="tpu_custom_call" | custom-call | flops 2147483648 | bytes 5242880 | tf_op jit(solution)/shard_map/pallas_call | solution.py:617
  56.2 0.3 collective-permute-done.12.piece
  56.5 0.0 collective-permute-done.13.first
  56.5 0.0 collective-permute-done.14.second
  56.5 0.8 %shard_map.80 = bf16[128,1024]{1,0:T(8,128)(2,1)S(1)} custom-call(s32[4]{0:T(128)S(1)} %pad_add_fusion.place, bf16[256,256]{1,0:T(8,128)(2,1)S(1)} %collective-permute-done.12.piece, bf16[128,2048]{1,0:T(8,128)(2,1)S(1)} %collective-permute-done.13.first, bf16[128,2048]{1,0:T(8,128)(2,1)S(1)} %collective-permute-done.14.second, ...), custom_call_target="tpu_custom_call" | custom-call | flops 268435456 | bytes 3145728 | tf_op jit(solution)/shard_map/pallas_call | solution.py:630
  57.3 6.5 %collective-permute-start.18 = (bf16[128,1024]{1,0:T(8,128)(2,1)S(1)}, bf16[128,1024]{1,0:T(8,128)(2,1)S(1)}, u32[]{:S(2)}, u32[]{:S(2)}) collective-permute-start(bf16[128,1024]{1,0:T(8,128)(2,1)S(1)} %shard_map.80), channel_id=1, source_target_pairs={{0,1},{1,0},{2,3},{3,2},{4,5},{5,4},{6,7},{7,6},{8,9},{9,8},{10,11... | collective-permute-start | bytes 786440 | tf_op jit(solution)/shard_map/ppermute | solution.py:642
  63.9 0.8 %shard_map.79 = bf16[128,1024]{1,0:T(8,128)(2,1)S(1)} custom-call(s32[4]{0:T(128)S(1)} %pad_add_fusion.place, bf16[256,256]{1,0:T(8,128)(2,1)S(1)} %collective-permute-done.12.piece, bf16[128,2048]{1,0:T(8,128)(2,1)S(1)} %collective-permute-done.13.first, bf16[128,2048]{1,0:T(8,128)(2,1)S(1)} %collective-permute-done.14.second, ...), custom_call_target="tpu_custom_call" | custom-call | flops 268435456 | bytes 3145728 | tf_op jit(solution)/shard_map/pallas_call | solution.py:630
  64.6 0.1 collective-permute-start.17
  64.7 1.2 %shard_map.78.keep = f32[128,2048]{1,0:T(8,128)S(1)} custom-call(s32[4]{0:T(128)S(1)} %pad_add_fusion.place, bf16[256,256]{1,0:T(8,128)(2,1)S(1)} %collective-permute-done.12.piece, bf16[128,2048]{1,0:T(8,128)(2,1)S(1)} %collective-permute-done.13.first, bf16[128,2048]{1,0:T(8,128)(2,1)S(1)} %collective-permute-done.14.second, ...), custom_call_target="tpu_custom_call" | custom-call | flops 268435456 | bytes 3145728 | tf_op jit(solution)/shard_map/pallas_call | solution.py:630
  66.0 0.0 collective-permute-done.18.refs_1_
  66.0 0.3 collective-permute-done.17.refs_0_
  66.3 0.9 %shard_map.81 = bf16[128,2048]{1,0:T(8,128)(2,1)} custom-call(f32[128,2048]{1,0:T(8,128)S(1)} %shard_map.78.keep, bf16[128,1024]{1,0:T(8,128)(2,1)S(1)} %collective-permute-done.17.refs_0_, bf16[128,1024]{1,0:T(8,128)(2,1)S(1)} %collective-permute-done.18.refs_1_), custom_call_target="tpu_custom_call" | custom-call | tf_op jit(solution)/shard_map/pallas_call | solution.py:646
  (3 shorter events, 0.0 us)
Async XLA Ops:
  0.0 37.4 %collective-permute-start.7 = (bf16[256,2048]{1,0:T(8,128)(2,1)}, bf16[256,2048]{1,0:T(8,128)(2,1)S(1)}, u32[]{:S(2)}, u32[]{:S(2)}) collective-permute-start(bf16[256,2048]{1,0:T(8,128)(2,1)} %refs_3_.1), channel_id=1, source_target_pairs={{0,2},{1,3},{2,0},{3,1},{4,6},{5,7},{6,4},{7,5},{8,10},{9,11},{10,... | collective-permute-start | bytes 3145736 | tf_op jit(solution)/shard_map/ppermute | solution.py:453
  2.1 35.2 %collective-permute-start.8 = (bf16[256,2048]{1,0:T(8,128)(2,1)}, bf16[256,2048]{1,0:T(8,128)(2,1)S(1)}, u32[]{:S(2)}, u32[]{:S(2)}) collective-permute-start(bf16[256,2048]{1,0:T(8,128)(2,1)} %refs_3_.1), channel_id=1, source_target_pairs={{0,6},{1,7},{2,4},{3,5},{4,2},{5,3},{6,0},{7,1},{8,14},{9,15},{10,... | collective-permute-start | bytes 3145736 | tf_op jit(solution)/shard_map/ppermute | solution.py:453
  4.1 6.0 %copy-start = (f32[1,4,2,128,128]{4,3,2,1,0:T(8,128)S(1)}, f32[1,4,2,128,128]{4,3,2,1,0:T(8,128)}, u32[]{:S(2)}) copy-start(f32[1,4,2,128,128]{4,3,2,1,0:T(8,128)} %param.10) | copy-start | bytes 1572868
  4.1 6.1 %copy-start.1 = (f32[1024,2]{0,1:T(2,128)S(1)}, f32[1024,2]{0,1:T(2,128)}, u32[]{:S(2)}) copy-start(f32[1024,2]{0,1:T(2,128)} %param.9) | copy-start | bytes 24580
  4.1 11.0 %copy-start.2 = (bf16[1024,2048]{1,0:T(8,128)(2,1)S(1)}, bf16[1024,2048]{1,0:T(8,128)(2,1)}, u32[]{:S(2)}) copy-start(bf16[1024,2048]{1,0:T(8,128)(2,1)} %acts.1) | copy-start | bytes 12582916
  4.1 11.0 %copy-start.4 = (bf16[2048,42]{0,1:T(8,128)(2,1)S(1)}, bf16[2048,42]{0,1:T(8,128)(2,1)}, u32[]{:S(2)}) copy-start(bf16[2048,42]{0,1:T(8,128)(2,1)} %param.8) | copy-start | bytes 516100
  11.4 8.1 %collective-permute-start = (bf16[528,128]{1,0:T(8,128)(2,1)S(1)}, bf16[528,128]{1,0:T(8,128)(2,1)S(1)}, u32[]{:S(2)}, u32[]{:S(2)}) collective-permute-start(bf16[528,128]{1,0:T(8,128)(2,1)S(1)} %get-tuple-element.32), channel_id=1, source_target_pairs={{0,16},{8,24},{16,0},{24,8},{32,48},{40,56},{48,32},{56,40},{64,80... | collective-permute-start | bytes 405512 | tf_op jit(solution)/shard_map/ppermute | solution.py:443
  14.2 5.6 %collective-permute-start.1 = (bf16[528,128]{1,0:T(8,128)(2,1)S(1)}, bf16[528,128]{1,0:T(8,128)(2,1)S(1)}, u32[]{:S(2)}, u32[]{:S(2)}) collective-permute-start(bf16[528,128]{1,0:T(8,128)(2,1)S(1)} %get-tuple-element.33), channel_id=1, source_target_pairs={{0,8},{8,0},{16,24},{24,16},{32,40},{40,32},{48,56},{56,48},{64,72... | collective-permute-start | bytes 405512 | tf_op jit(solution)/shard_map/ppermute | solution.py:443
  14.6 6.2 %collective-permute-start.2 = (bf16[528,128]{1,0:T(8,128)(2,1)S(1)}, bf16[528,128]{1,0:T(8,128)(2,1)S(1)}, u32[]{:S(2)}, u32[]{:S(2)}) collective-permute-start(bf16[528,128]{1,0:T(8,128)(2,1)S(1)} %get-tuple-element.34), channel_id=1, source_target_pairs={{0,24},{8,16},{16,8},{24,0},{32,56},{40,48},{48,40},{56,32},{64,88... | collective-permute-start | bytes 405512 | tf_op jit(solution)/shard_map/ppermute | solution.py:443
  21.5 3.9 %collective-permute-start.3 = (bf16[336,128]{1,0:T(8,128)(2,1)S(1)}, bf16[336,128]{1,0:T(8,128)(2,1)S(1)}, u32[]{:S(2)}, u32[]{:S(2)}) collective-permute-start(bf16[336,128]{1,0:T(8,128)(2,1)S(1)} %get-tuple-element.38.after.own), channel_id=1, source_target_pairs={{0,32},{8,40},{16,48},{24,56},{32,0},{40,8},{48,16},{56,24},{64,96... | collective-permute-start | bytes 258056 | tf_op jit(solution)/shard_map/ppermute | solution.py:448
  26.0 12.4 %collective-permute-start.4 = (bf16[336,128]{1,0:T(8,128)(2,1)S(1)}, bf16[336,128]{1,0:T(8,128)(2,1)S(1)}, u32[]{:S(2)}, u32[]{:S(2)}) collective-permute-start(bf16[336,128]{1,0:T(8,128)(2,1)S(1)} %get-tuple-element.42.after.own), channel_id=1, source_target_pairs={{0,160},{8,168},{16,176},{24,184},{32,128},{40,136},{48,144},{56,1... | collective-permute-start | bytes 258056 | tf_op jit(solution)/shard_map/ppermute | solution.py:448
  32.3 6.0 %collective-permute-start.5 = (bf16[336,128]{1,0:T(8,128)(2,1)S(1)}, bf16[336,128]{1,0:T(8,128)(2,1)S(1)}, u32[]{:S(2)}, u32[]{:S(2)}) collective-permute-start(bf16[336,128]{1,0:T(8,128)(2,1)S(1)} %get-tuple-element.42.after.own), channel_id=1, source_target_pairs={{0,192},{8,200},{16,208},{24,216},{32,96},{40,104},{48,112},{56,12... | collective-permute-start | bytes 258056 | tf_op jit(solution)/shard_map/ppermute | solution.py:448
  32.6 6.5 %collective-permute-start.6 = (bf16[336,128]{1,0:T(8,128)(2,1)S(1)}, bf16[336,128]{1,0:T(8,128)(2,1)S(1)}, u32[]{:S(2)}, u32[]{:S(2)}) collective-permute-start(bf16[336,128]{1,0:T(8,128)(2,1)S(1)} %get-tuple-element.42.after.own), channel_id=1, source_target_pairs={{0,224},{8,232},{16,240},{24,248},{32,64},{40,72},{48,80},{56,88},... | collective-permute-start | bytes 258056 | tf_op jit(solution)/shard_map/ppermute | solution.py:448
  37.5 19.0 %collective-permute-start.13 = (bf16[128,2048]{1,0:T(8,128)(2,1)S(1)}, bf16[128,2048]{1,0:T(8,128)(2,1)S(1)}, u32[]{:S(2)}, u32[]{:S(2)}) collective-permute-start(bf16[128,2048]{1,0:T(8,128)(2,1)S(1)} %get-tuple-element.45.after), channel_id=1, source_target_pairs={{0,6},{1,7},{2,4},{3,5},{4,2},{5,3},{6,0},{7,1},{8,14},{9,15},{10,... | collective-permute-start | bytes 1572872 | tf_op jit(solution)/shard_map/ppermute | solution.py:453
  38.3 18.2 %collective-permute-start.14 = (bf16[128,2048]{1,0:T(8,128)(2,1)S(1)}, bf16[128,2048]{1,0:T(8,128)(2,1)S(1)}, u32[]{:S(2)}, u32[]{:S(2)}) collective-permute-start(bf16[128,2048]{1,0:T(8,128)(2,1)S(1)} %get-tuple-element.49), channel_id=1, source_target_pairs={{0,2},{1,3},{2,0},{3,1},{4,6},{5,7},{6,4},{7,5},{8,10},{9,11},{10,... | collective-permute-start | bytes 1572872 | tf_op jit(solution)/shard_map/ppermute | solution.py:453
  39.7 5.2 %collective-permute-start.10 = (bf16[448,128]{1,0:T(8,128)(2,1)S(1)}, bf16[448,128]{1,0:T(8,128)(2,1)S(1)}, u32[]{:S(2)}, u32[]{:S(2)}) collective-permute-start(bf16[448,128]{1,0:T(8,128)(2,1)S(1)} %get-tuple-element.47.after.refs_4_), channel_id=1, source_target_pairs={{0,16},{8,24},{16,0},{24,8},{32,48},{40,56},{48,32},{56,40},{64,80... | collective-permute-start | bytes 344072 | tf_op jit(solution)/shard_map/ppermute | solution.py:443
  42.0 5.1 %collective-permute-start.11 = (bf16[448,128]{1,0:T(8,128)(2,1)S(1)}, bf16[448,128]{1,0:T(8,128)(2,1)S(1)}, u32[]{:S(2)}, u32[]{:S(2)}) collective-permute-start(bf16[448,128]{1,0:T(8,128)(2,1)S(1)} %get-tuple-element.47.after.refs_4_), channel_id=1, source_target_pairs={{0,24},{8,16},{16,8},{24,0},{32,56},{40,48},{48,40},{56,32},{64,88... | collective-permute-start | bytes 344072 | tf_op jit(solution)/shard_map/ppermute | solution.py:443
  42.7 4.4 %collective-permute-start.9 = (bf16[448,128]{1,0:T(8,128)(2,1)S(1)}, bf16[448,128]{1,0:T(8,128)(2,1)S(1)}, u32[]{:S(2)}, u32[]{:S(2)}) collective-permute-start(bf16[448,128]{1,0:T(8,128)(2,1)S(1)} %get-tuple-element.47.after.refs_4_), channel_id=1, source_target_pairs={{0,8},{8,0},{16,24},{24,16},{32,40},{40,32},{48,56},{56,48},{64,72... | collective-permute-start | bytes 344072 | tf_op jit(solution)/shard_map/ppermute | solution.py:443
  48.8 5.4 %copy-start.3 = (bf16[256,2048]{1,0:T(8,128)(2,1)S(1)}, bf16[256,2048]{1,0:T(8,128)(2,1)}, u32[]{:S(2)}) copy-start(bf16[256,2048]{1,0:T(8,128)(2,1)} %refs_3_.1) | copy-start | bytes 3145732
  48.8 5.1 %collective-permute-start.15 = (bf16[256,256]{1,0:T(8,128)(2,1)S(1)}, bf16[256,256]{1,0:T(8,128)(2,1)S(1)}, u32[]{:S(2)}, u32[]{:S(2)}) collective-permute-start(bf16[256,256]{1,0:T(8,128)(2,1)S(1)} %get-tuple-element.52), channel_id=1, source_target_pairs={{0,6},{1,7},{2,4},{3,5},{4,2},{5,3},{6,0},{7,1},{8,14},{9,15},{10,... | collective-permute-start | bytes 393224 | tf_op jit(solution)/shard_map/ppermute | solution.py:453
  50.4 3.8 %collective-permute-start.16 = (bf16[256,256]{1,0:T(8,128)(2,1)S(1)}, bf16[256,256]{1,0:T(8,128)(2,1)S(1)}, u32[]{:S(2)}, u32[]{:S(2)}) collective-permute-start(bf16[256,256]{1,0:T(8,128)(2,1)S(1)} %get-tuple-element.51.refs_5_), channel_id=1, source_target_pairs={{0,2},{1,3},{2,0},{3,1},{4,6},{5,7},{6,4},{7,5},{8,10},{9,11},{10,... | collective-permute-start | bytes 393224 | tf_op jit(solution)/shard_map/ppermute | solution.py:453
  51.0 5.5 %collective-permute-start.12 = (bf16[256,256]{1,0:T(8,128)(2,1)S(1)}, bf16[256,256]{1,0:T(8,128)(2,1)S(1)}, u32[]{:S(2)}, u32[]{:S(2)}) collective-permute-start(bf16[256,256]{1,0:T(8,128)(2,1)S(1)} %get-tuple-element.48), channel_id=1, source_target_pairs={{0,4},{1,5},{2,6},{3,7},{4,0},{5,1},{6,2},{7,3},{8,12},{9,13},{10,... | collective-permute-start | bytes 393224 | tf_op jit(solution)/shard_map/ppermute | solution.py:453
  57.3 8.6 %collective-permute-start.18 = (bf16[128,1024]{1,0:T(8,128)(2,1)S(1)}, bf16[128,1024]{1,0:T(8,128)(2,1)S(1)}, u32[]{:S(2)}, u32[]{:S(2)}) collective-permute-start(bf16[128,1024]{1,0:T(8,128)(2,1)S(1)} %shard_map.80), channel_id=1, source_target_pairs={{0,1},{1,0},{2,3},{3,2},{4,5},{5,4},{6,7},{7,6},{8,9},{9,8},{10,11... | collective-permute-start | bytes 786440 | tf_op jit(solution)/shard_map/ppermute | solution.py:642
  64.6 1.6 %collective-permute-start.17 = (bf16[128,1024]{1,0:T(8,128)(2,1)S(1)}, bf16[128,1024]{1,0:T(8,128)(2,1)S(1)}, u32[]{:S(2)}, u32[]{:S(2)}) collective-permute-start(bf16[128,1024]{1,0:T(8,128)(2,1)S(1)} %shard_map.79), channel_id=1, source_target_pairs={{0,1},{1,0},{2,3},{3,2},{4,5},{5,4},{6,7},{7,6},{8,9},{9,8},{10,11... | collective-permute-start | bytes 786440 | tf_op jit(solution)/shard_map/ppermute | solution.py:642

commit v6 on v3

--- a/solution.py
+++ b/solution.py
@@ -63,7 +63,6 @@
     for i in range(count):
         part = pl.ds(i * size, size)
         copies.append(pltpu.make_async_copy(source.at[part, :], target.at[part, :], sems.at[i]))
-        copies[-1].start(priority=1)
     return copies
 
 
@@ -72,8 +71,13 @@
     heads = query_weight.shape[1] // DH
     weight_copies = copy_parts(weight_hbm, weight, weight_sem)
     acts_copies = copy_parts(acts_hbm, acts, acts_sem)
+    half = len(acts_copies) // 2
+    for copy in weight_copies + acts_copies[:half]:
+        copy.start()
     for copy in weight_copies:
         copy.wait()
+    for copy in acts_copies[half:]:
+        copy.start()
     per_tile = len(acts_copies) * TILE // block
     for i in range(block // TILE):
         for copy in acts_copies[i * per_tile : (i + 1) * per_tile]:
@@ -196,7 +200,7 @@
         before = before + jnp.sum(gates, axis=1, keepdims=True)
 
 
-def within_kernel(place, own, two, one, three, after, states, onward, carry):
+def within_kernel(place, own, two, three, one, after, states, onward, carry):
     pieces = (own, one, two, three)
     x = place[0]
     heads = states.shape[1]
@@ -505,8 +509,8 @@
         place,
         pieces[0],
         pieces[2],
+        pieces[3],
         pieces[1],
-        pieces[3],
         lefts[0],
         specs=[SMEM] + [VMEM] * NX + [ANY],
     )

time: 66.9 us -> 66.8 us (level)
  no operation moved by 1% of the time
where the time goes in v6:
time: 66.8 us; the launch traced here: 66.7 us
  starting transfers between devices  33.9 us (51%)
  Pallas kernels  26.5 us (40%)
  waiting for transfers between devices  5.09 us (8%)
  other arithmetic  0.97 us (1%)
    pallas_call x13, Pallas kernels, small(): pl.pallas_call(kernel, out_shape=shapes, in_specs=specs or [SMEM if o.dty...  22.1 us
    ppermute x4, starting transfers between devices, across_z(): lax.ppermute(array, 'ctx', [(z * NX + x, target(z) % nz * NX + x) for z i...  11.2 us
    ppermute x7, starting transfers between devices, along_y(): lax.ppermute(array, 'head', [(y * 2 + c, (y ^ d) * 2 + c) for y in range(...  8.84 us
    ppermute x6, starting transfers between devices, along_x(): lax.ppermute(array, 'ctx', [(z * NX + x, z * NX + (x ^ d)) for z in range...  7.37 us
    ppermute x1, starting transfers between devices, shards(): got = lax.ppermute(send, 'head', [(i, i ^ 1) for i in range(nh)])  6.5 us
    ppermute x6, waiting for transfers between devices, along_x(): lax.ppermute(array, 'ctx', [(z * NX + x, z * NX + (x ^ d)) for z in range...  2.95 us
    pallas_call x2, Pallas kernels, add_far(): pl.pallas_call(functools.partial(far_kernel, side), grid=(width // column...  2.36 us
    pallas_call x1, Pallas kernels, shards(): pl.pallas_call(near_kernel, grid=(width // columns,), in_specs=[SMEM] + [...  1.99 us
  transfers between devices with their start and end apart: 18, of which 10 were waited for; matrix products, arithmetic and copies ran while one was open for 0% of the time, Pallas kernels for 38%

profile of v6, /device:TPU:1, one launch (start us, length us, event | category | flops | bytes accessed | tf_op | source)
XLA Modules:
  0.0 66.7 jit_solution(8960570570116367384)
XLA Ops:
  0.0 2.1 %collective-permute-start.7 = (bf16[256,2048]{1,0:T(8,128)(2,1)}, bf16[256,2048]{1,0:T(8,128)(2,1)S(1)}, u32[]{:S(2)}, u32[]{:S(2)}) collective-permute-start(bf16[256,2048]{1,0:T(8,128)(2,1)} %refs_3_.1), channel_id=1, source_target_pairs={{0,2},{1,3},{2,0},{3,1},{4,6},{5,7},{6,4},{7,5},{8,10},{9,11},{10,... | collective-permute-start | bytes 3145736 | tf_op jit(solution)/shard_map/ppermute | solution.py:444
  2.1 1.9 %collective-permute-start.8 = (bf16[256,2048]{1,0:T(8,128)(2,1)}, bf16[256,2048]{1,0:T(8,128)(2,1)S(1)}, u32[]{:S(2)}, u32[]{:S(2)}) collective-permute-start(bf16[256,2048]{1,0:T(8,128)(2,1)} %refs_3_.1), channel_id=1, source_target_pairs={{0,6},{1,7},{2,4},{3,5},{4,2},{5,3},{6,0},{7,1},{8,14},{9,15},{10,... | collective-permute-start | bytes 3145736 | tf_op jit(solution)/shard_map/ppermute | solution.py:444
  4.0 0.1 pad_add_fusion.place
  4.1 0.0 copy-start
  4.1 0.0 copy-start.1
  4.1 0.0 copy-start.2
  4.1 0.0 copy-start.4
  4.1 6.0 %shard_map.64 = (bf16[1024,512]{1,0:T(8,128)(2,1)S(1)}, bf16[2048,256]{1,0:T(8,128)(2,1)S(1)}) custom-call(bf16[1024,2048]{1,0:T(8,128)(2,1)} %acts.1, bf16[2048,768]{1,0:T(8,128)(2,1)} %weight_hbm.1), custom_call_target="tpu_custom_call" | custom-call | flops 2147483648 | bytes 1048576 | tf_op jit(solution)/shard_map/pallas_call | solution.py:407
  10.2 0.0 copy-done
  10.2 0.0 copy-done.1
  10.2 1.2 %shard_map.65 = (f32[8,2,128,128]{3,2,1,0:T(8,128)S(1)}, bf16[528,128]{1,0:T(8,128)(2,1)S(1)}, bf16[528,128]{1,0:T(8,128)(2,1)S(1)}, bf16[528,128]{1,0:T(8,128)(2,1)S(1)}, bf16[528,128]{1,0:T(8,128)(2,1)S(1)}) custom-call(s32[4]{0:T(128)S(1)} %pad_add_fusion.place, bf16[1024,512]{1,0:T(8,128)(2,1)S(1)} %get-tuple-element.30.kv, f32[2,1024]{1,0:T(2,128)S(1)} %bitcast.8, ...), custom_call_target="tpu_custom_call" | custom-call | bytes 1048576 | tf_op jit(solution)/shard_map/pallas_call | solution.py:407
  11.4 2.8 %collective-permute-start = (bf16[528,128]{1,0:T(8,128)(2,1)S(1)}, bf16[528,128]{1,0:T(8,128)(2,1)S(1)}, u32[]{:S(2)}, u32[]{:S(2)}) collective-permute-start(bf16[528,128]{1,0:T(8,128)(2,1)S(1)} %get-tuple-element.32), channel_id=1, source_target_pairs={{0,16},{8,24},{16,0},{24,8},{32,48},{40,56},{48,32},{56,40},{64,80... | collective-permute-start | bytes 405512 | tf_op jit(solution)/shard_map/ppermute | solution.py:434
  14.2 0.9 %collective-permute-start.1 = (bf16[528,128]{1,0:T(8,128)(2,1)S(1)}, bf16[528,128]{1,0:T(8,128)(2,1)S(1)}, u32[]{:S(2)}, u32[]{:S(2)}) collective-permute-start(bf16[528,128]{1,0:T(8,128)(2,1)S(1)} %get-tuple-element.33), channel_id=1, source_target_pairs={{0,24},{8,16},{16,8},{24,0},{32,56},{40,48},{48,40},{56,32},{64,88... | collective-permute-start | bytes 405512 | tf_op jit(solution)/shard_map/ppermute | solution.py:434
  15.1 0.0 collective-permute-start.2
  15.1 0.0 copy-done.2
  15.1 0.0 copy-done.4
  15.1 2.3 %shard_map.66 = (bf16[1024,256]{1,0:T(8,128)(2,1)S(1)}, f32[1024,128]{1,0:T(8,128)S(1)}) custom-call(bf16[1024,2048]{1,0:T(8,128)(2,1)S(1)} %copy-done.2, bf16[2048,256]{1,0:T(8,128)(2,1)S(1)} %get-tuple-element.35.weight, bf16[42,2048]{1,0:T(8,128)(2,1)S(1)} %bitcast.13, bf16[528,128]{1,0:T(8,128)(2,1)S(1)} %get-tuple-element.31.after.own), custom_call_target="tpu_custom_call" | custom-call | flops 2147483648 | bytes 1048576 | tf_op jit(solution)/shard_map/pallas_call | solution.py:407
  17.5 2.1 %shard_map.67.after.refs_2_ = bf16[1024,896]{1,0:T(8,128)(2,1)S(1)} custom-call(bf16[1024,256]{1,0:T(8,128)(2,1)S(1)} %get-tuple-element.36.query_rows, f32[1024,128]{1,0:T(8,128)S(1)} %get-tuple-element.37.level, f32[2,1024]{1,0:T(2,128)S(1)} %bitcast.9, bf16[528,128]{1,0:T(8,128)(2,1)S(1)} %get-tuple-element.31.after.own), custom_call_target="tpu_custom_call" | custom-call | flops 1073741824 | bytes 1048576 | tf_op jit(solution)/shard_map/pallas_call | solution.py:407
  19.5 0.0 collective-permute-done.two
  19.5 0.9 %collective-permute-done.1.three = bf16[528,128]{1,0:T(8,128)(2,1)S(1)} collective-permute-done((bf16[528,128]{1,0:T(8,128)(2,1)S(1)}, bf16[528,128]{1,0:T(8,128)(2,1)S(1)}, u32[]{:S(2)}, u32[]{:S(2)}) %collective-permute-start.1) | collective-permute-done | bytes 135200 | tf_op jit(solution)/shard_map/ppermute | solution.py:434
  20.4 0.2 collective-permute-done.2.one
  20.6 0.7 %shard_map.68 = (bf16[2,2,128,128]{3,2,1,0:T(8,128)(2,1)S(1)}, bf16[336,128]{1,0:T(8,128)(2,1)S(1)}, f32[8,128]{1,0:T(8,128)S(1)}) custom-call(s32[4]{0:T(128)S(1)} %pad_add_fusion.place, bf16[528,128]{1,0:T(8,128)(2,1)S(1)} %get-tuple-element.31.after.own, bf16[528,128]{1,0:T(8,128)(2,1)S(1)} %collective-permute-done.two, ...), custom_call_target="tpu_custom_call" | custom-call | bytes 1048576 | tf_op jit(solution)/shard_map/pallas_call | solution.py:407
  21.3 1.7 %collective-permute-start.3 = (bf16[336,128]{1,0:T(8,128)(2,1)S(1)}, bf16[336,128]{1,0:T(8,128)(2,1)S(1)}, u32[]{:S(2)}, u32[]{:S(2)}) collective-permute-start(bf16[336,128]{1,0:T(8,128)(2,1)S(1)} %get-tuple-element.38.after.own), channel_id=1, source_target_pairs={{0,32},{8,40},{16,48},{24,56},{32,0},{40,8},{48,16},{56,24},{64,96... | collective-permute-start | bytes 258056 | tf_op jit(solution)/shard_map/ppermute | solution.py:439
  23.1 1.9 %shard_map.69.after.refs_0_ = f32[1024,128]{1,0:T(8,128)S(1)} custom-call(bf16[1024,256]{1,0:T(8,128)(2,1)S(1)} %get-tuple-element.36.query_rows, bf16[1024,512]{1,0:T(8,128)(2,1)S(1)} %get-tuple-element.30.kv, f32[1024,128]{1,0:T(8,128)S(1)} %get-tuple-element.37.level, f32[2,1024]{1,0:T(2,128)S(1)} %bitcast.10, ...), custom_call_target="tpu_custom_call" | custom-call | flops 1073741824 | bytes 1048576 | tf_op jit(solution)/shard_map/pallas_call | solution.py:407
  25.0 0.3 collective-permute-done.3.got
  25.2 0.6 shard_map.70
  25.8 6.4 %collective-permute-start.4 = (bf16[336,128]{1,0:T(8,128)(2,1)S(1)}, bf16[336,128]{1,0:T(8,128)(2,1)S(1)}, u32[]{:S(2)}, u32[]{:S(2)}) collective-permute-start(bf16[336,128]{1,0:T(8,128)(2,1)S(1)} %get-tuple-element.42.after.own), channel_id=1, source_target_pairs={{0,160},{8,168},{16,176},{24,184},{32,128},{40,136},{48,144},{56,1... | collective-permute-start | bytes 258056 | tf_op jit(solution)/shard_map/ppermute | solution.py:439
  32.2 0.3 collective-permute-start.5
  32.5 2.9 %collective-permute-start.6 = (bf16[336,128]{1,0:T(8,128)(2,1)S(1)}, bf16[336,128]{1,0:T(8,128)(2,1)S(1)}, u32[]{:S(2)}, u32[]{:S(2)}) collective-permute-start(bf16[336,128]{1,0:T(8,128)(2,1)S(1)} %get-tuple-element.42.after.own), channel_id=1, source_target_pairs={{0,224},{8,232},{16,240},{24,248},{32,64},{40,72},{48,80},{56,88},... | collective-permute-start | bytes 258056 | tf_op jit(solution)/shard_map/ppermute | solution.py:439
  35.3 1.9 %shard_map.71.after.refs_1_ = f32[1024,128]{1,0:T(8,128)S(1)} custom-call(bf16[1024,256]{1,0:T(8,128)(2,1)S(1)} %get-tuple-element.36.query_rows, bf16[1024,512]{1,0:T(8,128)(2,1)S(1)} %get-tuple-element.30.kv, f32[1024,128]{1,0:T(8,128)S(1)} %get-tuple-element.37.level, f32[2,1024]{1,0:T(2,128)S(1)} %bitcast.11, ...), custom_call_target="tpu_custom_call" | custom-call | flops 1073741824 | bytes 1048576 | tf_op jit(solution)/shard_map/pallas_call | solution.py:407
  37.2 0.0 collective-permute-done.7.below.refs_5_
  37.2 0.0 collective-permute-done.8.above.refs_4_
  37.2 0.1 shard_map.72
  37.4 0.9 %collective-permute-start.13 = (bf16[128,2048]{1,0:T(8,128)(2,1)S(1)}, bf16[128,2048]{1,0:T(8,128)(2,1)S(1)}, u32[]{:S(2)}, u32[]{:S(2)}) collective-permute-start(bf16[128,2048]{1,0:T(8,128)(2,1)S(1)} %get-tuple-element.45.after), channel_id=1, source_target_pairs={{0,6},{1,7},{2,4},{3,5},{4,2},{5,3},{6,0},{7,1},{8,14},{9,15},{10,... | collective-permute-start | bytes 1572872 | tf_op jit(solution)/shard_map/ppermute | solution.py:444
  38.2 0.0 collective-permute-start.14
  38.2 0.0 collective-permute-done.4.far
  38.2 0.0 collective-permute-done.5.skip
  38.2 0.6 collective-permute-done.6.near
  38.8 0.6 shard_map.73
  39.4 2.3 %collective-permute-start.10 = (bf16[448,128]{1,0:T(8,128)(2,1)S(1)}, bf16[448,128]{1,0:T(8,128)(2,1)S(1)}, u32[]{:S(2)}, u32[]{:S(2)}) collective-permute-start(bf16[448,128]{1,0:T(8,128)(2,1)S(1)} %get-tuple-element.47.after.refs_4_), channel_id=1, source_target_pairs={{0,16},{8,24},{16,0},{24,8},{32,48},{40,56},{48,32},{56,40},{64,80... | collective-permute-start | bytes 344072 | tf_op jit(solution)/shard_map/ppermute | solution.py:434
  41.7 1.3 %collective-permute-start.11 = (bf16[448,128]{1,0:T(8,128)(2,1)S(1)}, bf16[448,128]{1,0:T(8,128)(2,1)S(1)}, u32[]{:S(2)}, u32[]{:S(2)}) collective-permute-start(bf16[448,128]{1,0:T(8,128)(2,1)S(1)} %get-tuple-element.47.after.refs_4_), channel_id=1, source_target_pairs={{0,24},{8,16},{16,8},{24,0},{32,56},{40,48},{48,40},{56,32},{64,88... | collective-permute-start | bytes 344072 | tf_op jit(solution)/shard_map/ppermute | solution.py:434
  43.1 0.0 collective-permute-start.9
  43.1 2.1 %shard_map.74.refs_3_ = bf16[1024,896]{1,0:T(8,128)(2,1)S(1)} custom-call(bf16[1024,256]{1,0:T(8,128)(2,1)S(1)} %get-tuple-element.36.query_rows, f32[1024,128]{1,0:T(8,128)S(1)} %get-tuple-element.37.level, f32[2,1024]{1,0:T(2,128)S(1)} %bitcast.12, bf16[448,128]{1,0:T(8,128)(2,1)S(1)} %get-tuple-element.47.after.refs_4_), custom_call_target="tpu_custom_call" | custom-call | flops 1073741824 | bytes 1048576 | tf_op jit(solution)/shard_map/pallas_call | solution.py:407
  45.1 0.0 collective-permute-done.10.refs_6_
  45.2 1.7 %collective-permute-done.11.refs_7_ = bf16[448,128]{1,0:T(8,128)(2,1)S(1)} collective-permute-done((bf16[448,128]{1,0:T(8,128)(2,1)S(1)}, bf16[448,128]{1,0:T(8,128)(2,1)S(1)}, u32[]{:S(2)}, u32[]{:S(2)}) %collective-permute-start.11) | collective-permute-done | bytes 114720 | tf_op jit(solution)/shard_map/ppermute | solution.py:434
  46.9 0.1 collective-permute-done.9.refs_5_
  47.0 1.6 %shard_map.75 = (bf16[256,256]{1,0:T(8,128)(2,1)S(1)}, bf16[256,256]{1,0:T(8,128)(2,1)S(1)}, bf16[256,256]{1,0:T(8,128)(2,1)S(1)}, bf16[2,896,128]{2,1,0:T(8,128)(2,1)S(1)}) custom-call(s32[4]{0:T(128)S(1)} %pad_add_fusion.place, f32[8,128]{1,0:T(8,128)S(1)} %get-tuple-element.46.carry, f32[1024,128]{1,0:T(8,128)S(1)} %shard_map.69.after.refs_0_, ...), custom_call_target="tpu_custom_call" | custom-call | flops 268435456 | bytes 1048576 | tf_op jit(solution)/shard_map/pallas_call | solution.py:407
  48.6 0.0 copy-start.3
  48.6 1.7 %collective-permute-start.15 = (bf16[256,256]{1,0:T(8,128)(2,1)S(1)}, bf16[256,256]{1,0:T(8,128)(2,1)S(1)}, u32[]{:S(2)}, u32[]{:S(2)}) collective-permute-start(bf16[256,256]{1,0:T(8,128)(2,1)S(1)} %get-tuple-element.52), channel_id=1, source_target_pairs={{0,6},{1,7},{2,4},{3,5},{4,2},{5,3},{6,0},{7,1},{8,14},{9,15},{10,... | collective-permute-start | bytes 393224 | tf_op jit(solution)/shard_map/ppermute | solution.py:444
  50.4 0.9 %collective-permute-start.16 = (bf16[256,256]{1,0:T(8,128)(2,1)S(1)}, bf16[256,256]{1,0:T(8,128)(2,1)S(1)}, u32[]{:S(2)}, u32[]{:S(2)}) collective-permute-start(bf16[256,256]{1,0:T(8,128)(2,1)S(1)} %get-tuple-element.51.refs_5_), channel_id=1, source_target_pairs={{0,2},{1,3},{2,0},{3,1},{4,6},{5,7},{6,4},{7,5},{8,10},{9,11},{10,... | collective-permute-start | bytes 393224 | tf_op jit(solution)/shard_map/ppermute | solution.py:444
  51.2 1.3 %collective-permute-start.12 = (bf16[256,256]{1,0:T(8,128)(2,1)S(1)}, bf16[256,256]{1,0:T(8,128)(2,1)S(1)}, u32[]{:S(2)}, u32[]{:S(2)}) collective-permute-start(bf16[256,256]{1,0:T(8,128)(2,1)S(1)} %get-tuple-element.48), channel_id=1, source_target_pairs={{0,4},{1,5},{2,6},{3,7},{4,0},{5,1},{6,2},{7,3},{8,12},{9,13},{10,... | collective-permute-start | bytes 393224 | tf_op jit(solution)/shard_map/ppermute | solution.py:444
  52.6 1.0 %shard_map.76.refs_0_ = bf16[256,256]{1,0:T(8,128)(2,1)S(1)} custom-call(s32[4]{0:T(128)S(1)} %pad_add_fusion.place, f32[1024,128]{1,0:T(8,128)S(1)} %shard_map.69.after.refs_0_, f32[1024,128]{1,0:T(8,128)S(1)} %shard_map.71.after.refs_1_, bf16[1024,896]{1,0:T(8,128)(2,1)S(1)} %shard_map.67.after.refs_2_, bf16[1024,896]{1,0:T(8,128)(2,1)S(1)} %shard_map.74.refs_3_, ...), custom_call_target="tpu_custom_call" | custom-call | flops 268435456 | bytes 1048576 | tf_op jit(solution)/shard_map/pallas_call | solution.py:407
  53.6 0.2 collective-permute-done.15.refs_1_
  53.8 0.5 collective-permute-done.16.refs_2_
  54.2 0.0 copy-done.3
  54.2 2.0 %shard_map.77 = (f32[128,2048]{1,0:T(8,128)S(1)}, f32[128,2048]{1,0:T(8,128)S(1)}) custom-call(s32[4]{0:T(128)S(1)} %pad_add_fusion.place, bf16[256,256]{1,0:T(8,128)(2,1)S(1)} %shard_map.76.refs_0_, bf16[256,256]{1,0:T(8,128)(2,1)S(1)} %collective-permute-done.15.refs_1_, bf16[256,256]{1,0:T(8,128)(2,1)S(1)} %collective-permute-done.16.refs_2_, ...), custom_call_target="tpu_custom_call" | custom-call | flops 2147483648 | bytes 5242880 | tf_op jit(solution)/shard_map/pallas_call | solution.py:608
  56.2 0.4 collective-permute-done.12.piece
  56.6 0.0 collective-permute-done.13.first
  56.6 0.0 collective-permute-done.14.second
  56.6 1.2 %shard_map.79 = bf16[128,2048]{1,0:T(8,128)(2,1)S(1)} custom-call(s32[4]{0:T(128)S(1)} %pad_add_fusion.place, bf16[256,256]{1,0:T(8,128)(2,1)S(1)} %collective-permute-done.12.piece, bf16[128,2048]{1,0:T(8,128)(2,1)S(1)} %collective-permute-done.13.first, bf16[128,2048]{1,0:T(8,128)(2,1)S(1)} %collective-permute-done.14.second, ...), custom_call_target="tpu_custom_call" | custom-call | flops 268435456 | bytes 3145728 | tf_op jit(solution)/shard_map/pallas_call | solution.py:620
  57.7 6.5 %collective-permute-start.17 = (bf16[128,2048]{1,0:T(8,128)(2,1)S(1)}, bf16[128,2048]{1,0:T(8,128)(2,1)S(1)}, u32[]{:S(2)}, u32[]{:S(2)}) collective-permute-start(bf16[128,2048]{1,0:T(8,128)(2,1)S(1)} %shard_map.79), channel_id=1, source_target_pairs={{0,1},{1,0},{2,3},{3,2},{4,5},{5,4},{6,7},{7,6},{8,9},{9,8},{10,11... | collective-permute-start | bytes 1572872 | tf_op jit(solution)/shard_map/ppermute | solution.py:631
  64.2 1.2 %shard_map.78 = f32[128,2048]{1,0:T(8,128)S(1)} custom-call(s32[4]{0:T(128)S(1)} %pad_add_fusion.place, bf16[256,256]{1,0:T(8,128)(2,1)S(1)} %collective-permute-done.12.piece, bf16[128,2048]{1,0:T(8,128)(2,1)S(1)} %collective-permute-done.13.first, bf16[128,2048]{1,0:T(8,128)(2,1)S(1)} %collective-permute-done.14.second, f32[128,2048]{1,0:T(8,128)S(1)} %get-tuple-element.53.near), custom_call_target="tpu_custom_call" | custom-call | flops 268435456 | bytes 3145728 | tf_op jit(solution)/shard_map/pallas_call | solution.py:620
  65.4 0.3 collective-permute-done.17
  65.8 0.9 %add_convert_fusion = bf16[128,2048]{1,0:T(8,128)(2,1)} fusion(f32[128,2048]{1,0:T(8,128)S(1)} %shard_map.78, bf16[128,2048]{1,0:T(8,128)(2,1)S(1)} %collective-permute-done.17), kind=kLoop, calls=%fused_computation | loop fusion | flops 786432 | bytes 2097152 | tf_op jit(solution)/shard_map/convert_element_type | solution.py:633
Async XLA Ops:
  0.0 37.2 %collective-permute-start.7 = (bf16[256,2048]{1,0:T(8,128)(2,1)}, bf16[256,2048]{1,0:T(8,128)(2,1)S(1)}, u32[]{:S(2)}, u32[]{:S(2)}) collective-permute-start(bf16[256,2048]{1,0:T(8,128)(2,1)} %refs_3_.1), channel_id=1, source_target_pairs={{0,2},{1,3},{2,0},{3,1},{4,6},{5,7},{6,4},{7,5},{8,10},{9,11},{10,... | collective-permute-start | bytes 3145736 | tf_op jit(solution)/shard_map/ppermute | solution.py:444
  2.1 35.1 %collective-permute-start.8 = (bf16[256,2048]{1,0:T(8,128)(2,1)}, bf16[256,2048]{1,0:T(8,128)(2,1)S(1)}, u32[]{:S(2)}, u32[]{:S(2)}) collective-permute-start(bf16[256,2048]{1,0:T(8,128)(2,1)} %refs_3_.1), channel_id=1, source_target_pairs={{0,6},{1,7},{2,4},{3,5},{4,2},{5,3},{6,0},{7,1},{8,14},{9,15},{10,... | collective-permute-start | bytes 3145736 | tf_op jit(solution)/shard_map/ppermute | solution.py:444
  4.1 6.0 %copy-start = (f32[1,4,2,128,128]{4,3,2,1,0:T(8,128)S(1)}, f32[1,4,2,128,128]{4,3,2,1,0:T(8,128)}, u32[]{:S(2)}) copy-start(f32[1,4,2,128,128]{4,3,2,1,0:T(8,128)} %param.10) | copy-start | bytes 1572868
  4.1 6.1 %copy-start.1 = (f32[1024,2]{0,1:T(2,128)S(1)}, f32[1024,2]{0,1:T(2,128)}, u32[]{:S(2)}) copy-start(f32[1024,2]{0,1:T(2,128)} %param.9) | copy-start | bytes 24580
  4.1 11.0 %copy-start.2 = (bf16[1024,2048]{1,0:T(8,128)(2,1)S(1)}, bf16[1024,2048]{1,0:T(8,128)(2,1)}, u32[]{:S(2)}) copy-start(bf16[1024,2048]{1,0:T(8,128)(2,1)} %acts.1) | copy-start | bytes 12582916
  4.1 11.0 %copy-start.4 = (bf16[2048,42]{0,1:T(8,128)(2,1)S(1)}, bf16[2048,42]{0,1:T(8,128)(2,1)}, u32[]{:S(2)}) copy-start(bf16[2048,42]{0,1:T(8,128)(2,1)} %param.8) | copy-start | bytes 516100
  11.4 8.1 %collective-permute-start = (bf16[528,128]{1,0:T(8,128)(2,1)S(1)}, bf16[528,128]{1,0:T(8,128)(2,1)S(1)}, u32[]{:S(2)}, u32[]{:S(2)}) collective-permute-start(bf16[528,128]{1,0:T(8,128)(2,1)S(1)} %get-tuple-element.32), channel_id=1, source_target_pairs={{0,16},{8,24},{16,0},{24,8},{32,48},{40,56},{48,32},{56,40},{64,80... | collective-permute-start | bytes 405512 | tf_op jit(solution)/shard_map/ppermute | solution.py:434
  14.2 6.2 %collective-permute-start.1 = (bf16[528,128]{1,0:T(8,128)(2,1)S(1)}, bf16[528,128]{1,0:T(8,128)(2,1)S(1)}, u32[]{:S(2)}, u32[]{:S(2)}) collective-permute-start(bf16[528,128]{1,0:T(8,128)(2,1)S(1)} %get-tuple-element.33), channel_id=1, source_target_pairs={{0,24},{8,16},{16,8},{24,0},{32,56},{40,48},{48,40},{56,32},{64,88... | collective-permute-start | bytes 405512 | tf_op jit(solution)/shard_map/ppermute | solution.py:434
  15.1 5.5 %collective-permute-start.2 = (bf16[528,128]{1,0:T(8,128)(2,1)S(1)}, bf16[528,128]{1,0:T(8,128)(2,1)S(1)}, u32[]{:S(2)}, u32[]{:S(2)}) collective-permute-start(bf16[528,128]{1,0:T(8,128)(2,1)S(1)} %get-tuple-element.34), channel_id=1, source_target_pairs={{0,8},{8,0},{16,24},{24,16},{32,40},{40,32},{48,56},{56,48},{64,72... | collective-permute-start | bytes 405512 | tf_op jit(solution)/shard_map/ppermute | solution.py:434
  21.3 3.9 %collective-permute-start.3 = (bf16[336,128]{1,0:T(8,128)(2,1)S(1)}, bf16[336,128]{1,0:T(8,128)(2,1)S(1)}, u32[]{:S(2)}, u32[]{:S(2)}) collective-permute-start(bf16[336,128]{1,0:T(8,128)(2,1)S(1)} %get-tuple-element.38.after.own), channel_id=1, source_target_pairs={{0,32},{8,40},{16,48},{24,56},{32,0},{40,8},{48,16},{56,24},{64,96... | collective-permute-start | bytes 258056 | tf_op jit(solution)/shard_map/ppermute | solution.py:439
  25.8 12.4 %collective-permute-start.4 = (bf16[336,128]{1,0:T(8,128)(2,1)S(1)}, bf16[336,128]{1,0:T(8,128)(2,1)S(1)}, u32[]{:S(2)}, u32[]{:S(2)}) collective-permute-start(bf16[336,128]{1,0:T(8,128)(2,1)S(1)} %get-tuple-element.42.after.own), channel_id=1, source_target_pairs={{0,160},{8,168},{16,176},{24,184},{32,128},{40,136},{48,144},{56,1... | collective-permute-start | bytes 258056 | tf_op jit(solution)/shard_map/ppermute | solution.py:439
  32.2 6.0 %collective-permute-start.5 = (bf16[336,128]{1,0:T(8,128)(2,1)S(1)}, bf16[336,128]{1,0:T(8,128)(2,1)S(1)}, u32[]{:S(2)}, u32[]{:S(2)}) collective-permute-start(bf16[336,128]{1,0:T(8,128)(2,1)S(1)} %get-tuple-element.42.after.own), channel_id=1, source_target_pairs={{0,192},{8,200},{16,208},{24,216},{32,96},{40,104},{48,112},{56,12... | collective-permute-start | bytes 258056 | tf_op jit(solution)/shard_map/ppermute | solution.py:439
  32.5 6.3 %collective-permute-start.6 = (bf16[336,128]{1,0:T(8,128)(2,1)S(1)}, bf16[336,128]{1,0:T(8,128)(2,1)S(1)}, u32[]{:S(2)}, u32[]{:S(2)}) collective-permute-start(bf16[336,128]{1,0:T(8,128)(2,1)S(1)} %get-tuple-element.42.after.own), channel_id=1, source_target_pairs={{0,224},{8,232},{16,240},{24,248},{32,64},{40,72},{48,80},{56,88},... | collective-permute-start | bytes 258056 | tf_op jit(solution)/shard_map/ppermute | solution.py:439
  37.4 19.2 %collective-permute-start.13 = (bf16[128,2048]{1,0:T(8,128)(2,1)S(1)}, bf16[128,2048]{1,0:T(8,128)(2,1)S(1)}, u32[]{:S(2)}, u32[]{:S(2)}) collective-permute-start(bf16[128,2048]{1,0:T(8,128)(2,1)S(1)} %get-tuple-element.45.after), channel_id=1, source_target_pairs={{0,6},{1,7},{2,4},{3,5},{4,2},{5,3},{6,0},{7,1},{8,14},{9,15},{10,... | collective-permute-start | bytes 1572872 | tf_op jit(solution)/shard_map/ppermute | solution.py:444
  38.2 18.4 %collective-permute-start.14 = (bf16[128,2048]{1,0:T(8,128)(2,1)S(1)}, bf16[128,2048]{1,0:T(8,128)(2,1)S(1)}, u32[]{:S(2)}, u32[]{:S(2)}) collective-permute-start(bf16[128,2048]{1,0:T(8,128)(2,1)S(1)} %get-tuple-element.49), channel_id=1, source_target_pairs={{0,2},{1,3},{2,0},{3,1},{4,6},{5,7},{6,4},{7,5},{8,10},{9,11},{10,... | collective-permute-start | bytes 1572872 | tf_op jit(solution)/shard_map/ppermute | solution.py:444
  39.4 5.8 %collective-permute-start.10 = (bf16[448,128]{1,0:T(8,128)(2,1)S(1)}, bf16[448,128]{1,0:T(8,128)(2,1)S(1)}, u32[]{:S(2)}, u32[]{:S(2)}) collective-permute-start(bf16[448,128]{1,0:T(8,128)(2,1)S(1)} %get-tuple-element.47.after.refs_4_), channel_id=1, source_target_pairs={{0,16},{8,24},{16,0},{24,8},{32,48},{40,56},{48,32},{56,40},{64,80... | collective-permute-start | bytes 344072 | tf_op jit(solution)/shard_map/ppermute | solution.py:434
  41.7 5.1 %collective-permute-start.11 = (bf16[448,128]{1,0:T(8,128)(2,1)S(1)}, bf16[448,128]{1,0:T(8,128)(2,1)S(1)}, u32[]{:S(2)}, u32[]{:S(2)}) collective-permute-start(bf16[448,128]{1,0:T(8,128)(2,1)S(1)} %get-tuple-element.47.after.refs_4_), channel_id=1, source_target_pairs={{0,24},{8,16},{16,8},{24,0},{32,56},{40,48},{48,40},{56,32},{64,88... | collective-permute-start | bytes 344072 | tf_op jit(solution)/shard_map/ppermute | solution.py:434
  43.1 3.9 %collective-permute-start.9 = (bf16[448,128]{1,0:T(8,128)(2,1)S(1)}, bf16[448,128]{1,0:T(8,128)(2,1)S(1)}, u32[]{:S(2)}, u32[]{:S(2)}) collective-permute-start(bf16[448,128]{1,0:T(8,128)(2,1)S(1)} %get-tuple-element.47.after.refs_4_), channel_id=1, source_target_pairs={{0,8},{8,0},{16,24},{24,16},{32,40},{40,32},{48,56},{56,48},{64,72... | collective-permute-start | bytes 344072 | tf_op jit(solution)/shard_map/ppermute | solution.py:434
  48.6 5.6 %copy-start.3 = (bf16[256,2048]{1,0:T(8,128)(2,1)S(1)}, bf16[256,2048]{1,0:T(8,128)(2,1)}, u32[]{:S(2)}) copy-start(bf16[256,2048]{1,0:T(8,128)(2,1)} %refs_3_.1) | copy-start | bytes 3145732
  48.6 5.1 %collective-permute-start.15 = (bf16[256,256]{1,0:T(8,128)(2,1)S(1)}, bf16[256,256]{1,0:T(8,128)(2,1)S(1)}, u32[]{:S(2)}, u32[]{:S(2)}) collective-permute-start(bf16[256,256]{1,0:T(8,128)(2,1)S(1)} %get-tuple-element.52), channel_id=1, source_target_pairs={{0,6},{1,7},{2,4},{3,5},{4,2},{5,3},{6,0},{7,1},{8,14},{9,15},{10,... | collective-permute-start | bytes 393224 | tf_op jit(solution)/shard_map/ppermute | solution.py:444
  50.4 3.8 %collective-permute-start.16 = (bf16[256,256]{1,0:T(8,128)(2,1)S(1)}, bf16[256,256]{1,0:T(8,128)(2,1)S(1)}, u32[]{:S(2)}, u32[]{:S(2)}) collective-permute-start(bf16[256,256]{1,0:T(8,128)(2,1)S(1)} %get-tuple-element.51.refs_5_), channel_id=1, source_target_pairs={{0,2},{1,3},{2,0},{3,1},{4,6},{5,7},{6,4},{7,5},{8,10},{9,11},{10,... | collective-permute-start | bytes 393224 | tf_op jit(solution)/shard_map/ppermute | solution.py:444
  51.2 5.3 %collective-permute-start.12 = (bf16[256,256]{1,0:T(8,128)(2,1)S(1)}, bf16[256,256]{1,0:T(8,128)(2,1)S(1)}, u32[]{:S(2)}, u32[]{:S(2)}) collective-permute-start(bf16[256,256]{1,0:T(8,128)(2,1)S(1)} %get-tuple-element.48), channel_id=1, source_target_pairs={{0,4},{1,5},{2,6},{3,7},{4,0},{5,1},{6,2},{7,3},{8,12},{9,13},{10,... | collective-permute-start | bytes 393224 | tf_op jit(solution)/shard_map/ppermute | solution.py:444
  57.7 8.0 %collective-permute-start.17 = (bf16[128,2048]{1,0:T(8,128)(2,1)S(1)}, bf16[128,2048]{1,0:T(8,128)(2,1)S(1)}, u32[]{:S(2)}, u32[]{:S(2)}) collective-permute-start(bf16[128,2048]{1,0:T(8,128)(2,1)S(1)} %shard_map.79), channel_id=1, source_target_pairs={{0,1},{1,0},{2,3},{3,2},{4,5},{5,4},{6,7},{7,6},{8,9},{9,8},{10,11... | collective-permute-start | bytes 1572872 | tf_op jit(solution)/shard_map/ppermute | solution.py:631
